TPU v7x, 32 devices: a whole 2x2x4 slice. The times are simulated.
32 devices in a mesh: groups: 2 (over x), state: 16 (over z, y, core).
Axes of the slice: x: 2, y: 2, z: 4, core: 2. Of those that a mesh axis runs over, the one named last changes fastest.
Arguments:
- background_draws_table: float32 [256, 65536], P('state', 'groups'), parts along dimension 1
- measurement_reading: float32 [512, 32], P('groups'), parts along dimension 0, may hold values from -8 to 8
- measurement_precision: float32 [512, 32], P('groups'), parts along dimension 0, may hold values from 0.25 to 4
- sensed_point_position: int32 [512, 32], P('groups'), parts along dimension 0, may hold values from 0 to 127
- measurement_tally: int32 [512], P('groups'), parts along dimension 0, may hold values from 1 to 32, as said below
- adjacent_tile_number: int32 [512, 5], P(('groups', 'state')), parts along dimension 0, may hold values from -1 to 255, as said below
Outputs:
- analysis: float32 [256, 65536], P('state', 'groups'), parts along dimension 1
There are 2 independent parts, one for each index of `groups`. A program takes and returns all parts, laid end to end along the dimension named above; each array names one. Nothing has to cross between parts.
Inputs may be any that keep to these rules, and one draw needn't show every extreme that they name: `measurement_tally`: every block's count is at least 1 and at most 32; some block has exactly 32. `adjacent_tile_number`: entry j of row b is either b + j - 2 or -1; it is -1 where b + j - 2 lies outside the grid of blocks, and the middle entry is always b.
All inputs are finite; a program needn't handle non-finite values.
Results may differ from a plain program's by a relative error of at most 0.0003.
Values sent between devices are 32-bit elements; how exact they have to be, the bound alone decides.
No kernel may reach another device: no remote copies, remote signals or barrier semaphores. Data moves between devices by JAX's collectives and lax.ppermute only.
A program may use at most 128 MiB of HBM per device.

v0:
```python
import jax
import jax.numpy as jnp
from jax import lax
from jax.sharding import PartitionSpec as P

PARTITION_SPAN = 128
OB = 32
R = 2
NS_ITERS = 5
LOC = 128


PRECISE = lax.Precision.HIGHEST


def extended(cells, sides, width):
    for axis, dim in sides:
        count = lax.axis_size(axis)
        ends = count - 1
        head = lax.slice_in_dim(cells, 0, width, axis=dim)
        tail = lax.slice_in_dim(cells, cells.shape[dim] - width, cells.shape[dim], axis=dim)
        cells = jnp.concatenate(
            [
                lax.ppermute(tail, axis, [(i, (i + 1) % count) for i in range(ends)]),
                cells,
                lax.ppermute(head, axis, [((i + 1) % count, i) for i in range(ends)]),
            ],
            axis=dim,
        )
    return cells


def transform(obs_anom, innovation, weight):
    sample_fields = obs_anom.shape[0]
    scaled = obs_anom * weight[None, :]
    spread = jnp.dot(scaled, obs_anom.T, precision=PRECISE) / (sample_fields - 1.0)
    norm_size = 1.0 + jnp.sqrt(jnp.sum(spread * spread))
    identity = jnp.eye(sample_fields, dtype=jnp.float32)
    forward = (identity + spread) / norm_size
    inverse = identity
    for sweep_index in range(NS_ITERS):
        middle = 1.5 * identity - 0.5 * jnp.dot(inverse, forward, precision=PRECISE)
        forward = jnp.dot(forward, middle, precision=PRECISE)
        inverse = jnp.dot(middle, inverse, precision=PRECISE)
    inv_root = inverse / jnp.sqrt(norm_size)
    pull_vec = jnp.dot(scaled, innovation, precision=PRECISE) / (sample_fields - 1.0)
    mean_weight = jnp.dot(
        inv_root, jnp.dot(inv_root, pull_vec, precision=PRECISE), precision=PRECISE
    )
    return inv_root + mean_weight[:, None]


def stacked(source_arr, along, partition_amount):
    window_len = 2 * R + 1
    slabs = [
        lax.slice_in_dim(source_arr, offset, offset + partition_amount, axis=along)
        for offset in range(window_len)
    ]
    return jnp.stack(slabs, axis=along + 1)


def body(
    background_draws_table,
    measurement_reading,
    measurement_precision,
    sensed_point_position,
    measurement_tally,
    adjacent_tile_number,
):
    field_dimension = lax.axis_size("state")
    position = lax.axis_index("state")
    adjacent_samples, whole_grid_field = background_draws_table.shape
    anomaly_grid_points = whole_grid_field // field_dimension
    partition_amount = anomaly_grid_points // PARTITION_SPAN
    sample_fields = adjacent_samples * field_dimension
    window_len = 2 * R + 1
    first_block = position * partition_amount
    regrouped_field = background_draws_table.reshape(
        adjacent_samples, field_dimension, anomaly_grid_points
    )
    gathered = lax.all_to_all(regrouped_field, "state", split_axis=1, concat_axis=0, tiled=True)
    ocean_vectors = gathered.reshape(sample_fields, anomaly_grid_points)
    own_cells = lax.dynamic_slice_in_dim(sensed_point_position, first_block, partition_amount, 0)
    picked = jnp.take_along_axis(
        ocean_vectors.reshape(sample_fields, partition_amount, PARTITION_SPAN),
        own_cells[None, :, :],
        axis=2,
    )
    window = extended(picked, (("state", 1),), R)
    expected_ocean_background = jnp.mean(ocean_vectors, axis=0)
    spread_departures = ocean_vectors - expected_ocean_background[None, :]
    frame_len = partition_amount + 2 * R
    values = lax.dynamic_slice_in_dim(
        jnp.pad(measurement_reading, ((R, R), (0, 0))), first_block, frame_len, 0
    )
    inv_var = lax.dynamic_slice_in_dim(
        jnp.pad(measurement_precision, ((R, R), (0, 0))), first_block, frame_len, 0
    )
    cell_win = lax.dynamic_slice_in_dim(
        jnp.pad(sensed_point_position, ((R, R), (0, 0))), first_block, frame_len, 0
    )
    counts = lax.dynamic_slice_in_dim(
        jnp.pad(measurement_tally, ((R, R),)), first_block, frame_len, 0
    )
    obs_raw = stacked(window, 1, partition_amount)
    obs_mean = jnp.mean(obs_raw, axis=0)
    obs_anom = obs_raw - obs_mean[None]
    innovation = stacked(values, 0, partition_amount) - obs_mean
    usable = adjacent_tile_number >= 0
    active = (
        jnp.arange(OB, dtype=jnp.int32)[None, None, :]
        < stacked(counts, 0, partition_amount)[:, :, None]
    )
    offsets = (jnp.arange(window_len, dtype=jnp.int32) - R) * PARTITION_SPAN
    distance = (
        offsets.astype(jnp.float32)[None, :, None]
        + stacked(cell_win, 0, partition_amount).astype(jnp.float32)
        - 0.5 * (PARTITION_SPAN - 1)
    )
    weight = (
        stacked(inv_var, 0, partition_amount)
        * jnp.exp(-0.5 * (distance / LOC) ** 2)
        * active.astype(jnp.float32)
        * usable.astype(jnp.float32)[:, :, None]
    )
    width_obs = window_len * OB
    flat_anom = obs_anom.transpose(1, 0, 2, 3).reshape(partition_amount, sample_fields, width_obs)
    matrices = jax.vmap(transform)(
        flat_anom,
        innovation.reshape(partition_amount, width_obs),
        weight.reshape(partition_amount, width_obs),
    )
    block_anom = spread_departures.reshape(sample_fields, partition_amount, PARTITION_SPAN)
    analysis_result_vectors = expected_ocean_background.reshape(partition_amount, PARTITION_SPAN)[
        None
    ] + jnp.einsum("jbc,bjk->kbc", block_anom, matrices, precision=PRECISE)
    result = lax.all_to_all(
        analysis_result_vectors.reshape(sample_fields, 1, anomaly_grid_points),
        "state",
        split_axis=0,
        concat_axis=1,
        tiled=True,
    )
    return result.reshape(adjacent_samples, whole_grid_field)


def solution(mesh):
    return jax.shard_map(
        body,
        mesh=mesh,
        in_specs=(
            P("state", "groups"),
            P("groups", None),
            P("groups", None),
            P("groups", None),
            P("groups"),
            P(("groups", "state"), None),
        ),
        out_specs=P("state", "groups"),
        check_vma=False,
    )
```

profile of v0, /device:TPU:0, one launch (start us, length us, event | category | flops | bytes accessed | tf_op | source)
XLA Modules:
  0.0 236.2 jit_solution(466567902662209374)
XLA Ops:
  0.0 3.2 %copy.153 = f32[2,16,8,2048]{3,2,0,1:T(8,128)} copy(f32[2,16,8,2048]{3,2,1,0:T(8,128)} %bitcast.164) | data formatting | bytes 4194304 | tf_op jit(solution)/shard_map/reshape | solution.py:78
  3.2 7.4 %all-to-all-start = ((f32[16,16,2048]{2,0,1:T(8,128)}), f32[16,16,2048]{2,0,1:T(8,128)S(1)}, u32[]{:S(2)}, u32[]{:S(2)}) async-start(f32[16,16,2048]{2,0,1:T(8,128)} %bitcast.162), calls=%async_computation | async-start | bytes 4194304 | tf_op jit(solution)/shard_map/all_to_all | solution.py:81
  11.0 0.1 copy.116
  11.1 0.1 copy.120
  11.1 0.1 copy.118
  11.2 0.1 compare_and_fusion
  11.8 0.1 mul.100
  12.5 0.1 copy.121
  13.1 38.6 %all-to-all-done = f32[16,16,2048]{2,0,1:T(8,128)S(1)} async-done(((f32[16,16,2048]{2,0,1:T(8,128)}), f32[16,16,2048]{2,0,1:T(8,128)S(1)}, u32[]{:S(2)}, u32[]{:S(2)}) %all-to-all-start) | async-done | bytes 2097184 | tf_op jit(solution)/shard_map/all_to_all | solution.py:81
  51.7 0.1 reduce_sum.27
  51.8 1.7 copy.136
  53.5 1.9 copy.108
  55.5 3.9 %gather_fusion = f32[512,256]{1,0:T(8,128)S(1)} fusion(f32[256,16,128]{0,2,1:T(8,128)S(1)} %copy.108, s32[512]{0:T(512)S(1)} %reshape.150), kind=kCustom, calls=%fused_computation | custom fusion | bytes 1052672 | tf_op jit(solution)/shard_map/jit(take_along_axis)/gather | solution.py:84
  59.4 0.1 broadcast_select_fusion
  59.6 1.3 collective-permute-start.1
  60.9 3.8 %collective-permute-start = (f32[256,2,32]{0,2,1:T(8,128)S(1)}, f32[256,2,32]{0,2,1:T(8,128)S(1)}, u32[]{:S(2)}, u32[]{:S(2)}) collective-permute-start(f32[256,2,32]{0,2,1:T(8,128)S(1)} %get-tuple-element.8), channel_id=1, source_target_pairs={{0,1},{1,2},{2,3},{3,4},{4,5},{5,6},{6,7},{7,8},{8,9},{9,10},{10,1... | collective-permute-start | bytes 196616 | tf_op jit(solution)/shard_map/ppermute | solution.py:24
  64.6 3.1 %broadcast_subtract_fusion.1 = f32[256,16,128]{2,1,0:T(8,128)} fusion(f32[16,128]{1,0:T(8,128)S(1)} %multiply_bitcast_fusion, f32[32,8,16,128]{3,2,1,0:T(8,128)} %copy.136), kind=kLoop, calls=%fused_computation.52 | loop fusion | flops 524288 | bytes 4202496 | tf_op jit(solution)/shard_map/sub | solution.py:91
  67.7 0.8 fusion.53
  68.6 0.8 fusion.57
  69.4 0.9 bitcast_dynamic-update-slice_fusion
  70.3 0.8 fusion.50
  71.2 0.8 fusion.55
  72.0 2.2 reduce_sum.28
  74.2 2.1 broadcast_subtract_fusion
  76.4 7.4 %multiply_reduce_fusion = (f32[16]{0:T(128)S(1)}, f32[16,256,256]{2,1,0:T(8,128)S(1)}) fusion(f32[16,256,160]{1,2,0:T(8,128)S(1)} %bitcast.155, f32[16,160]{1,0:T(8,128)S(1)} %select_multiply_fusion), kind=kOutput, calls=%fused_computation.14 | convolution fusion | flops 2017067008 | bytes 6826048 | tf_op jit(solution)/shard_map/vmap()/dot_general | solution.py:36
  83.8 2.9 %fusion.62 = f32[256,16,256]{2,0,1:T(8,128)S(1)} fusion(f32[16,256,256]{2,1,0:T(8,128)S(1)} %get-tuple-element.17, f32[16]{0:T(128)S(1)} %get-tuple-element.9, f32[256,256]{1,0:T(8,128)S(1)} %fusion.59), kind=kOutput, calls=%fused_computation.75 | convolution fusion | flops 3224436736 | bytes 8650816 | tf_op jit(solution)/shard_map/vmap()/dot_general | solution.py:42
  86.7 5.6 %fusion = f32[16,256,256]{2,1,0:T(8,128)S(1)} fusion(f32[256,16,256]{2,0,1:T(8,128)S(1)} %fusion.62, f32[256,256]{1,0:T(8,128)S(1)} %fusion.60, f32[16,256,256]{2,1,0:T(8,128)S(1)} %get-tuple-element.17, f32[16]{0:T(128)S(1)} %get-tuple-element.9, f32[256,256]{1,0:T(8,128)S(1)} %fusion.59), kind=kOutput, calls=%fused_computation.1 | convolution fusion | flops 3226468352 | bytes 13107264 | tf_op jit(solution)/shard_map/vmap()/dot_general | solution.py:43
  92.4 2.4 fusion.2
  94.7 5.0 %fusion.88 = f32[16,256,256]{2,1,0:T(8,128)S(1)} fusion(f32[16,256,256]{2,1,0:T(8,128)S(1)} %fusion.2, f32[16,256,256]{2,1,0:T(8,128)S(1)} %fusion), kind=kOutput, calls=%fused_computation.148 | convolution fusion | flops 3221225472 | bytes 12582912 | tf_op jit(solution)/shard_map/vmap()/dot_general | solution.py:42
  99.8 5.4 %fusion.13 = f32[16,256,256]{2,1,0:T(8,128)S(1)} fusion(f32[16,256,256]{2,1,0:T(8,128)S(1)} %fusion, f32[16,256,256]{2,1,0:T(8,128)S(1)} %fusion.88, f32[256,256]{1,0:T(8,128)S(1)} %fusion.60), kind=kOutput, calls=%fused_computation.20 | convolution fusion | flops 3223322624 | bytes 12845056 | tf_op jit(solution)/shard_map/vmap()/dot_general | solution.py:43
  105.2 5.1 %fusion.14 = f32[16,256,256]{2,1,0:T(8,128)S(1)} fusion(f32[16,256,256]{2,1,0:T(8,128)S(1)} %fusion.2, f32[16,256,256]{2,1,0:T(8,128)S(1)} %fusion.88, f32[256,256]{1,0:T(8,128)S(1)} %fusion.60), kind=kOutput, calls=%fused_computation.21 | convolution fusion | flops 3223322624 | bytes 12845056 | tf_op jit(solution)/shard_map/vmap()/dot_general | solution.py:44
  110.2 5.5 %fusion.89 = f32[16,256,256]{2,1,0:T(8,128)S(1)} fusion(f32[16,256,256]{2,1,0:T(8,128)S(1)} %fusion.14, f32[16,256,256]{2,1,0:T(8,128)S(1)} %fusion.13), kind=kOutput, calls=%fused_computation.149 | convolution fusion | flops 3221225472 | bytes 12582912 | tf_op jit(solution)/shard_map/vmap()/dot_general | solution.py:42
  115.7 5.2 %fusion.15 = f32[16,256,256]{2,1,0:T(8,128)S(1)} fusion(f32[16,256,256]{2,1,0:T(8,128)S(1)} %fusion.13, f32[16,256,256]{2,1,0:T(8,128)S(1)} %fusion.89, f32[256,256]{1,0:T(8,128)S(1)} %fusion.60), kind=kOutput, calls=%fused_computation.22 | convolution fusion | flops 3223322624 | bytes 12845056 | tf_op jit(solution)/shard_map/vmap()/dot_general | solution.py:43
  120.9 5.1 %fusion.16 = f32[16,256,256]{2,1,0:T(8,128)S(1)} fusion(f32[16,256,256]{2,1,0:T(8,128)S(1)} %fusion.14, f32[16,256,256]{2,1,0:T(8,128)S(1)} %fusion.89, f32[256,256]{1,0:T(8,128)S(1)} %fusion.60), kind=kOutput, calls=%fused_computation.23 | convolution fusion | flops 3223322624 | bytes 12845056 | tf_op jit(solution)/shard_map/vmap()/dot_general | solution.py:44
  126.0 5.2 %fusion.90 = f32[16,256,256]{2,1,0:T(8,128)S(1)} fusion(f32[16,256,256]{2,1,0:T(8,128)S(1)} %fusion.16, f32[16,256,256]{2,1,0:T(8,128)S(1)} %fusion.15), kind=kOutput, calls=%fused_computation.150 | convolution fusion | flops 3221225472 | bytes 12582912 | tf_op jit(solution)/shard_map/vmap()/dot_general | solution.py:42
  131.2 5.8 %fusion.18 = f32[16,256,256]{2,1,0:T(8,128)} fusion(f32[16,256,256]{2,1,0:T(8,128)S(1)} %fusion.16, f32[16,256,256]{2,1,0:T(8,128)S(1)} %fusion.90, f32[256,256]{1,0:T(8,128)S(1)} %fusion.60), kind=kOutput, calls=%fused_computation.25 | convolution fusion | flops 3223322624 | bytes 12845056 | tf_op jit(solution)/shard_map/vmap()/dot_general | solution.py:44
  137.0 5.8 %fusion.17 = f32[16,256,256]{2,1,0:T(8,128)} fusion(f32[16,256,256]{2,1,0:T(8,128)S(1)} %fusion.15, f32[16,256,256]{2,1,0:T(8,128)S(1)} %fusion.90, f32[256,256]{1,0:T(8,128)S(1)} %fusion.60), kind=kOutput, calls=%fused_computation.24 | convolution fusion | flops 3223322624 | bytes 12845056 | tf_op jit(solution)/shard_map/vmap()/dot_general | solution.py:43
  142.9 0.1 reshape.169
  143.0 1.6 fusion.9
  144.6 8.6 %fusion.91 = f32[16,256,256]{2,1,0:T(8,128)S(1)} fusion(f32[16,256,256]{2,1,0:T(8,128)} %fusion.18, f32[16,256,256]{2,1,0:T(8,128)} %fusion.17), kind=kOutput, calls=%fused_computation.151 | convolution fusion | flops 3221225472 | bytes 12582912 | tf_op jit(solution)/shard_map/vmap()/dot_general | solution.py:42
  153.2 5.1 %broadcast_divide_fusion = f32[16,256,256]{2,1,0:T(8,128)S(1)} fusion(f32[16]{0:T(128)S(1)} %get-tuple-element.10, f32[16,256,256]{2,1,0:T(8,128)S(1)} %copy-done, f32[16,256,256]{2,1,0:T(8,128)S(1)} %fusion.91, f32[256,256]{1,0:T(8,128)S(1)} %fusion.60), kind=kOutput, calls=%fused_computation.29 | convolution fusion | flops 3224371200 | bytes 12845120 | tf_op jit(solution)/shard_map/vmap()/dot_general | solution.py:44
  158.3 3.6 %fusion.72 = f32[16,1,256]{2,1,0:T(1,128)S(1)} fusion(f32[16,256,256]{2,1,0:T(8,128)S(1)} %broadcast_divide_fusion, f32[16,256,1]{1,0,2:T(8,128)S(1)} %fusion.69), kind=kOutput, calls=%fused_computation.120 | convolution fusion | flops 12582912 | bytes 4227072 | tf_op jit(solution)/shard_map/vmap()/dot_general | solution.py:48
  161.9 3.6 %fusion.70 = f32[16,1,256]{2,1,0:T(1,128)S(1)} fusion(f32[16,256,256]{2,1,0:T(8,128)S(1)} %broadcast_divide_fusion, f32[16,256,1]{1,0,2:T(8,128)S(1)} %bitcast.167), kind=kOutput, calls=%fused_computation.117 | convolution fusion | flops 12582912 | bytes 4227072 | tf_op jit(solution)/shard_map/vmap()/dot_general | solution.py:47
  165.5 5.1 %fusion.41 = f32[16,256,128]{1,2,0:T(8,128)S(1)} fusion(f32[256,16,128]{2,1,0:T(8,128)S(1)} %copy-done.1, f32[16,256,256]{2,1,0:T(8,128)S(1)} %broadcast_divide_fusion, f32[16,256]{1,0:T(8,128)S(1)} %bitcast.166, f32[16,128]{1,0:T(8,128)S(1)} %multiply_bitcast_fusion), kind=kOutput, calls=%fused_computation.48 | convolution fusion | flops 1612185600 | bytes 8413184 | tf_op jit(solution)/shard_map/jbc,bjk->kbc/dot_general | solution.py:136
  170.6 3.6 %copy.124 = f32[256,1,2048]{2,1,0:T(1,128)} copy(f32[256,1,2048]{0,2,1:T(8,128)S(1)} %bitcast.161) | data formatting | bytes 4194304 | tf_op jit(solution)/shard_map/reshape | solution.py:138
  174.2 59.5 %all_to_all.30 = f32[256,1,2048]{2,1,0:T(1,128)S(1)} all-to-all(f32[256,1,2048]{2,1,0:T(1,128)} %copy.124), channel_id=1, replica_groups=mesh['groups'=2,'state'=16] {'state'}, dimensions={0} | all-to-all | bytes 4194304 | tf_op jit(solution)/shard_map/all_to_all | solution.py:137
  233.7 0.9 copy.133
  234.5 1.5 copy.137
  (63 shorter events, 1.9 us)
Async XLA Ops:
  0.0 10.8 %copy-start.6 = (s32[256]{0:T(256)S(1)}, s32[256]{0:T(256)}, u32[]{:S(2)}) copy-start(s32[256]{0:T(256)} %param.10) | copy-start | bytes 3076
  0.0 11.0 %copy-start.5 = (s32[16,5]{0,1:T(8,128)S(1)}, s32[16,5]{0,1:T(8,128)}, u32[]{:S(2)}) copy-start(s32[16,5]{0,1:T(8,128)} %param.11) | copy-start | bytes 964
  0.0 11.1 %copy-start.3 = (s32[256,32]{0,1:T(8,128)S(1)}, s32[256,32]{0,1:T(8,128)}, u32[]{:S(2)}) copy-start(s32[256,32]{0,1:T(8,128)} %param.9) | copy-start | bytes 98308
  0.0 12.1 %copy-start.2 = (f32[256,32]{0,1:T(8,128)S(1)}, f32[256,32]{0,1:T(8,128)}, u32[]{:S(2)}) copy-start(f32[256,32]{0,1:T(8,128)} %param.8) | copy-start | bytes 98308
  0.0 12.5 %copy-start.4 = (f32[256,32]{0,1:T(8,128)S(1)}, f32[256,32]{0,1:T(8,128)}, u32[]{:S(2)}) copy-start(f32[256,32]{0,1:T(8,128)} %param.7) | copy-start | bytes 98308
  3.2 48.5 %all-to-all-start = ((f32[16,16,2048]{2,0,1:T(8,128)}), f32[16,16,2048]{2,0,1:T(8,128)S(1)}, u32[]{:S(2)}, u32[]{:S(2)}) async-start(f32[16,16,2048]{2,0,1:T(8,128)} %bitcast.162), calls=%async_computation | async-start | bytes 4194304 | tf_op jit(solution)/shard_map/all_to_all | solution.py:81
  59.6 10.8 %collective-permute-start.1 = (f32[256,2,32]{0,2,1:T(8,128)S(1)}, f32[256,2,32]{0,2,1:T(8,128)S(1)}, u32[]{:S(2)}, u32[]{:S(2)}) collective-permute-start(f32[256,2,32]{0,2,1:T(8,128)S(1)} %get-tuple-element.7), channel_id=1, source_target_pairs={{1,0},{2,1},{3,2},{4,3},{5,4},{6,5},{7,6},{8,7},{9,8},{10,9},{11,1... | collective-permute-start | bytes 196616 | tf_op jit(solution)/shard_map/ppermute | solution.py:26
  60.9 6.9 %collective-permute-start = (f32[256,2,32]{0,2,1:T(8,128)S(1)}, f32[256,2,32]{0,2,1:T(8,128)S(1)}, u32[]{:S(2)}, u32[]{:S(2)}) collective-permute-start(f32[256,2,32]{0,2,1:T(8,128)S(1)} %get-tuple-element.8), channel_id=1, source_target_pairs={{0,1},{1,2},{2,3},{3,4},{4,5},{5,6},{6,7},{7,8},{8,9},{9,10},{10,1... | collective-permute-start | bytes 196616 | tf_op jit(solution)/shard_map/ppermute | solution.py:24
  144.6 8.6 %copy-start = (f32[16,256,256]{2,1,0:T(8,128)S(1)}, f32[16,256,256]{2,1,0:T(8,128)}, u32[]{:S(2)}) copy-start(f32[16,256,256]{2,1,0:T(8,128)} %fusion.18) | copy-start | bytes 12582916
  158.3 7.2 %copy-start.1 = (f32[256,16,128]{2,1,0:T(8,128)S(1)}, f32[256,16,128]{2,1,0:T(8,128)}, u32[]{:S(2)}) copy-start(f32[256,16,128]{2,1,0:T(8,128)} %broadcast_subtract_fusion.1) | copy-start | bytes 6291460
where the time goes:
time: 240 us; the launch traced here: 236 us
  matrix products  94 us (39%)
  blocking collectives  59.5 us (25%)
  waiting for transfers between devices  38.6 us (16%)
  local copies, waits for them, and re-layouts  18.9 us (8%)
  starting transfers between devices  12.5 us (5%)
  other arithmetic  12.2 us (5%)
    all_to_all x1, blocking collectives, body(): lax.all_to_all(analysis_result_vectors.reshape(sample_fields, 1, anomaly_...  59.5 us
    all_to_all x1, waiting for transfers between devices, body(): lax.all_to_all(regrouped_field, 'state', split_axis=1, concat_axis=0, til...  38.6 us
    dot_general x5, matrix products, transform(): middle = 1.5 * identity - 0.5 * jnp.dot(inverse, forward, precision=PRECISE)  27.1 us
    dot_general x5, matrix products, transform(): inverse = jnp.dot(middle, inverse, precision=PRECISE)  23.4 us
    dot_general x4, matrix products, transform(): forward = jnp.dot(forward, middle, precision=PRECISE)  22.1 us
    dot_general x1, matrix products, transform(): jnp.dot(scaled, obs_anom.T, precision=PRECISE) / (sample_fields - 1.0)  7.44 us
    all_to_all x1, starting transfers between devices, body(): lax.all_to_all(regrouped_field, 'state', split_axis=1, concat_axis=0, til...  7.4 us
    dot_general x1, matrix products, body(): jnp.einsum('jbc,bjk->kbc', block_anom, matrices, precision=PRECISE)  5.08 us
  transfers between devices with their start and end apart: 3, of which 1 were waited for; matrix products, arithmetic and copies ran while one was open for 3% of the time, Pallas kernels for 0%

commit v1 on v0

v1 whole, which is shorter than its diff:
```python
import jax
import jax.numpy as jnp
from jax import lax
from jax.experimental import pallas as pl
from jax.experimental.pallas import tpu as pltpu
from jax.sharding import PartitionSpec as P

PARTITION_SPAN = 128
OB = 32
R = 2
NS_ITERS = 5
LOC = 128

QUAD = PARTITION_SPAN // OB
NN = (((1,), (0,)), ((), ()))
NT = (((1,), (1,)), ((), ()))


def halves(values):
    high = values.astype(jnp.bfloat16)
    return high, (values - high.astype(jnp.float32)).astype(jnp.bfloat16)


def times(left, right, dims):
    (left_high, left_low), (right_high, right_low) = left, right
    return lax.dot_general(
        jnp.concatenate([left_high, left_high, left_low], axis=1),
        jnp.concatenate([right_high, right_low, right_high], axis=dims[0][1][0]),
        dims,
        preferred_element_type=jnp.float32,
    )


def updated(blocks):
    scaled = []
    for fields, seen, root_weight, reading in blocks:
        seen_mean = jnp.mean(seen, axis=0, keepdims=True)
        pull = (reading - seen_mean) * root_weight
        scaled.append(
            (halves((seen - seen_mean) * root_weight), halves(jnp.broadcast_to(pull, (16, pull.shape[1]))))
        )
    products = [(times(root, root, NT), times(pull, root, NT)) for root, pull in scaled]
    states = []
    for (fields, *_), (spread, pull) in zip(blocks, products):
        squares = jnp.sum(jnp.sum(spread * spread, axis=0, keepdims=True), axis=1, keepdims=True)
        norm_size = 1.0 + jnp.sqrt(squares)
        unit = 1.0 / norm_size
        cells = fields.T
        centre = jnp.mean(cells, axis=1, keepdims=True)
        chain = jnp.concatenate([cells - centre, pull], axis=0)
        states.append((norm_size, centre, unit, spread * unit, chain))
    for sweep in range(NS_ITERS):
        last = sweep + 1 == NS_ITERS
        parts = [(halves(rest), halves(chain)) for *_, rest, chain in states]
        moved = [times(chain, rest, NN) for rest, chain in parts]
        square = [None if last else times(rest, rest, NN) for rest, _ in parts]
        gains = [1.5 - 0.5 * unit for _, _, unit, _, _ in states]
        chains = [gain * state[-1] - 0.5 * move for gain, state, move in zip(gains, states, moved)]
        if last:
            states = [(*state[:4], chain) for state, chain in zip(states, chains)]
            break
        middle = [
            (gain - 0.5 * unit) * rest - 0.5 * sq
            for gain, (_, _, unit, rest, _), sq in zip(gains, states, square)
        ]
        cubic = [times(halves(mid), rest, NN) for mid, (rest, _) in zip(middle, parts)]
        states = [
            (
                norm_size,
                centre,
                unit * gain * gain,
                gain * mid - (0.5 * unit * gain) * rest - 0.5 * cube,
                chain,
            )
            for (norm_size, centre, unit, rest, _), gain, mid, cube, chain in zip(
                states, gains, middle, cubic, chains
            )
        ]
    results = []
    for norm_size, centre, _, _, chain in states:
        chain = chain * lax.rsqrt(norm_size)
        moved = chain[:PARTITION_SPAN]
        shift = jnp.sum(moved * chain[PARTITION_SPAN : PARTITION_SPAN + 1], axis=1, keepdims=True)
        results.append((moved + (centre + shift)).T)
    return results


def pick_kernel(fields_ref, position_ref, seen_ref):
    members, width = fields_ref.shape
    span = PARTITION_SPAN
    amount = width // span
    lanes = lax.broadcasted_iota(jnp.int32, (members, span), 1)
    for quad in range(amount // QUAD):
        index = jnp.broadcast_to(position_ref[quad : quad + 1, :], (members, span))
        total = None
        for spot in range(QUAD):
            block = (quad * QUAD + spot - R) % amount
            found = jnp.take_along_axis(fields_ref[:, block * span : (block + 1) * span], index, axis=1)
            total = found if spot == 0 else jnp.where(lanes // OB == spot, found, total)
        seen_ref[:, quad * span : (quad + 1) * span] = total


def update_kernel(fields_ref, before_ref, own_ref, after_ref, weight_ref, reading_ref, result_ref):
    members, span = before_ref.shape
    step = pl.program_id(0)
    steps = pl.num_programs(0)
    lanes = lax.broadcasted_iota(jnp.int32, (members, span), 1)
    here = own_ref[:, pl.ds(pl.multiple_of(step * span, span), span)]
    following = own_ref[:, pl.ds(pl.multiple_of(lax.rem(step + 1, steps) * span, span), span)]
    first = jnp.where((step == 0) & (lanes < R * OB), before_ref[...], here)
    second = jnp.where((step == steps - 1) & (lanes >= R * OB), after_ref[...], following)
    seen = jnp.concatenate([first, second], axis=1)
    blocks = [
        (
            fields_ref[:, spot * span : (spot + 1) * span],
            seen,
            weight_ref[pl.ds(step * QUAD + spot, 1), :],
            reading_ref[pl.ds(step * QUAD + spot, 1), :],
        )
        for spot in range(QUAD)
    ]
    for spot, result in enumerate(updated(blocks)):
        result_ref[:, spot * span : (spot + 1) * span] = result


def windows(frame):
    quads = frame.reshape(-1, QUAD * OB)
    pairs = jnp.concatenate([quads[:-1], quads[1:]], axis=1)
    return jnp.broadcast_to(pairs[:, None, :], (pairs.shape[0], QUAD, pairs.shape[1])).reshape(-1, pairs.shape[1])


def body(
    background_draws_table,
    measurement_reading,
    measurement_precision,
    sensed_point_position,
    measurement_tally,
    adjacent_tile_number,
):
    devices = lax.axis_size("state")
    place = lax.axis_index("state")
    own_members, all_cells = background_draws_table.shape
    cells = all_cells // devices
    amount = cells // PARTITION_SPAN
    members = own_members * devices
    first_block = place * amount
    span = PARTITION_SPAN

    sent = background_draws_table.reshape(own_members, devices, cells).transpose(1, 0, 2)
    fields = lax.all_to_all(sent, "state", split_axis=0, concat_axis=0, tiled=True).reshape(members, cells)

    def frame(array):
        padded = jnp.pad(array, ((R, R),) + ((0, 0),) * (array.ndim - 1))
        return lax.dynamic_slice_in_dim(padded, first_block, amount + 2 * R, 0)

    position = windows(frame(sensed_point_position))
    reading = windows(frame(measurement_reading))
    precision = windows(frame(measurement_precision))
    tally = windows(jnp.broadcast_to(frame(measurement_tally)[:, None], (amount + 2 * R, OB)))
    lane = jnp.arange(2 * QUAD * OB, dtype=jnp.int32)[None, :]
    neighbour = lane // OB - (jnp.arange(amount, dtype=jnp.int32) % QUAD)[:, None]
    usable = jnp.zeros(neighbour.shape, jnp.bool_)
    for j in range(2 * R + 1):
        usable |= (neighbour == j) & (adjacent_tile_number[:, j : j + 1] >= 0)
    distance = (
        ((neighbour - R) * span).astype(jnp.float32) + position.astype(jnp.float32) - 0.5 * (span - 1)
    )
    weight = jnp.where(
        usable & (lane % OB < tally), precision * jnp.exp(-0.5 * (distance / LOC) ** 2), 0.0
    )
    root_weight = jnp.sqrt(weight / (members - 1.0))

    own_position = lax.dynamic_slice_in_dim(sensed_point_position, first_block, amount, 0)
    quad_position = jnp.roll(own_position, R, axis=0).reshape(amount // QUAD, QUAD * OB)
    vmem = pl.BlockSpec(memory_space=pltpu.VMEM)
    own_seen = pl.pallas_call(
        pick_kernel,
        out_shape=jax.ShapeDtypeStruct((members, amount * OB), jnp.float32),
        in_specs=[vmem, vmem],
        out_specs=vmem,
        compiler_params=pltpu.CompilerParams(vmem_limit_bytes=16 << 20),
    )(fields, quad_position)
    edge = own_seen[:, : QUAD * OB]
    before = lax.ppermute(edge, "state", [(i, i + 1) for i in range(devices - 1)])
    after = lax.ppermute(edge, "state", [(i + 1, i) for i in range(devices - 1)])
    steps = amount // QUAD

    def whole(*shape):
        return pl.BlockSpec(shape, lambda step: (0, 0))

    analysis = pl.pallas_call(
        update_kernel,
        grid=(steps,),
        out_shape=jax.ShapeDtypeStruct((members, cells), jnp.float32),
        in_specs=[
            pl.BlockSpec((members, QUAD * span), lambda step: (0, step)),
            whole(members, QUAD * OB),
            whole(members, amount * OB),
            whole(members, QUAD * OB),
            whole(amount, 2 * QUAD * OB),
            whole(amount, 2 * QUAD * OB),
        ],
        out_specs=pl.BlockSpec((members, QUAD * span), lambda step: (0, step)),
        compiler_params=pltpu.CompilerParams(vmem_limit_bytes=40 << 20),
    )(fields, before, own_seen, after, root_weight, reading)

    result = lax.all_to_all(
        analysis.reshape(devices, own_members, cells), "state", split_axis=0, concat_axis=0, tiled=True
    )
    return result.transpose(1, 0, 2).reshape(own_members, all_cells)


def solution(mesh):
    return jax.shard_map(
        body,
        mesh=mesh,
        in_specs=(
            P("state", "groups"),
            P("groups", None),
            P("groups", None),
            P("groups", None),
            P("groups"),
            P(("groups", "state"), None),
        ),
        out_specs=P("state", "groups"),
        check_vma=False,
    )
```

time: 240 us -> 148 us (0.62); the launches traced: 236 us -> 147 us
  matrix products: 94 us -> 0 us
  Pallas kernels: 0 us -> 25.8 us
  local copies, waits for them, and re-layouts: 18.9 us -> 6.82 us
  other arithmetic: 12.2 us -> 0.22 us
  blocking collectives: 59.5 us -> 62.4 us
    dot_general x19 -> x0, matrix products: 94 us -> none  [the longest x5 27.1 us: transform(): middle = 1.5 * identity - 0.5 * jnp.dot(inverse, forward, precision=PRECISE)]
    pallas_call x0 -> x2, Pallas kernels: none -> 25.8 us  [the longest x1 25.2 us: body(): pl.pallas_call(update_kernel, grid=(steps,), out_shape=jax.ShapeDtypeStru...]
    sub x3 -> x0, other arithmetic: 5.24 us -> none  [the longest x1 3.08 us: body(): spread_departures = ocean_vectors - expected_ocean_background[None, :]]
    unnamed x31 -> x10, local copies, waits for them, and re-layouts: 4.72 us -> 0.02 us
    gather x3 -> x0, local copies, waits for them, and re-layouts: 4.07 us -> none  [body(): jnp.take_along_axis(ocean_vectors.reshape(sample_fields, partition_amount...]
    unnamed x4 -> x0, other arithmetic: 3.46 us -> none
    all_to_all x1, blocking collectives: 59.5 us -> 62.4 us  [body(): lax.all_to_all(analysis.reshape(devices, own_members, cells), 'state', sp...]
    reshape x2 -> x6, local copies, waits for them, and re-layouts: 6.78 us -> 4.8 us  [the longest x1 3.13 us: body(): background_draws_table.reshape(own_members, devices, cells)]
  transfers between devices with their start and end apart: 3 -> 3, of which waited for: 1 -> 2; matrix products, arithmetic and copies ran while one was open for 3% -> 2% of each run, Pallas kernels for 0% -> 0%
where the time goes in v1:
time: 148 us; the launch traced here: 147 us
  blocking collectives  62.4 us (42%)
  waiting for transfers between devices  39.6 us (27%)
  Pallas kernels  25.8 us (17%)
  starting transfers between devices  12.1 us (8%)
  local copies, waits for them, and re-layouts  6.82 us (5%)
    all_to_all x1, blocking collectives, body(): lax.all_to_all(analysis.reshape(devices, own_members, cells), 'state', sp...  62.4 us
    all_to_all x1, waiting for transfers between devices, body(): lax.all_to_all(sent, 'state', split_axis=0, concat_axis=0, tiled=True)  38.7 us
    pallas_call x1, Pallas kernels, body(): pl.pallas_call(update_kernel, grid=(steps,), out_shape=jax.ShapeDtypeStru...  25.2 us
    all_to_all x1, starting transfers between devices, body(): lax.all_to_all(sent, 'state', split_axis=0, concat_axis=0, tiled=True)  7.53 us
    ppermute x1, starting transfers between devices, body(): lax.ppermute(edge, 'state', [(i, i + 1) for i in range(devices - 1)])  3.31 us
    reshape x1, local copies, waits for them, and re-layouts, body(): background_draws_table.reshape(own_members, devices, cells)  3.13 us
  transfers between devices with their start and end apart: 3, of which 2 were waited for; matrix products, arithmetic and copies ran while one was open for 2% of the time, Pallas kernels for 0%

profile of v1, /device:TPU:0, one launch (start us, length us, event | category | flops | bytes accessed | tf_op | source)
XLA Modules:
  0.0 147.2 jit_solution(4786835524819813605)
XLA Ops:
  0.0 3.1 %copy.22 = f32[2,16,8,2048]{3,2,0,1:T(8,128)} copy(f32[2,16,8,2048]{3,2,1,0:T(8,128)} %bitcast.27) | data formatting | bytes 4194304 | tf_op jit(solution)/shard_map/reshape | solution.py:149
  3.1 0.0 copy-start.4
  3.1 0.0 copy-start
  3.1 0.0 copy-start.1
  3.1 0.0 copy-start.3
  3.2 7.5 %all-to-all-start = ((f32[16,16,2048]{2,1,0:T(8,128)}), f32[16,16,2048]{2,1,0:T(8,128)S(1)}, u32[]{:S(2)}, u32[]{:S(2)}) async-start(f32[16,16,2048]{2,1,0:T(8,128)} %bitcast.25), calls=%async_computation | async-start | bytes 4194304 | tf_op jit(solution)/shard_map/all_to_all | solution.py:150
  10.7 0.0 copy-done.4
  10.7 0.1 pad_dynamic-slice_fusion.6
  10.8 0.1 fusion.24
  10.9 0.1 broadcast_in_dim.46
  11.0 0.1 broadcast_in_dim.49
  11.0 0.1 broadcast_in_dim.50
  11.1 0.1 broadcast_in_dim.51
  11.2 0.1 broadcast_in_dim.47
  11.3 0.1 broadcast_in_dim.48
  11.4 0.0 copy-done
  11.4 0.1 constant_dynamic-slice_fusion.1
  11.5 0.1 constant_dynamic-slice_fusion
  11.6 0.1 pad_add_fusion
  11.6 0.1 copy.11
  11.7 0.1 reshape.118.position_ref
  11.8 0.1 pad_dynamic-slice_fusion.2
  11.9 0.1 copy.14
  11.9 0.1 slice.95
  12.0 0.1 copy.15
  12.1 0.1 slice.97
  12.2 0.0 copy-done.1
  12.2 0.0 copy-done.2
  12.2 0.1 pad_dynamic-slice_fusion
  12.3 0.1 copy.16
  12.4 0.1 slice.99
  12.5 0.1 copy.17
  12.6 0.1 slice.101
  12.6 0.1 copy.13
  12.7 0.1 slice.93
  12.8 0.1 copy.12
  12.8 0.1 slice.91
  13.0 0.0 copy-done.3
  13.1 38.7 %all-to-all-done = f32[16,16,2048]{2,1,0:T(8,128)S(1)} async-done(((f32[16,16,2048]{2,1,0:T(8,128)}), f32[16,16,2048]{2,1,0:T(8,128)S(1)}, u32[]{:S(2)}, u32[]{:S(2)}) %all-to-all-start) | async-done | bytes 2097184 | tf_op jit(solution)/shard_map/all_to_all | solution.py:150
  51.8 0.6 shard_map.64.own_ref
  52.5 1.3 collective-permute-start.1
  53.8 3.3 %collective-permute-start = (f32[256,128]{1,0:T(8,128)S(1)}, f32[256,128]{1,0:T(8,128)S(1)}, u32[]{:S(2)}, u32[]{:S(2)}) collective-permute-start(f32[256,128]{1,0:T(8,128)S(1)} %slice.102), channel_id=1, source_target_pairs={{0,1},{1,2},{2,3},{3,4},{4,5},{5,6},{6,7},{7,8},{8,9},{9,10},{10,1... | collective-permute-start | bytes 393224 | tf_op jit(solution)/shard_map/ppermute | solution.py:184
  57.1 0.1 fusion.11.weight_ref
  57.2 0.0 collective-permute-done.1.after_ref
  57.2 0.8 collective-permute-done.before_ref
  58.0 25.2 %shard_map.65 = f32[256,2048]{1,0:T(8,128)S(1)} custom-call(f32[256,2048]{1,0:T(8,128)S(1)} %bitcast.23, f32[256,128]{1,0:T(8,128)S(1)} %collective-permute-done.before_ref, f32[256,512]{1,0:T(8,128)S(1)} %shard_map.64.own_ref, f32[256,128]{1,0:T(8,128)S(1)} %collective-permute-done.1.after_ref, f32[16,256]{1,0:T(8,128)S(1)} %fusion.11.weight_ref, ...), custom_call_target="tpu_custom_call" | custom-call | tf_op jit(solution)/shard_map/pallas_call | solution.py:191
  83.2 62.4 %all_to_all.10 = f32[16,16,2048]{2,1,0:T(8,128)S(1)} all-to-all(f32[16,16,2048]{2,1,0:T(8,128)S(1)} %bitcast.24), channel_id=1, replica_groups=mesh['groups'=2,'state'=16] {'state'}, dimensions={0} | all-to-all | bytes 4194304 | tf_op jit(solution)/shard_map/all_to_all | solution.py:207
  145.6 1.5 %copy.20 = f32[16,2,8,2048]{3,2,0,1:T(8,128)} copy(f32[16,2,8,2048]{3,2,1,0:T(8,128)S(1)} %bitcast.26) | data formatting | bytes 4194304 | tf_op jit(solution)/shard_map/reshape | solution.py:210
  (17 shorter events, 0.1 us)
Async XLA Ops:
  3.1 7.6 %copy-start.4 = (s32[256]{0:T(256)S(1)}, s32[256]{0:T(256)}, u32[]{:S(2)}) copy-start(s32[256]{0:T(256)} %param.10) | copy-start | bytes 3076
  3.1 8.2 %copy-start = (s32[256,32]{0,1:T(8,128)S(1)}, s32[256,32]{0,1:T(8,128)}, u32[]{:S(2)}) copy-start(s32[256,32]{0,1:T(8,128)} %param.9) | copy-start | bytes 98308
  3.1 9.1 %copy-start.1 = (f32[256,32]{0,1:T(8,128)S(1)}, f32[256,32]{0,1:T(8,128)}, u32[]{:S(2)}) copy-start(f32[256,32]{0,1:T(8,128)} %param.7) | copy-start | bytes 98308
  3.1 9.1 %copy-start.2 = (f32[256,32]{0,1:T(8,128)S(1)}, f32[256,32]{0,1:T(8,128)}, u32[]{:S(2)}) copy-start(f32[256,32]{0,1:T(8,128)} %param.8) | copy-start | bytes 98308
  3.1 9.9 %copy-start.3 = (s32[16,5]{0,1:T(8,128)S(1)}, s32[16,5]{0,1:T(8,128)}, u32[]{:S(2)}) copy-start(s32[16,5]{0,1:T(8,128)} %param.11) | copy-start | bytes 964
  3.2 48.6 %all-to-all-start = ((f32[16,16,2048]{2,1,0:T(8,128)}), f32[16,16,2048]{2,1,0:T(8,128)S(1)}, u32[]{:S(2)}, u32[]{:S(2)}) async-start(f32[16,16,2048]{2,1,0:T(8,128)} %bitcast.25), calls=%async_computation | async-start | bytes 4194304 | tf_op jit(solution)/shard_map/all_to_all | solution.py:150
  52.5 4.7 %collective-permute-start.1 = (f32[256,128]{1,0:T(8,128)S(1)}, f32[256,128]{1,0:T(8,128)S(1)}, u32[]{:S(2)}, u32[]{:S(2)}) collective-permute-start(f32[256,128]{1,0:T(8,128)S(1)} %slice.102), channel_id=1, source_target_pairs={{1,0},{2,1},{3,2},{4,3},{5,4},{6,5},{7,6},{8,7},{9,8},{10,9},{11,1... | collective-permute-start | bytes 393224 | tf_op jit(solution)/shard_map/ppermute | solution.py:185
  53.8 4.3 %collective-permute-start = (f32[256,128]{1,0:T(8,128)S(1)}, f32[256,128]{1,0:T(8,128)S(1)}, u32[]{:S(2)}, u32[]{:S(2)}) collective-permute-start(f32[256,128]{1,0:T(8,128)S(1)} %slice.102), channel_id=1, source_target_pairs={{0,1},{1,2},{2,3},{3,4},{4,5},{5,6},{6,7},{7,8},{8,9},{9,10},{10,1... | collective-permute-start | bytes 393224 | tf_op jit(solution)/shard_map/ppermute | solution.py:184

commit v2 on v1

v2 whole, which is shorter than its diff:
```python
import functools

import jax
import jax.numpy as jnp
from jax import lax
from jax.experimental import pallas as pl
from jax.experimental.pallas import tpu as pltpu
from jax.sharding import PartitionSpec as P

PARTITION_SPAN = 128
OB = 32
R = 2
NS_ITERS = 5
LOC = 128

QUAD = PARTITION_SPAN // OB
INNER = 4
NN = (((1,), (0,)), ((), ()))
NT = (((1,), (1,)), ((), ()))


def halves(values):
    high = values.astype(jnp.bfloat16)
    return high, (values - high.astype(jnp.float32)).astype(jnp.bfloat16)


def times(left, right, dims):
    (left_high, left_low), (right_high, right_low) = left, right
    return lax.dot_general(
        jnp.concatenate([left_high, left_high, left_low], axis=1),
        jnp.concatenate([right_high, right_low, right_high], axis=dims[0][1][0]),
        dims,
        preferred_element_type=jnp.float32,
    )


def updated(blocks):
    turns = [analysis(*block) for block in blocks]
    results = [None] * len(turns)
    while None in results:
        for index, turn in enumerate(turns):
            if results[index] is None:
                results[index] = next(turn)
    return results


def analysis(fields, seen, root_weight, reading):
    seen_mean = jnp.mean(seen, axis=0, keepdims=True)
    pull = (reading - seen_mean) * root_weight
    root = halves((seen - seen_mean) * root_weight)
    spread = times(root, root, NT)
    pull = times(halves(jnp.broadcast_to(pull, (16, pull.shape[1]))), root, NT)
    yield None
    squares = jnp.sum(jnp.sum(spread * spread, axis=0, keepdims=True), axis=1, keepdims=True)
    norm_size = 1.0 + jnp.sqrt(squares)
    unit = 1.0 / norm_size
    rest = spread * (-0.5 * unit)
    cells = fields.T
    centre = jnp.mean(cells, axis=1, keepdims=True)
    chain = jnp.concatenate([cells - centre, pull], axis=0)
    for sweep in range(NS_ITERS - 1):
        parts = halves(rest)
        gain = 1.5 - 0.5 * unit
        if sweep < NS_ITERS - 2:
            square = times(parts, parts, NN)
        moved = times(halves(chain), parts, NN)
        yield None
        if sweep < NS_ITERS - 2:
            once = (gain - 0.5 * unit) * rest + square
            cubic = times(halves(once), parts, NN)
        chain = gain * chain + moved
        if sweep < NS_ITERS - 2:
            yield None
            rest = gain * once - (0.5 * unit * gain) * rest + cubic
            unit = unit * gain * gain
    moved = times(halves(chain), parts, NN)
    yield None
    end = (-0.5 * unit) * chain + moved
    for _ in range(2):
        moved = times(halves(end), parts, NN)
        yield None
        end = gain * end + moved
    chain = (1.5 * chain + end) * lax.rsqrt(norm_size)
    moved = chain[:PARTITION_SPAN]
    shift = jnp.sum(moved * chain[PARTITION_SPAN : PARTITION_SPAN + 1], axis=1, keepdims=True)
    yield (moved + (centre + shift)).T


def picked(fields, position):
    members = fields[0].shape[0]
    span = PARTITION_SPAN
    index = jnp.broadcast_to(position, (members, span))
    lanes = lax.broadcasted_iota(jnp.int32, (members, span), 1)
    total = None
    for spot, field in enumerate(fields):
        found = jnp.take_along_axis(field, index, axis=1)
        total = found if spot == 0 else jnp.where(lanes // OB == spot, found, total)
    return total


def pick_kernel(fields_ref, position_ref, seen_ref):
    span = PARTITION_SPAN
    quads = position_ref.shape[0]
    amount = quads * QUAD
    for quad in range(quads):
        blocks = [(quad * QUAD + spot - R) % amount for spot in range(QUAD)]
        fields = [fields_ref[:, block * span : (block + 1) * span] for block in blocks]
        seen_ref[:, quad * span : (quad + 1) * span] = picked(fields, position_ref[quad : quad + 1, :])


def update_kernel(fields_ref, before_ref, own_ref, after_ref, weight_ref, reading_ref, result_ref):
    members, span = before_ref.shape
    step = pl.program_id(0)
    steps = pl.num_programs(0)
    lanes = lax.broadcasted_iota(jnp.int32, (members, span), 1)
    here = own_ref[:, pl.ds(pl.multiple_of(step * span, span), span)]
    following = own_ref[:, pl.ds(pl.multiple_of(lax.rem(step + 1, steps) * span, span), span)]
    first = jnp.where((step == 0) & (lanes < R * OB), before_ref[...], here)
    second = jnp.where((step == steps - 1) & (lanes >= R * OB), after_ref[...], following)
    seen = jnp.concatenate([first, second], axis=1)
    blocks = [
        (
            fields_ref[:, spot * span : (spot + 1) * span],
            seen,
            weight_ref[pl.ds(step * QUAD + spot, 1), :],
            reading_ref[pl.ds(step * QUAD + spot, 1), :],
        )
        for spot in range(QUAD)
    ]
    for spot, result in enumerate(updated(blocks)):
        result_ref[:, spot * span : (spot + 1) * span] = result


def terms_kernel(
    amount, members, reading_ref, precision_ref, position_ref, tally_ref, adjacent_ref, weight_ref, shown_ref, quad_ref
):
    first_block = lax.axis_index("state") * amount
    total = tally_ref.shape[0]
    quads = amount // QUAD
    span = PARTITION_SPAN
    lane = lax.broadcasted_iota(jnp.int32, (1, span), 1)
    low = lane < R * OB

    def tile(ref, quad):
        row = first_block // QUAD + quad
        before = ref[pl.ds(jnp.maximum(row - 1, 0), 1), :]
        after = ref[pl.ds(jnp.minimum(row, total // QUAD - 1), 1), :]
        return pltpu.roll(jnp.where(low, after, before), R * OB, 1)

    def counts(quad):
        found = jnp.zeros((1, span), jnp.int32)
        for spot in range(QUAD):
            block = jnp.clip(first_block + quad * QUAD + spot - R, 0, total - 1)
            found = jnp.where(lane // OB == spot, tally_ref[block], found)
        return found

    def pair(tiles, quad):
        return jnp.concatenate(tiles[quad : quad + 2], axis=1)

    positions = [tile(position_ref, quad) for quad in range(quads + 1)]
    readings = [tile(reading_ref, quad) for quad in range(quads + 1)]
    precisions = [tile(precision_ref, quad) for quad in range(quads + 1)]
    tallies = [counts(quad) for quad in range(quads + 1)]
    wide = lax.broadcasted_iota(jnp.int32, (1, 2 * span), 1)
    for block in range(amount):
        quad, spot = divmod(block, QUAD)
        neighbour = wide // OB - spot
        usable = jnp.zeros((1, 2 * span), jnp.float32)
        for j in range(2 * R + 1):
            there = jnp.where(adjacent_ref[block, j] >= 0, 1.0, 0.0)
            usable = jnp.where(neighbour == j, there, usable)
        distance = (
            ((neighbour - R) * span).astype(jnp.float32)
            + pair(positions, quad).astype(jnp.float32)
            - 0.5 * (span - 1)
        )
        decay = jnp.exp(-0.5 * (distance / LOC) ** 2)
        active = jnp.where(wide % OB < pair(tallies, quad), usable, 0.0)
        weight = pair(precisions, quad) * decay * active
        weight_ref[block : block + 1, :] = jnp.sqrt(weight / (members - 1.0))
        shown_ref[block : block + 1, :] = pair(readings, quad)
    edge = jnp.where(low, positions[quads], positions[0])
    for quad in range(quads):
        quad_ref[quad : quad + 1, :] = positions[quad] if quad else edge


def window_terms(reading, precision, position, tally, adjacent, members):
    amount = adjacent.shape[0]
    lanes = QUAD * OB
    vmem = pl.BlockSpec(memory_space=pltpu.VMEM)
    smem = pl.BlockSpec(memory_space=pltpu.SMEM)
    terms = jax.ShapeDtypeStruct((amount, 2 * lanes), jnp.float32)
    return pl.pallas_call(
        functools.partial(terms_kernel, amount, members),
        out_shape=[terms, terms, jax.ShapeDtypeStruct((amount // QUAD, lanes), jnp.int32)],
        in_specs=[vmem, vmem, vmem, smem, smem],
        out_specs=[vmem, vmem, vmem],
    )(*(array.reshape(-1, lanes) for array in (reading, precision, position)), tally, adjacent)


def part_kernel(fields_ref, position_ref, sent_ref, held_ref, sems):
    devices = sent_ref.shape[0]
    cells = fields_ref.shape[1] // devices
    span = PARTITION_SPAN
    half = R * span
    quads = cells // (QUAD * span)
    low = lax.broadcasted_iota(jnp.int32, (1, span), 1) < R * OB
    into, out = [], []
    for device in range(devices):
        source = fields_ref.at[:, pl.ds(device * cells, cells)]
        into.append(pltpu.make_async_copy(source, held_ref.at[device, :, pl.ds(0, cells)], sems.at[device]))
        out.append(pltpu.make_async_copy(held_ref.at[device], sent_ref.at[device], sems.at[devices + device]))
    for copy in into:
        copy.start()
    for copy in into:
        copy.wait()
    for device in range(devices):
        left, right = max(device - 1, 0), min(device + 1, devices - 1)
        before = position_ref[left * quads + quads - 1 : (left + 1) * quads, :]
        after = position_ref[right * quads : right * quads + 1, :]
        position = pltpu.roll(jnp.where(low, after, before), R * OB, 1)
        blocks = [(left, cells - half + spot * span) for spot in range(R)]
        blocks += [(right, spot * span) for spot in range(R)]
        fields = [held_ref[owner, :, start : start + span] for owner, start in blocks]
        held_ref[device, :, cells : cells + span] = picked(fields, position)
        out[device].start()
    for copy in out:
        copy.wait()


def turn_kernel(rows, parts, *refs):
    given, made = refs[:-parts], refs[-parts:]
    width = given[0].shape[1]
    many = made[0].shape[0] // rows
    for number, source in enumerate(given):
        side, i = divmod(number, many)
        for j, target in enumerate(made):
            target[i * rows : (i + 1) * rows, side * width : (side + 1) * width] = source[j * rows : (j + 1) * rows, :]


def place_kernel(distances, cells, starts, *refs):
    *parts, result_ref, sems = refs
    place = lax.axis_index("state")
    rows = result_ref.shape[0]
    width = QUAD * PARTITION_SPAN
    started = []
    for i, part in enumerate(parts):
        for j in range(part.shape[0] // rows):
            device = place ^ distances[i][j] if distances else j
            for k, start in enumerate(starts):
                source = part.at[pl.ds(j * rows, rows), pl.ds(k * width, width)]
                target = result_ref.at[:, pl.ds(pl.multiple_of(device * cells + start, width), width)]
                started.append(pltpu.make_async_copy(source, target, sems.at[len(started)]))
                started[-1].start()
    for copy in started:
        copy.wait()


def place_more_kernel(distances, cells, starts, *refs):
    *parts, _, result_ref, sems = refs
    place_kernel(distances, cells, starts, *parts, result_ref, sems)


def reordered(ref, devices):
    place = lax.axis_index("state")
    rows = ref.shape[0] // devices
    starts = [pl.multiple_of((place ^ distance) * rows, rows) for distance in range(devices)]
    return jnp.concatenate([ref[pl.ds(start, rows), :] for start in starts], axis=0)


def blocks_of(fields, here, there, first, weight_ref, reading_ref):
    span = PARTITION_SPAN
    seen = jnp.concatenate([here, there], axis=1)
    blocks = []
    for spot in range(QUAD):
        terms = [ref[pl.ds(first + spot, 1), :] for ref in (weight_ref, reading_ref)]
        blocks.append((fields[:, spot * span : (spot + 1) * span], seen, *terms))
    return blocks


def head_kernel(quad, devices, fields_ref, here_ref, there_ref, beyond_ref, weight_ref, reading_ref, *results):
    span = PARTITION_SPAN
    fields, here, there, beyond = [
        reordered(ref, devices) for ref in (fields_ref, here_ref, there_ref, beyond_ref)
    ]
    if quad == 0:
        left = lax.broadcasted_iota(jnp.int32, here.shape, 1) < R * OB
        here = jnp.where(left, beyond, here)
    for spot, result in enumerate(updated(blocks_of(fields, here, there, quad * QUAD, weight_ref, reading_ref))):
        start = 0
        for result_ref in results:
            rows = result_ref.shape[0]
            result_ref[:, spot * span : (spot + 1) * span] = result[start : start + rows]
            start += rows


def tail_kernel(fields_ref, here_ref, there_ref, beyond_ref, weight_ref, reading_ref, result_ref):
    span = PARTITION_SPAN
    step, steps = pl.program_id(0), pl.num_programs(0)
    right = lax.broadcasted_iota(jnp.int32, here_ref.shape, 1) >= R * OB
    there = jnp.where(right & (step == steps - 1), beyond_ref[...], there_ref[...])
    first = weight_ref.shape[0] + (step - steps) * QUAD
    blocks = blocks_of(fields_ref[...], here_ref[...], there, first, weight_ref, reading_ref)
    for spot, result in enumerate(updated(blocks)):
        result_ref[:, spot * span : (spot + 1) * span] = result


def in_stages(fields, positions, quad_position, root_weight, reading, devices):
    own_members, all_cells = fields.shape
    cells = all_cells // devices
    amount = cells // PARTITION_SPAN
    members = own_members * devices
    outer = devices // INNER
    quads = amount // QUAD
    width = QUAD * PARTITION_SPAN
    lanes = QUAD * OB
    early = quads // 2
    late = quads - early
    anywhere = pl.BlockSpec(memory_space=pl.ANY)
    vmem = pl.BlockSpec(memory_space=pltpu.VMEM)
    whole = jax.ShapeDtypeStruct((own_members, all_cells), jnp.float32)

    def call(kernel, inputs, outputs, grant=16, **options):
        return pl.pallas_call(
            kernel,
            out_shape=outputs,
            in_specs=inputs,
            compiler_params=pltpu.CompilerParams(vmem_limit_bytes=grant << 20),
            cost_estimate=pl.CostEstimate(flops=1, bytes_accessed=1, transcendentals=0),
            **options,
        )

    def columns(size, index):
        return pl.BlockSpec((members, size), lambda step: (0, index))

    def full(array):
        return pl.BlockSpec(array.shape, lambda step: (0, 0))

    def group(parts, size):
        return jax.ShapeDtypeStruct((members // parts, size), jnp.float32)

    def swapped(arrays, unit):
        pairs = [[(i, i ^ (unit * k)) for i in range(devices)] for k in range(len(arrays))]
        return [arrays[0]] + [lax.ppermute(arrays[k], "state", pairs[k]) for k in range(1, len(arrays))]

    def placed(parts, order, starts, result):
        options = dict(out_specs=anywhere, scratch_shapes=[pltpu.SemaphoreType.DMA((devices * len(starts),))])
        if result is None:
            kernel = functools.partial(place_kernel, order, cells, starts)
            return call(kernel, [vmem] * len(parts), whole, **options)(*parts)
        kernel = functools.partial(place_more_kernel, order, cells, starts)
        aliases = {len(parts): 0}
        return call(kernel, [vmem] * len(parts) + [anywhere], whole, input_output_aliases=aliases, **options)(
            *parts, result
        )

    def exchanged(array):
        return lax.all_to_all(array, "state", split_axis=0, concat_axis=0, tiled=True)

    sent = call(
        part_kernel,
        [anywhere, vmem],
        jax.ShapeDtypeStruct((devices, own_members, cells + lanes), jnp.float32),
        grant=56,
        out_specs=anywhere,
        scratch_shapes=[
            pltpu.VMEM((devices, own_members, cells + lanes), jnp.float32),
            pltpu.SemaphoreType.DMA((2 * devices,)),
        ],
    )(fields, positions.reshape(-1, lanes))
    fields = exchanged(sent).reshape(members, cells + lanes)
    terms = [root_weight, reading]
    seen = call(
        pick_kernel, [vmem, vmem], jax.ShapeDtypeStruct((members, quads * lanes), jnp.float32), out_specs=vmem
    )(fields, quad_position)

    sets = []
    for quad in range(early):
        groups = call(
            functools.partial(head_kernel, quad, devices),
            [
                columns(width, quad),
                columns(lanes, quad),
                columns(lanes, quad + 1),
                columns(lanes, cells // lanes),
                *[full(term) for term in terms],
            ],
            [group(outer, width)] * outer,
            grant=40,
            grid=(1,),
            out_specs=[pl.BlockSpec((members // outer, width), lambda step: (0, 0))] * outer,
        )(fields, seen, seen, fields, *terms)
        seen, groups = lax.optimization_barrier((seen, groups))
        sets.append(swapped(groups, INNER))

    ends = call(
        tail_kernel,
        [
            pl.BlockSpec((members, width), lambda step: (0, early + step)),
            pl.BlockSpec((members, lanes), lambda step: (0, early + step)),
            pl.BlockSpec((members, lanes), lambda step: (0, (early + step + 1) % quads)),
            columns(lanes, cells // lanes),
            *[full(term) for term in terms],
        ],
        jax.ShapeDtypeStruct((members, late * width), jnp.float32),
        grant=40,
        grid=(late,),
        out_specs=pl.BlockSpec((members, width), lambda step: (0, step)),
    )(fields, seen, seen, fields, *terms)
    ends, sets = lax.optimization_barrier((ends, sets))
    ends = exchanged(ends.reshape(devices, own_members, late * width)).reshape(members, late * width)

    near = call(
        functools.partial(turn_kernel, own_members, INNER),
        [vmem] * (outer * early),
        [group(INNER, early * width)] * INNER,
        out_specs=[vmem] * INNER,
    )(*[array for arrays in sets for array in arrays])
    order = [[far * INNER + close for far in range(outer)] for close in range(INNER)]
    result = placed(swapped(near, 1), order, [quad * width for quad in range(early)], None)
    return placed([ends], None, [quad * width for quad in range(early, quads)], result)


def by_all_to_all(fields, _, quad_position, root_weight, reading, devices):
    own_members, all_cells = fields.shape
    cells = all_cells // devices
    amount = cells // PARTITION_SPAN
    members = own_members * devices
    span = PARTITION_SPAN
    sent = fields.reshape(own_members, devices, cells).transpose(1, 0, 2)
    fields = lax.all_to_all(sent, "state", split_axis=0, concat_axis=0, tiled=True).reshape(members, cells)
    vmem = pl.BlockSpec(memory_space=pltpu.VMEM)
    own_seen = pl.pallas_call(
        pick_kernel,
        out_shape=jax.ShapeDtypeStruct((members, amount * OB), jnp.float32),
        in_specs=[vmem, vmem],
        out_specs=vmem,
        compiler_params=pltpu.CompilerParams(vmem_limit_bytes=16 << 20),
    )(fields, quad_position)
    edge = own_seen[:, : QUAD * OB]
    before = lax.ppermute(edge, "state", [(i, i + 1) for i in range(devices - 1)])
    after = lax.ppermute(edge, "state", [(i + 1, i) for i in range(devices - 1)])
    steps = amount // QUAD

    def whole(*shape):
        return pl.BlockSpec(shape, lambda step: (0, 0))

    analysis = pl.pallas_call(
        update_kernel,
        grid=(steps,),
        out_shape=jax.ShapeDtypeStruct((members, cells), jnp.float32),
        in_specs=[
            pl.BlockSpec((members, QUAD * span), lambda step: (0, step)),
            whole(members, QUAD * OB),
            whole(members, amount * OB),
            whole(members, QUAD * OB),
            whole(amount, 2 * QUAD * OB),
            whole(amount, 2 * QUAD * OB),
        ],
        out_specs=pl.BlockSpec((members, QUAD * span), lambda step: (0, step)),
        compiler_params=pltpu.CompilerParams(vmem_limit_bytes=40 << 20),
    )(fields, before, own_seen, after, root_weight, reading)
    result = lax.all_to_all(
        analysis.reshape(devices, own_members, cells), "state", split_axis=0, concat_axis=0, tiled=True
    )
    return result.transpose(1, 0, 2).reshape(own_members, all_cells)


def body(
    background_draws_table,
    measurement_reading,
    measurement_precision,
    sensed_point_position,
    measurement_tally,
    adjacent_tile_number,
):
    devices = lax.axis_size("state")
    root_weight, reading, quad_position = window_terms(
        measurement_reading,
        measurement_precision,
        sensed_point_position,
        measurement_tally,
        adjacent_tile_number,
        background_draws_table.shape[0] * devices,
    )
    way = in_stages if devices == INNER * INNER else by_all_to_all
    return way(background_draws_table, sensed_point_position, quad_position, root_weight, reading, devices)


def solution(mesh):
    return jax.shard_map(
        body,
        mesh=mesh,
        in_specs=(
            P("state", "groups"),
            P("groups", None),
            P("groups", None),
            P("groups", None),
            P("groups"),
            P(("groups", "state"), None),
        ),
        out_specs=P("state", "groups"),
        check_vma=False,
    )
```

time: 148 us -> 131 us (0.89)
  blocking collectives: 62.4 us -> 0 us
  waiting for transfers between devices: 39.6 us -> 62.2 us
  starting transfers between devices: 12.1 us -> 30.3 us
  Pallas kernels: 25.8 us -> 32.7 us
  local copies, waits for them, and re-layouts: 6.82 us -> 4.55 us
    all_to_all x1 -> x0, blocking collectives: 62.4 us -> none  [body(): lax.all_to_all(analysis.reshape(devices, own_members, cells), 'state', sp...]
    ppermute x2 -> x9, waiting for transfers between devices: 0.84 us -> 22.9 us  [swapped(): lax.ppermute(arrays[k], 'state', pairs[k])]
    ppermute x2 -> x9, starting transfers between devices: 4.6 us -> 18 us  [swapped(): lax.ppermute(arrays[k], 'state', pairs[k])]
    pallas_call x2 -> x9, Pallas kernels: 25.8 us -> 32.7 us  [the longest x1 12.2 us: in_stages(): call(tail_kernel, [pl.BlockSpec((members, width), lambda step: (0, early...]
    all_to_all x1 -> x2, starting transfers between devices: 7.53 us -> 12.3 us  [exchanged(): lax.all_to_all(array, 'state', split_axis=0, concat_axis=0, tiled=True)]
    reshape x6 -> x3, local copies, waits for them, and re-layouts: 4.8 us -> 2.12 us  [the longest x2 1.41 us: window_terms(): array.reshape(-1, lanes)]
    unnamed x10 -> x16, local copies, waits for them, and re-layouts: 0.02 us -> 2.43 us
    all_to_all x1 -> x2, waiting for transfers between devices: 38.7 us -> 39.3 us  [exchanged(): lax.all_to_all(array, 'state', split_axis=0, concat_axis=0, tiled=True)]
  transfers between devices with their start and end apart: 3 -> 11, of which waited for: 2 -> 3; matrix products, arithmetic and copies ran while one was open for 2% -> 2% of each run, Pallas kernels for 0% -> 16%
where the time goes in v2:
time: 131 us; the launch traced here: 130 us
  waiting for transfers between devices  62.2 us (47%)
  Pallas kernels  32.7 us (25%)
  starting transfers between devices  30.3 us (23%)
  local copies, waits for them, and re-layouts  4.55 us (3%)
    all_to_all x2, waiting for transfers between devices, exchanged(): lax.all_to_all(array, 'state', split_axis=0, concat_axis=0, tiled=True)  39.3 us
    ppermute x9, waiting for transfers between devices, swapped(): lax.ppermute(arrays[k], 'state', pairs[k])  22.9 us
    ppermute x9, starting transfers between devices, swapped(): lax.ppermute(arrays[k], 'state', pairs[k])  18 us
    all_to_all x2, starting transfers between devices, exchanged(): lax.all_to_all(array, 'state', split_axis=0, concat_axis=0, tiled=True)  12.3 us
    pallas_call x1, Pallas kernels, in_stages(): call(tail_kernel, [pl.BlockSpec((members, width), lambda step: (0, early...  12.2 us
    pallas_call x2, Pallas kernels, in_stages(): call(functools.partial(head_kernel, quad, devices), [columns(width, quad)...  11.4 us
    pallas_call x1, Pallas kernels, in_stages(): call(part_kernel, [anywhere, vmem], jax.ShapeDtypeStruct((devices, own_me...  4.17 us
  transfers between devices with their start and end apart: 11, of which 3 were waited for; matrix products, arithmetic and copies ran while one was open for 2% of the time, Pallas kernels for 16%

profile of v2, /device:TPU:0, one launch (start us, length us, event | category | flops | bytes accessed | tf_op | source)
XLA Modules:
  0.0 130.1 jit_solution(1566008983995806569)
XLA Ops:
  0.0 0.9 copy.12
  0.9 0.7 reshape.19.position_ref
  1.6 4.2 %shard_map.64 = f32[16,16,2176]{2,1,0:T(8,128)} custom-call(f32[16,32768]{1,0:T(8,128)} %fields_ref.1, s32[64,128]{1,0:T(8,128)} %reshape.19.position_ref), custom_call_target="tpu_custom_call" | custom-call | flops 1 | bytes 1 | tf_op jit(solution)/shard_map/pallas_call | solution.py:360
  5.7 0.0 copy-start.5
  5.8 0.0 copy-start.3
  5.8 0.0 copy-start.4
  5.8 7.5 %all-to-all-start = ((f32[16,16,2176]{2,1,0:T(8,128)}), f32[16,16,2176]{2,1,0:T(8,128)S(1)}, u32[]{:S(2)}, u32[]{:S(2)}) async-start(f32[16,16,2176]{2,1,0:T(8,128)} %shard_map.64), calls=%async_computation | async-start | bytes 4456448 | tf_op jit(solution)/shard_map/all_to_all | solution.py:358
  13.3 0.0 copy-done.5
  13.3 0.7 copy.15.adjacent_ref
  14.0 0.0 copy-done.3
  14.0 0.1 copy.13
  14.1 0.7 reshape.21.reading_ref
  14.8 0.0 copy-done.4
  14.8 0.1 copy.14
  14.9 0.7 reshape.22.precision_ref
  15.6 1.8 %shard_map.65 = (f32[16,256]{1,0:T(8,128)}, f32[16,256]{1,0:T(8,128)}, s32[4,128]{1,0:T(4,128)}) custom-call(f32[64,128]{1,0:T(8,128)} %reshape.21.reading_ref, f32[64,128]{1,0:T(8,128)} %reshape.22.precision_ref, s32[64,128]{1,0:T(8,128)} %reshape.19.position_ref, s32[256]{0:T(256)} %tally_ref.1, s32[16,5]{1,0:T(8,128)} %copy.15.adjacent_ref), custom_call_target="tpu_custom_call" | custom-call | tf_op jit(solution)/shard_map/pallas_call | solution.py:193
  17.4 0.0 copy-start
  17.4 39.3 %all-to-all-done = f32[16,16,2176]{2,1,0:T(8,128)S(1)} async-done(((f32[16,16,2176]{2,1,0:T(8,128)}), f32[16,16,2176]{2,1,0:T(8,128)S(1)}, u32[]{:S(2)}, u32[]{:S(2)}) %all-to-all-start) | async-done | bytes 2228256 | tf_op jit(solution)/shard_map/all_to_all | solution.py:358
  56.7 0.7 copy-done.2
  57.4 0.6 shard_map.66.here_ref.there_ref
  58.0 0.0 copy-done
  58.0 0.0 copy-done.1
  58.0 5.6 %shard_map.67 = (f32[64,512]{1,0:T(8,128)S(1)}, f32[64,512]{1,0:T(8,128)S(1)}, f32[64,512]{1,0:T(8,128)S(1)}, f32[64,512]{1,0:T(8,128)S(1)}) custom-call(f32[256,2176]{1,0:T(8,128)S(1)} %bitcast.4, f32[256,512]{1,0:T(8,128)S(1)} %shard_map.66.here_ref.there_ref, f32[256,512]{1,0:T(8,128)S(1)} %shard_map.66.here_ref.there_ref, f32[256,2176]{1,0:T(8,128)S(1)} %bitcast.5, ...), custom_call_target="tpu_custom_call" | custom-call | flops 1 | bytes 1 | tf_op jit(solution)/shard_map/pallas_call | solution.py:379
  63.6 7.3 %collective-permute-start = (f32[64,512]{1,0:T(8,128)S(1)}, f32[64,512]{1,0:T(8,128)S(1)}, u32[]{:S(2)}, u32[]{:S(2)}) collective-permute-start(f32[64,512]{1,0:T(8,128)S(1)} %get-tuple-element.53), channel_id=1, source_target_pairs={{0,4},{1,5},{2,6},{3,7},{4,0},{5,1},{6,2},{7,3},{8,12},{9,13},{10,... | collective-permute-start | bytes 393224 | tf_op jit(solution)/shard_map/ppermute | solution.py:344
  70.9 2.7 %collective-permute-start.1 = (f32[64,512]{1,0:T(8,128)S(1)}, f32[64,512]{1,0:T(8,128)S(1)}, u32[]{:S(2)}, u32[]{:S(2)}) collective-permute-start(f32[64,512]{1,0:T(8,128)S(1)} %get-tuple-element.54), channel_id=1, source_target_pairs={{0,8},{1,9},{2,10},{3,11},{4,12},{5,13},{6,14},{7,15},{8,0},{9,1},... | collective-permute-start | bytes 393224 | tf_op jit(solution)/shard_map/ppermute | solution.py:344
  73.7 1.4 %collective-permute-start.2 = (f32[64,512]{1,0:T(8,128)S(1)}, f32[64,512]{1,0:T(8,128)S(1)}, u32[]{:S(2)}, u32[]{:S(2)}) collective-permute-start(f32[64,512]{1,0:T(8,128)S(1)} %get-tuple-element.55), channel_id=1, source_target_pairs={{0,12},{1,13},{2,14},{3,15},{4,8},{5,9},{6,10},{7,11},{8,4},{9,5},... | collective-permute-start | bytes 393224 | tf_op jit(solution)/shard_map/ppermute | solution.py:344
  75.1 5.8 %shard_map.68 = (f32[64,512]{1,0:T(8,128)S(1)}, f32[64,512]{1,0:T(8,128)S(1)}, f32[64,512]{1,0:T(8,128)S(1)}, f32[64,512]{1,0:T(8,128)S(1)}) custom-call(f32[256,2176]{1,0:T(8,128)S(1)} %bitcast.6, f32[256,512]{1,0:T(8,128)S(1)} %shard_map.66.here_ref.there_ref, f32[256,512]{1,0:T(8,128)S(1)} %shard_map.66.here_ref.there_ref, f32[256,2176]{1,0:T(8,128)S(1)} %bitcast.7, ...), custom_call_target="tpu_custom_call" | custom-call | flops 1 | bytes 1 | tf_op jit(solution)/shard_map/pallas_call | solution.py:379
  80.8 0.6 collective-permute-start.3
  81.5 2.4 %collective-permute-start.4 = (f32[64,512]{1,0:T(8,128)S(1)}, f32[64,512]{1,0:T(8,128)S(1)}, u32[]{:S(2)}, u32[]{:S(2)}) collective-permute-start(f32[64,512]{1,0:T(8,128)S(1)} %get-tuple-element.58), channel_id=1, source_target_pairs={{0,8},{1,9},{2,10},{3,11},{4,12},{5,13},{6,14},{7,15},{8,0},{9,1},... | collective-permute-start | bytes 393224 | tf_op jit(solution)/shard_map/ppermute | solution.py:344
  83.9 0.0 collective-permute-done.refs_1_
  83.9 1.4 %collective-permute-start.5 = (f32[64,512]{1,0:T(8,128)S(1)}, f32[64,512]{1,0:T(8,128)S(1)}, u32[]{:S(2)}, u32[]{:S(2)}) collective-permute-start(f32[64,512]{1,0:T(8,128)S(1)} %get-tuple-element.59), channel_id=1, source_target_pairs={{0,12},{1,13},{2,14},{3,15},{4,8},{5,9},{6,10},{7,11},{8,4},{9,5},... | collective-permute-start | bytes 393224 | tf_op jit(solution)/shard_map/ppermute | solution.py:344
  85.3 12.2 %shard_map.69 = f32[256,1024]{1,0:T(8,128)} custom-call(f32[256,2176]{1,0:T(8,128)S(1)} %bitcast.8, f32[256,512]{1,0:T(8,128)S(1)} %shard_map.66.here_ref.there_ref, f32[256,512]{1,0:T(8,128)S(1)} %shard_map.66.here_ref.there_ref, f32[256,2176]{1,0:T(8,128)S(1)} %bitcast.9, f32[16,256]{1,0:T(8,128)S(1)} %copy-done, f32[16,256]{1,0:T(8,128)S(1)} %copy-done.1), custom_call_target="tpu_custom_call" | custom-call | flops 1 | bytes 1 | tf_op jit(solution)/shard_map/pallas_call | solution.py:396
  97.5 0.0 collective-permute-done.1.refs_2_
  97.5 0.0 collective-permute-done.2.refs_3_
  97.5 0.0 collective-permute-done.3.refs_5_
  97.5 0.0 collective-permute-done.4.refs_6_
  97.5 0.0 collective-permute-done.5.refs_7_
  97.5 4.8 %all-to-all-start.1 = ((f32[16,16,1024]{2,1,0:T(8,128)}), f32[16,16,1024]{2,1,0:T(8,128)S(1)}, u32[]{:S(2)}, u32[]{:S(2)}) async-start(f32[16,16,1024]{2,1,0:T(8,128)} %bitcast.1), calls=%async_computation.1 | async-start | bytes 2097152 | tf_op jit(solution)/shard_map/all_to_all | solution.py:358
  102.3 0.1 shard_map.70
  102.4 0.5 collective-permute-start.6
  102.9 1.7 %collective-permute-start.7 = (f32[64,1024]{1,0:T(8,128)S(1)}, f32[64,1024]{1,0:T(8,128)S(1)}, u32[]{:S(2)}, u32[]{:S(2)}) collective-permute-start(f32[64,1024]{1,0:T(8,128)S(1)} %get-tuple-element.71), channel_id=1, source_target_pairs={{0,2},{1,3},{2,0},{3,1},{4,6},{5,7},{6,4},{7,5},{8,10},{9,11},{10,... | collective-permute-start | bytes 786440 | tf_op jit(solution)/shard_map/ppermute | solution.py:344
  104.6 0.0 collective-permute-start.8
  104.6 0.0 collective-permute-done.6.refs_1_
  104.6 15.4 %collective-permute-done.7.refs_2_ = f32[64,1024]{1,0:T(8,128)S(1)} collective-permute-done((f32[64,1024]{1,0:T(8,128)S(1)}, f32[64,1024]{1,0:T(8,128)S(1)}, u32[]{:S(2)}, u32[]{:S(2)}) %collective-permute-start.7) | collective-permute-done | bytes 262176 | tf_op jit(solution)/shard_map/ppermute | solution.py:344
  120.0 7.5 %collective-permute-done.8.refs_3_ = f32[64,1024]{1,0:T(8,128)S(1)} collective-permute-done((f32[64,1024]{1,0:T(8,128)S(1)}, f32[64,1024]{1,0:T(8,128)S(1)}, u32[]{:S(2)}, u32[]{:S(2)}) %collective-permute-start.8) | collective-permute-done | bytes 262176 | tf_op jit(solution)/shard_map/ppermute | solution.py:344
  127.4 1.2 shard_map.71.refs_1_
  128.7 0.0 all-to-all-done.1
  128.7 1.2 shard_map.72
  (2 shorter events, 0.0 us)
Async XLA Ops:
  5.7 7.6 %copy-start.5 = (s32[16,5]{0,1:T(8,128)S(1)}, s32[16,5]{0,1:T(8,128)}, u32[]{:S(2)}) copy-start(s32[16,5]{0,1:T(8,128)} %param.11) | copy-start | bytes 964
  5.8 8.3 %copy-start.3 = (f32[256,32]{0,1:T(8,128)S(1)}, f32[256,32]{0,1:T(8,128)}, u32[]{:S(2)}) copy-start(f32[256,32]{0,1:T(8,128)} %param.7) | copy-start | bytes 98308
  5.8 9.0 %copy-start.4 = (f32[256,32]{0,1:T(8,128)S(1)}, f32[256,32]{0,1:T(8,128)}, u32[]{:S(2)}) copy-start(f32[256,32]{0,1:T(8,128)} %param.8) | copy-start | bytes 98308
  5.8 50.9 %all-to-all-start = ((f32[16,16,2176]{2,1,0:T(8,128)}), f32[16,16,2176]{2,1,0:T(8,128)S(1)}, u32[]{:S(2)}, u32[]{:S(2)}) async-start(f32[16,16,2176]{2,1,0:T(8,128)} %shard_map.64), calls=%async_computation | async-start | bytes 4456448 | tf_op jit(solution)/shard_map/all_to_all | solution.py:358
  17.4 40.6 %copy-start = (f32[16,256]{1,0:T(8,128)S(1)}, f32[16,256]{1,0:T(8,128)}, u32[]{:S(2)}) copy-start(f32[16,256]{1,0:T(8,128)} %get-tuple-element.40.weight_ref) | copy-start | bytes 49156
  17.4 40.6 %copy-start.1 = (f32[16,256]{1,0:T(8,128)S(1)}, f32[16,256]{1,0:T(8,128)}, u32[]{:S(2)}) copy-start(f32[16,256]{1,0:T(8,128)} %get-tuple-element.41.reading_ref) | copy-start | bytes 49156
  56.7 0.7 copy-start.2
  63.6 20.3 %collective-permute-start = (f32[64,512]{1,0:T(8,128)S(1)}, f32[64,512]{1,0:T(8,128)S(1)}, u32[]{:S(2)}, u32[]{:S(2)}) collective-permute-start(f32[64,512]{1,0:T(8,128)S(1)} %get-tuple-element.53), channel_id=1, source_target_pairs={{0,4},{1,5},{2,6},{3,7},{4,0},{5,1},{6,2},{7,3},{8,12},{9,13},{10,... | collective-permute-start | bytes 393224 | tf_op jit(solution)/shard_map/ppermute | solution.py:344
  70.9 26.6 %collective-permute-start.1 = (f32[64,512]{1,0:T(8,128)S(1)}, f32[64,512]{1,0:T(8,128)S(1)}, u32[]{:S(2)}, u32[]{:S(2)}) collective-permute-start(f32[64,512]{1,0:T(8,128)S(1)} %get-tuple-element.54), channel_id=1, source_target_pairs={{0,8},{1,9},{2,10},{3,11},{4,12},{5,13},{6,14},{7,15},{8,0},{9,1},... | collective-permute-start | bytes 393224 | tf_op jit(solution)/shard_map/ppermute | solution.py:344
  73.7 23.8 %collective-permute-start.2 = (f32[64,512]{1,0:T(8,128)S(1)}, f32[64,512]{1,0:T(8,128)S(1)}, u32[]{:S(2)}, u32[]{:S(2)}) collective-permute-start(f32[64,512]{1,0:T(8,128)S(1)} %get-tuple-element.55), channel_id=1, source_target_pairs={{0,12},{1,13},{2,14},{3,15},{4,8},{5,9},{6,10},{7,11},{8,4},{9,5},... | collective-permute-start | bytes 393224 | tf_op jit(solution)/shard_map/ppermute | solution.py:344
  80.8 16.7 %collective-permute-start.3 = (f32[64,512]{1,0:T(8,128)S(1)}, f32[64,512]{1,0:T(8,128)S(1)}, u32[]{:S(2)}, u32[]{:S(2)}) collective-permute-start(f32[64,512]{1,0:T(8,128)S(1)} %get-tuple-element.57), channel_id=1, source_target_pairs={{0,4},{1,5},{2,6},{3,7},{4,0},{5,1},{6,2},{7,3},{8,12},{9,13},{10,... | collective-permute-start | bytes 393224 | tf_op jit(solution)/shard_map/ppermute | solution.py:344
  81.5 16.1 %collective-permute-start.4 = (f32[64,512]{1,0:T(8,128)S(1)}, f32[64,512]{1,0:T(8,128)S(1)}, u32[]{:S(2)}, u32[]{:S(2)}) collective-permute-start(f32[64,512]{1,0:T(8,128)S(1)} %get-tuple-element.58), channel_id=1, source_target_pairs={{0,8},{1,9},{2,10},{3,11},{4,12},{5,13},{6,14},{7,15},{8,0},{9,1},... | collective-permute-start | bytes 393224 | tf_op jit(solution)/shard_map/ppermute | solution.py:344
  83.9 13.6 %collective-permute-start.5 = (f32[64,512]{1,0:T(8,128)S(1)}, f32[64,512]{1,0:T(8,128)S(1)}, u32[]{:S(2)}, u32[]{:S(2)}) collective-permute-start(f32[64,512]{1,0:T(8,128)S(1)} %get-tuple-element.59), channel_id=1, source_target_pairs={{0,12},{1,13},{2,14},{3,15},{4,8},{5,9},{6,10},{7,11},{8,4},{9,5},... | collective-permute-start | bytes 393224 | tf_op jit(solution)/shard_map/ppermute | solution.py:344
  97.5 31.1 %all-to-all-start.1 = ((f32[16,16,1024]{2,1,0:T(8,128)}), f32[16,16,1024]{2,1,0:T(8,128)S(1)}, u32[]{:S(2)}, u32[]{:S(2)}) async-start(f32[16,16,1024]{2,1,0:T(8,128)} %bitcast.1), calls=%async_computation.1 | async-start | bytes 2097152 | tf_op jit(solution)/shard_map/all_to_all | solution.py:358
  102.4 2.2 %collective-permute-start.6 = (f32[64,1024]{1,0:T(8,128)S(1)}, f32[64,1024]{1,0:T(8,128)S(1)}, u32[]{:S(2)}, u32[]{:S(2)}) collective-permute-start(f32[64,1024]{1,0:T(8,128)S(1)} %get-tuple-element.70), channel_id=1, source_target_pairs={{0,1},{1,0},{2,3},{3,2},{4,5},{5,4},{6,7},{7,6},{8,9},{9,8},{10,11... | collective-permute-start | bytes 786440 | tf_op jit(solution)/shard_map/ppermute | solution.py:344
  102.9 17.1 %collective-permute-start.7 = (f32[64,1024]{1,0:T(8,128)S(1)}, f32[64,1024]{1,0:T(8,128)S(1)}, u32[]{:S(2)}, u32[]{:S(2)}) collective-permute-start(f32[64,1024]{1,0:T(8,128)S(1)} %get-tuple-element.71), channel_id=1, source_target_pairs={{0,2},{1,3},{2,0},{3,1},{4,6},{5,7},{6,4},{7,5},{8,10},{9,11},{10,... | collective-permute-start | bytes 786440 | tf_op jit(solution)/shard_map/ppermute | solution.py:344
  104.6 22.9 %collective-permute-start.8 = (f32[64,1024]{1,0:T(8,128)S(1)}, f32[64,1024]{1,0:T(8,128)S(1)}, u32[]{:S(2)}, u32[]{:S(2)}) collective-permute-start(f32[64,1024]{1,0:T(8,128)S(1)} %get-tuple-element.72), channel_id=1, source_target_pairs={{0,3},{1,2},{2,1},{3,0},{4,7},{5,6},{6,5},{7,4},{8,11},{9,10},{10,... | collective-permute-start | bytes 786440 | tf_op jit(solution)/shard_map/ppermute | solution.py:344

commit v3 on v2

--- a/solution.py
+++ b/solution.py
@@ -108,6 +108,31 @@
         seen_ref[:, quad * span : (quad + 1) * span] = picked(fields, position_ref[quad : quad + 1, :])
 
 
+def pick_first_kernel(fields_ref, position_ref, seen_ref):
+    span = PARTITION_SPAN
+    amount = fields_ref.shape[1] // span - 1
+    beyond = fields_ref[:, amount * span :]
+    low = lax.broadcasted_iota(jnp.int32, beyond.shape, 1) < R * OB
+    for quad in range(seen_ref.shape[1] // span):
+        blocks = [max(quad * QUAD + spot - R, 0) for spot in range(QUAD)]
+        fields = [fields_ref[:, block * span : (block + 1) * span] for block in blocks]
+        found = picked(fields, position_ref[quad : quad + 1, :])
+        seen_ref[:, quad * span : (quad + 1) * span] = found if quad else jnp.where(low, beyond, found)
+
+
+def pick_second_kernel(fields_ref, beyond_ref, position_ref, seen_ref):
+    span = PARTITION_SPAN
+    quads = position_ref.shape[0]
+    amount = fields_ref.shape[1] // span
+    low = lax.broadcasted_iota(jnp.int32, beyond_ref.shape, 1) < R * OB
+    for index in range(seen_ref.shape[1] // span):
+        blocks = [min(index * QUAD + spot, amount - 1) for spot in range(QUAD)]
+        fields = [fields_ref[:, block * span : (block + 1) * span] for block in blocks]
+        quad = (quads - seen_ref.shape[1] // span + 1 + index) % quads
+        found = picked(fields, position_ref[quad : quad + 1, :])
+        seen_ref[:, index * span : (index + 1) * span] = found if quad else jnp.where(low, found, beyond_ref[...])
+
+
 def update_kernel(fields_ref, before_ref, own_ref, after_ref, weight_ref, reading_ref, result_ref):
     members, span = before_ref.shape
     step = pl.program_id(0)
@@ -198,33 +223,62 @@
     )(*(array.reshape(-1, lanes) for array in (reading, precision, position)), tally, adjacent)
 
 
-def part_kernel(fields_ref, position_ref, sent_ref, held_ref, sems):
-    devices = sent_ref.shape[0]
+def copied(copies):
+    for copy in copies:
+        copy.start()
+    return copies
+
+
+def into_held(fields_ref, held_ref, sems, start, size):
+    devices = held_ref.shape[0]
     cells = fields_ref.shape[1] // devices
-    span = PARTITION_SPAN
-    half = R * span
-    quads = cells // (QUAD * span)
-    low = lax.broadcasted_iota(jnp.int32, (1, span), 1) < R * OB
-    into, out = [], []
-    for device in range(devices):
-        source = fields_ref.at[:, pl.ds(device * cells, cells)]
-        into.append(pltpu.make_async_copy(source, held_ref.at[device, :, pl.ds(0, cells)], sems.at[device]))
-        out.append(pltpu.make_async_copy(held_ref.at[device], sent_ref.at[device], sems.at[devices + device]))
-    for copy in into:
-        copy.start()
-    for copy in into:
+    sources = [fields_ref.at[:, pl.ds(device * cells + start, size)] for device in range(devices)]
+    targets = [held_ref.at[device, :, pl.ds(0, size)] for device in range(devices)]
+    return copied([pltpu.make_async_copy(*pair, sems.at[index]) for index, pair in enumerate(zip(sources, targets))])
+
+
+def first_part_kernel(split, fields_ref, position_ref, sent_ref, held_ref, sems):
+    devices, rows, _ = sent_ref.shape
+    cells = fields_ref.shape[1] // devices
+    span = PARTITION_SPAN
+    amount = cells // span
+    into = into_held(fields_ref, held_ref, sems, 0, cells)
+
+    def out(number, some, start, size, to):
+        source = held_ref.at[some, :, pl.ds(start, size)]
+        target = sent_ref.at[some, :, pl.ds(to, size)]
+        return copied([pltpu.make_async_copy(source, target, sems.at[devices + number])])
+
+    away = []
+    for device, copy in enumerate(into):
         copy.wait()
-    for device in range(devices):
-        left, right = max(device - 1, 0), min(device + 1, devices - 1)
-        before = position_ref[left * quads + quads - 1 : (left + 1) * quads, :]
-        after = position_ref[right * quads : right * quads + 1, :]
-        position = pltpu.roll(jnp.where(low, after, before), R * OB, 1)
-        blocks = [(left, cells - half + spot * span) for spot in range(R)]
-        blocks += [(right, spot * span) for spot in range(R)]
-        fields = [held_ref[owner, :, start : start + span] for owner, start in blocks]
-        held_ref[device, :, cells : cells + span] = picked(fields, position)
-        out[device].start()
-    for copy in out:
+        if device % INNER == INNER - 1:
+            away += out(len(away), pl.ds(device + 1 - INNER, INNER), 0, split, 0)
+
+    def shifted(array, distance):
+        if distance > 0:
+            return jnp.concatenate([array[:distance], array[:-distance]], axis=0)
+        return jnp.concatenate([array[-distance:], array[distance:]], axis=0)
+
+    beyond = [(amount - R + spot, 1) for spot in range(R)] + [(spot, -1) for spot in range(R)]
+    positions = position_ref[...].T.reshape(devices, amount, OB)
+    position = jnp.concatenate([shifted(positions[:, block], distance) for block, distance in beyond], axis=1)
+    position = jnp.broadcast_to(position[:, None], (devices, rows, span)).reshape(devices * rows, span)
+    fields = [
+        shifted(held_ref[:, :, block * span : (block + 1) * span].reshape(devices * rows, span), distance * rows)
+        for block, distance in beyond
+    ]
+    held_ref[:, :, cells : cells + span] = picked(fields, position).reshape(devices, rows, span)
+    away += out(len(away), pl.ds(0, devices), cells, span, split)
+    for copy in away:
+        copy.wait()
+
+
+def second_part_kernel(split, fields_ref, sent_ref, held_ref, sems):
+    devices, _, size = sent_ref.shape
+    for copy in into_held(fields_ref, held_ref, sems, split, size):
+        copy.wait()
+    for copy in copied([pltpu.make_async_copy(held_ref, sent_ref, sems.at[devices])]):
         copy.wait()
 
 
@@ -238,27 +292,26 @@
             target[i * rows : (i + 1) * rows, side * width : (side + 1) * width] = source[j * rows : (j + 1) * rows, :]
 
 
-def place_kernel(distances, cells, starts, *refs):
+def place_kernel(distances, cells, start, *refs):
     *parts, result_ref, sems = refs
     place = lax.axis_index("state")
     rows = result_ref.shape[0]
-    width = QUAD * PARTITION_SPAN
+    width = parts[0].shape[1]
     started = []
     for i, part in enumerate(parts):
         for j in range(part.shape[0] // rows):
             device = place ^ distances[i][j] if distances else j
-            for k, start in enumerate(starts):
-                source = part.at[pl.ds(j * rows, rows), pl.ds(k * width, width)]
-                target = result_ref.at[:, pl.ds(pl.multiple_of(device * cells + start, width), width)]
-                started.append(pltpu.make_async_copy(source, target, sems.at[len(started)]))
-                started[-1].start()
+            source = part.at[pl.ds(j * rows, rows), :]
+            target = result_ref.at[:, pl.ds(pl.multiple_of(device * cells + start, width), width)]
+            started.append(pltpu.make_async_copy(source, target, sems.at[len(started)]))
+            started[-1].start()
     for copy in started:
         copy.wait()
 
 
-def place_more_kernel(distances, cells, starts, *refs):
+def place_more_kernel(distances, cells, start, *refs):
     *parts, _, result_ref, sems = refs
-    place_kernel(distances, cells, starts, *parts, result_ref, sems)
+    place_kernel(distances, cells, start, *parts, result_ref, sems)
 
 
 def reordered(ref, devices):
@@ -278,14 +331,9 @@
     return blocks
 
 
-def head_kernel(quad, devices, fields_ref, here_ref, there_ref, beyond_ref, weight_ref, reading_ref, *results):
-    span = PARTITION_SPAN
-    fields, here, there, beyond = [
-        reordered(ref, devices) for ref in (fields_ref, here_ref, there_ref, beyond_ref)
-    ]
-    if quad == 0:
-        left = lax.broadcasted_iota(jnp.int32, here.shape, 1) < R * OB
-        here = jnp.where(left, beyond, here)
+def head_kernel(quad, devices, fields_ref, here_ref, there_ref, weight_ref, reading_ref, *results):
+    span = PARTITION_SPAN
+    fields, here, there = [reordered(ref, devices) for ref in (fields_ref, here_ref, there_ref)]
     for spot, result in enumerate(updated(blocks_of(fields, here, there, quad * QUAD, weight_ref, reading_ref))):
         start = 0
         for result_ref in results:
@@ -294,14 +342,15 @@
             start += rows
 
 
-def tail_kernel(fields_ref, here_ref, there_ref, beyond_ref, weight_ref, reading_ref, result_ref):
-    span = PARTITION_SPAN
-    step, steps = pl.program_id(0), pl.num_programs(0)
-    right = lax.broadcasted_iota(jnp.int32, here_ref.shape, 1) >= R * OB
-    there = jnp.where(right & (step == steps - 1), beyond_ref[...], there_ref[...])
-    first = weight_ref.shape[0] + (step - steps) * QUAD
-    blocks = blocks_of(fields_ref[...], here_ref[...], there, first, weight_ref, reading_ref)
-    for spot, result in enumerate(updated(blocks)):
+def tail_kernel(first_ref, begin_ref, end_ref, here_ref, tiles_ref, weight_ref, reading_ref, result_ref):
+    span = PARTITION_SPAN
+    step = pl.program_id(0)
+    begin = jnp.where(step == 0, first_ref[...], begin_ref[...])
+    fields = jnp.concatenate([begin, end_ref[...]], axis=1)
+    here = jnp.where(step == 0, here_ref[...], tiles_ref[:, :span])
+    there = jnp.where(step == 0, tiles_ref[:, :span], tiles_ref[:, span:])
+    first = weight_ref.shape[0] + (step - 2) * QUAD
+    for spot, result in enumerate(updated(blocks_of(fields, here, there, first, weight_ref, reading_ref))):
         result_ref[:, spot * span : (spot + 1) * span] = result
 
 
@@ -314,19 +363,20 @@
     quads = amount // QUAD
     width = QUAD * PARTITION_SPAN
     lanes = QUAD * OB
-    early = quads // 2
-    late = quads - early
+    early = quads - 2
+    late = 2
+    half = R * PARTITION_SPAN
     anywhere = pl.BlockSpec(memory_space=pl.ANY)
     vmem = pl.BlockSpec(memory_space=pltpu.VMEM)
     whole = jax.ShapeDtypeStruct((own_members, all_cells), jnp.float32)
 
-    def call(kernel, inputs, outputs, grant=16, **options):
+    def call(kernel, inputs, outputs, grant=16, cost=1, **options):
         return pl.pallas_call(
             kernel,
             out_shape=outputs,
             in_specs=inputs,
             compiler_params=pltpu.CompilerParams(vmem_limit_bytes=grant << 20),
-            cost_estimate=pl.CostEstimate(flops=1, bytes_accessed=1, transcendentals=0),
+            cost_estimate=pl.CostEstimate(flops=cost, bytes_accessed=1, transcendentals=0),
             **options,
         )
 
@@ -343,12 +393,12 @@
         pairs = [[(i, i ^ (unit * k)) for i in range(devices)] for k in range(len(arrays))]
         return [arrays[0]] + [lax.ppermute(arrays[k], "state", pairs[k]) for k in range(1, len(arrays))]
 
-    def placed(parts, order, starts, result):
-        options = dict(out_specs=anywhere, scratch_shapes=[pltpu.SemaphoreType.DMA((devices * len(starts),))])
+    def placed(parts, order, start, result):
+        options = dict(out_specs=anywhere, scratch_shapes=[pltpu.SemaphoreType.DMA((devices,))])
         if result is None:
-            kernel = functools.partial(place_kernel, order, cells, starts)
+            kernel = functools.partial(place_kernel, order, cells, start)
             return call(kernel, [vmem] * len(parts), whole, **options)(*parts)
-        kernel = functools.partial(place_more_kernel, order, cells, starts)
+        kernel = functools.partial(place_more_kernel, order, cells, start)
         aliases = {len(parts): 0}
         return call(kernel, [vmem] * len(parts) + [anywhere], whole, input_output_aliases=aliases, **options)(
             *parts, result
@@ -357,68 +407,85 @@
     def exchanged(array):
         return lax.all_to_all(array, "state", split_axis=0, concat_axis=0, tiled=True)
 
-    sent = call(
-        part_kernel,
-        [anywhere, vmem],
-        jax.ShapeDtypeStruct((devices, own_members, cells + lanes), jnp.float32),
-        grant=56,
-        out_specs=anywhere,
-        scratch_shapes=[
-            pltpu.VMEM((devices, own_members, cells + lanes), jnp.float32),
-            pltpu.SemaphoreType.DMA((2 * devices,)),
-        ],
-    )(fields, positions.reshape(-1, lanes))
-    fields = exchanged(sent).reshape(members, cells + lanes)
+    split = early * width + half
+    def part(kernel, arguments, size, held):
+        return call(
+            functools.partial(kernel, split),
+            [anywhere] + [vmem] * (len(arguments) - 1),
+            jax.ShapeDtypeStruct((devices, own_members, size), jnp.float32),
+            grant=56,
+            out_specs=anywhere,
+            scratch_shapes=[
+                pltpu.VMEM((devices, own_members, held), jnp.float32),
+                pltpu.SemaphoreType.DMA((2 * devices,)),
+            ],
+        )(*arguments)
+
+    first = part(first_part_kernel, [fields, positions.T], split + lanes, cells + lanes)
+    second = part(second_part_kernel, [fields], cells - split, cells - split)
+    first = exchanged(first).reshape(members, split + lanes)
+    first, second, quad_position, root_weight, reading = lax.optimization_barrier(
+        (first, second, quad_position, root_weight, reading)
+    )
+    second = exchanged(second).reshape(members, cells - split)
     terms = [root_weight, reading]
     seen = call(
-        pick_kernel, [vmem, vmem], jax.ShapeDtypeStruct((members, quads * lanes), jnp.float32), out_specs=vmem
-    )(fields, quad_position)
+        pick_first_kernel,
+        [vmem, vmem],
+        jax.ShapeDtypeStruct((members, (early + 1) * lanes), jnp.float32),
+        out_specs=vmem,
+    )(first, quad_position)
 
     sets = []
     for quad in range(early):
         groups = call(
             functools.partial(head_kernel, quad, devices),
-            [
-                columns(width, quad),
-                columns(lanes, quad),
-                columns(lanes, quad + 1),
-                columns(lanes, cells // lanes),
-                *[full(term) for term in terms],
-            ],
+            [columns(width, quad), columns(lanes, quad), columns(lanes, quad + 1), *[full(term) for term in terms]],
             [group(outer, width)] * outer,
             grant=40,
             grid=(1,),
             out_specs=[pl.BlockSpec((members // outer, width), lambda step: (0, 0))] * outer,
-        )(fields, seen, seen, fields, *terms)
-        seen, groups = lax.optimization_barrier((seen, groups))
+        )(first, seen, seen, *terms)
+        if quad + 1 < early:
+            seen, groups = lax.optimization_barrier((seen, groups))
+        else:
+            _, second = lax.optimization_barrier((groups, second))
         sets.append(swapped(groups, INNER))
 
+    tiles = call(
+        pick_second_kernel,
+        [full(second), columns(lanes, split // lanes), full(quad_position)],
+        jax.ShapeDtypeStruct((members, 2 * lanes), jnp.float32),
+        grid=(1,),
+        out_specs=columns(2 * lanes, 0),
+    )(second, first, quad_position)
     ends = call(
         tail_kernel,
         [
-            pl.BlockSpec((members, width), lambda step: (0, early + step)),
-            pl.BlockSpec((members, lanes), lambda step: (0, early + step)),
-            pl.BlockSpec((members, lanes), lambda step: (0, (early + step + 1) % quads)),
-            columns(lanes, cells // lanes),
+            columns(half, split // half - 1),
+            columns(half, 1),
+            pl.BlockSpec((members, half), lambda step: (0, 2 * step)),
+            columns(lanes, early),
+            full(tiles),
             *[full(term) for term in terms],
         ],
         jax.ShapeDtypeStruct((members, late * width), jnp.float32),
         grant=40,
         grid=(late,),
         out_specs=pl.BlockSpec((members, width), lambda step: (0, step)),
-    )(fields, seen, seen, fields, *terms)
-    ends, sets = lax.optimization_barrier((ends, sets))
+    )(first, second, second, seen, tiles, *terms)
     ends = exchanged(ends.reshape(devices, own_members, late * width)).reshape(members, late * width)
 
     near = call(
         functools.partial(turn_kernel, own_members, INNER),
         [vmem] * (outer * early),
         [group(INNER, early * width)] * INNER,
+        cost=1 << 36,
         out_specs=[vmem] * INNER,
     )(*[array for arrays in sets for array in arrays])
     order = [[far * INNER + close for far in range(outer)] for close in range(INNER)]
-    result = placed(swapped(near, 1), order, [quad * width for quad in range(early)], None)
-    return placed([ends], None, [quad * width for quad in range(early, quads)], result)
+    result = placed([ends], None, early * width, None)
+    return placed(swapped(near, 1), order, 0, result)
 
 
 def by_all_to_all(fields, _, quad_position, root_weight, reading, devices):

time: 131 us -> 120 us (0.916)
  waiting for transfers between devices: 62.2 us -> 41.7 us
  starting transfers between devices: 30.3 us -> 34.3 us
  Pallas kernels: 32.7 us -> 35.9 us
  local copies, waits for them, and re-layouts: 4.55 us -> 6.91 us
    ppermute x9, waiting for transfers between devices: 22.9 us -> 1.02 us  [swapped(): lax.ppermute(arrays[k], 'state', pairs[k])]
    all_to_all x2 -> x3, starting transfers between devices: 12.3 us -> 23.3 us  [exchanged(): lax.all_to_all(array, 'state', split_axis=0, concat_axis=0, tiled=True)]
    ppermute x9, starting transfers between devices: 18 us -> 10.9 us  [swapped(): lax.ppermute(arrays[k], 'state', pairs[k])]
    unnamed x16 -> x30, local copies, waits for them, and re-layouts: 2.43 us -> 4.82 us
    pallas_call x3 -> x5, Pallas kernels: 17 us -> 18.4 us  [the longest x1 11.4 us: in_stages(): call(tail_kernel, [columns(half, split // half - 1), columns(half, 1), pl...]
    all_to_all x2 -> x3, waiting for transfers between devices: 39.3 us -> 40.7 us  [exchanged(): lax.all_to_all(array, 'state', split_axis=0, concat_axis=0, tiled=True)]
  transfers between devices with their start and end apart: 11 -> 12, of which waited for: 3 -> 3; matrix products, arithmetic and copies ran while one was open for 2% -> 3% of each run, Pallas kernels for 16% -> 26%
where the time goes in v3:
time: 120 us; the launch traced here: 119 us
  waiting for transfers between devices  41.7 us (35%)
  Pallas kernels  35.9 us (30%)
  starting transfers between devices  34.3 us (29%)
  local copies, waits for them, and re-layouts  6.91 us (6%)
    all_to_all x3, waiting for transfers between devices, exchanged(): lax.all_to_all(array, 'state', split_axis=0, concat_axis=0, tiled=True)  40.7 us
    all_to_all x3, starting transfers between devices, exchanged(): lax.all_to_all(array, 'state', split_axis=0, concat_axis=0, tiled=True)  23.3 us
    pallas_call x2, Pallas kernels, in_stages(): call(functools.partial(head_kernel, quad, devices), [columns(width, quad)...  12.6 us
    pallas_call x1, Pallas kernels, in_stages(): call(tail_kernel, [columns(half, split // half - 1), columns(half, 1), pl...  11.4 us
    ppermute x9, starting transfers between devices, swapped(): lax.ppermute(arrays[k], 'state', pairs[k])  10.9 us
    pallas_call x2, Pallas kernels, part(): call(functools.partial(kernel, split), [anywhere] + [vmem] * (len(argumen...  6.16 us
    unnamed x30, local copies, waits for them, and re-layouts  4.82 us
  transfers between devices with their start and end apart: 12, of which 3 were waited for; matrix products, arithmetic and copies ran while one was open for 3% of the time, Pallas kernels for 26%

profile of v3, /device:TPU:0, one launch (start us, length us, event | category | flops | bytes accessed | tf_op | source)
XLA Modules:
  0.0 119.2 jit_solution(16302248700894853511)
XLA Ops:
  0.0 3.8 %shard_map.64 = f32[16,16,1408]{2,1,0:T(8,128)} custom-call(f32[16,32768]{1,0:T(8,128)} %fields_ref.3, s32[32,256]{1,0:T(8,128)} %bitcast.15), custom_call_target="tpu_custom_call" | custom-call | flops 1 | bytes 1 | tf_op jit(solution)/shard_map/pallas_call | solution.py:412
  3.8 7.4 %all-to-all-start = ((f32[16,16,1408]{2,1,0:T(8,128)}), f32[16,16,1408]{2,1,0:T(8,128)S(1)}, u32[]{:S(2)}, u32[]{:S(2)}) async-start(f32[16,16,1408]{2,1,0:T(8,128)} %shard_map.64), calls=%async_computation | async-start | bytes 2883584 | tf_op jit(solution)/shard_map/all_to_all | solution.py:408
  11.2 0.0 copy-start.9
  11.3 0.0 copy-start.12
  11.3 0.0 copy-start.10
  11.3 0.0 copy-start.11
  11.3 2.3 %shard_map.65 = f32[16,16,768]{2,1,0:T(8,128)} custom-call(f32[16,32768]{1,0:T(8,128)} %fields_ref.3), custom_call_target="tpu_custom_call" | custom-call | flops 1 | bytes 1 | tf_op jit(solution)/shard_map/pallas_call | solution.py:412
  13.6 0.1 copy.14
  13.7 0.7 copy.15.adjacent_ref
  14.4 0.1 copy.12
  14.5 0.7 reshape.22.reading_ref
  15.2 0.1 copy.13
  15.3 0.7 reshape.23.precision_ref
  16.0 0.7 reshape.24.position_ref
  16.7 1.8 %shard_map.66 = (f32[16,256]{1,0:T(8,128)}, f32[16,256]{1,0:T(8,128)}, s32[4,128]{1,0:T(4,128)}) custom-call(f32[64,128]{1,0:T(8,128)} %reshape.22.reading_ref, f32[64,128]{1,0:T(8,128)} %reshape.23.precision_ref, s32[64,128]{1,0:T(8,128)} %reshape.24.position_ref, s32[256]{0:T(256)} %tally_ref.1, s32[16,5]{1,0:T(8,128)} %copy.15.adjacent_ref), custom_call_target="tpu_custom_call" | custom-call | tf_op jit(solution)/shard_map/pallas_call | solution.py:218
  18.5 22.4 %all-to-all-done = f32[16,16,1408]{2,1,0:T(8,128)S(1)} async-done(((f32[16,16,1408]{2,1,0:T(8,128)}), f32[16,16,1408]{2,1,0:T(8,128)S(1)}, u32[]{:S(2)}, u32[]{:S(2)}) %all-to-all-start) | async-done | bytes 1441824 | tf_op jit(solution)/shard_map/all_to_all | solution.py:408
  40.9 8.6 %all-to-all-start.1 = ((f32[16,16,768]{2,1,0:T(8,128)}), f32[16,16,768]{2,1,0:T(8,128)S(1)}, u32[]{:S(2)}, u32[]{:S(2)}) async-start(f32[16,16,768]{2,1,0:T(8,128)} %shard_map.65), calls=%async_computation.1 | async-start | bytes 1572864 | tf_op jit(solution)/shard_map/all_to_all | solution.py:408
  49.5 0.7 copy-done.3
  50.2 0.4 shard_map.67.here_ref.there_ref
  50.7 6.2 %shard_map.68 = (f32[64,512]{1,0:T(8,128)S(1)}, f32[64,512]{1,0:T(8,128)S(1)}, f32[64,512]{1,0:T(8,128)}, f32[64,512]{1,0:T(8,128)S(1)}) custom-call(f32[256,1408]{1,0:T(8,128)S(1)} %bitcast.6, f32[256,384]{1,0:T(8,128)S(1)} %shard_map.67.here_ref.there_ref, f32[256,384]{1,0:T(8,128)S(1)} %shard_map.67.here_ref.there_ref, f32[16,256]{1,0:T(8,128)S(1)} %copy-done.1, ...), custom_call_target="tpu_custom_call" | custom-call | flops 1 | bytes 1 | tf_op jit(solution)/shard_map/pallas_call | solution.py:441
  56.9 1.9 %collective-permute-start = (f32[64,512]{1,0:T(8,128)S(1)}, f32[64,512]{1,0:T(8,128)S(1)}, u32[]{:S(2)}, u32[]{:S(2)}) collective-permute-start(f32[64,512]{1,0:T(8,128)S(1)} %get-tuple-element.43), channel_id=1, source_target_pairs={{0,4},{1,5},{2,6},{3,7},{4,0},{5,1},{6,2},{7,3},{8,12},{9,13},{10,... | collective-permute-start | bytes 393224 | tf_op jit(solution)/shard_map/ppermute | solution.py:394
  58.8 2.4 %collective-permute-start.1 = (f32[64,512]{1,0:T(8,128)}, f32[64,512]{1,0:T(8,128)S(1)}, u32[]{:S(2)}, u32[]{:S(2)}) collective-permute-start(f32[64,512]{1,0:T(8,128)} %get-tuple-element.44), channel_id=1, source_target_pairs={{0,8},{1,9},{2,10},{3,11},{4,12},{5,13},{6,14},{7,15},{8,0},{9,1},... | collective-permute-start | bytes 393224 | tf_op jit(solution)/shard_map/ppermute | solution.py:394
  61.2 0.1 collective-permute-start.2
  61.3 6.3 %shard_map.69 = (f32[64,512]{1,0:T(8,128)S(1)}, f32[64,512]{1,0:T(8,128)}, f32[64,512]{1,0:T(8,128)}, f32[64,512]{1,0:T(8,128)}) custom-call(f32[256,1408]{1,0:T(8,128)S(1)} %bitcast.7, f32[256,384]{1,0:T(8,128)S(1)} %shard_map.67.here_ref.there_ref, f32[256,384]{1,0:T(8,128)S(1)} %shard_map.67.here_ref.there_ref, f32[16,256]{1,0:T(8,128)S(1)} %copy-done.1, ...), custom_call_target="tpu_custom_call" | custom-call | flops 1 | bytes 1 | tf_op jit(solution)/shard_map/pallas_call | solution.py:441
  67.6 0.6 copy-done.5
  68.2 1.0 collective-permute-start.3
  69.3 3.3 %collective-permute-start.4 = (f32[64,512]{1,0:T(8,128)}, f32[64,512]{1,0:T(8,128)}, u32[]{:S(2)}, u32[]{:S(2)}) collective-permute-start(f32[64,512]{1,0:T(8,128)} %get-tuple-element.49), channel_id=1, source_target_pairs={{0,8},{1,9},{2,10},{3,11},{4,12},{5,13},{6,14},{7,15},{8,0},{9,1},... | collective-permute-start | bytes 393224 | tf_op jit(solution)/shard_map/ppermute | solution.py:394
  72.5 0.0 collective-permute-done.refs_1_
  72.5 0.1 collective-permute-start.5
  72.6 0.5 shard_map.71.tiles_ref
  73.1 11.4 %shard_map.72 = f32[256,1024]{1,0:T(8,128)S(1)} custom-call(f32[256,1408]{1,0:T(8,128)S(1)} %bitcast.9, f32[256,768]{1,0:T(8,128)S(1)} %bitcast.11, f32[256,768]{1,0:T(8,128)S(1)} %bitcast.12, f32[256,384]{1,0:T(8,128)S(1)} %shard_map.67.here_ref.there_ref, f32[256,256]{1,0:T(8,128)S(1)} %shard_map.71.tiles_ref, f32[16,256]{1,0:T(8,128)S(1)} %copy-done.1, ...), custom_call_target="tpu_custom_call" | custom-call | flops 1 | bytes 1 | tf_op jit(solution)/shard_map/pallas_call | solution.py:462
  84.5 0.0 copy-start
  84.5 1.0 copy-done
  85.4 7.3 %all-to-all-start.2 = ((f32[16,16,1024]{2,1,0:T(8,128)}), f32[16,16,1024]{2,1,0:T(8,128)S(1)}, u32[]{:S(2)}, u32[]{:S(2)}) async-start(f32[16,16,1024]{2,1,0:T(8,128)} %bitcast.14), calls=%async_computation.2 | async-start | bytes 2097152 | tf_op jit(solution)/shard_map/all_to_all | solution.py:408
  92.8 0.0 collective-permute-done.2.refs_3_
  92.8 0.0 collective-permute-done.3.refs_5_
  92.8 0.6 copy-done.7
  93.5 0.0 collective-permute-done.4.refs_6_
  93.5 0.0 collective-permute-done.5.refs_7_
  93.5 0.9 copy-done.8
  94.4 1.0 shard_map.70
  95.4 0.5 collective-permute-start.6
  95.9 1.7 %collective-permute-start.7 = (f32[64,1024]{1,0:T(8,128)S(1)}, f32[64,1024]{1,0:T(8,128)S(1)}, u32[]{:S(2)}, u32[]{:S(2)}) collective-permute-start(f32[64,1024]{1,0:T(8,128)S(1)} %get-tuple-element.53), channel_id=1, source_target_pairs={{0,2},{1,3},{2,0},{3,1},{4,6},{5,7},{6,4},{7,5},{8,10},{9,11},{10,... | collective-permute-start | bytes 786440 | tf_op jit(solution)/shard_map/ppermute | solution.py:394
  97.6 18.2 %all-to-all-done.2 = f32[16,16,1024]{2,1,0:T(8,128)S(1)} async-done(((f32[16,16,1024]{2,1,0:T(8,128)}), f32[16,16,1024]{2,1,0:T(8,128)S(1)}, u32[]{:S(2)}, u32[]{:S(2)}) %all-to-all-start.2) | async-done | bytes 1048608 | tf_op jit(solution)/shard_map/all_to_all | solution.py:408
  115.8 1.1 shard_map.73.refs_4_
  116.9 0.0 collective-permute-done.6.refs_1_
  116.9 1.0 collective-permute-done.8.refs_3_
  117.9 1.1 shard_map.74
  (20 shorter events, 0.0 us)
Async XLA Ops:
  3.8 37.1 %all-to-all-start = ((f32[16,16,1408]{2,1,0:T(8,128)}), f32[16,16,1408]{2,1,0:T(8,128)S(1)}, u32[]{:S(2)}, u32[]{:S(2)}) async-start(f32[16,16,1408]{2,1,0:T(8,128)} %shard_map.64), calls=%async_computation | async-start | bytes 2883584 | tf_op jit(solution)/shard_map/all_to_all | solution.py:408
  11.2 2.4 %copy-start.9 = (s32[256,32]{0,1:T(8,128)S(1)}, s32[256,32]{0,1:T(8,128)}, u32[]{:S(2)}) copy-start(s32[256,32]{0,1:T(8,128)} %param.9) | copy-start | bytes 98308
  11.3 2.5 %copy-start.12 = (s32[16,5]{0,1:T(8,128)S(1)}, s32[16,5]{0,1:T(8,128)}, u32[]{:S(2)}) copy-start(s32[16,5]{0,1:T(8,128)} %param.11) | copy-start | bytes 964
  11.3 3.1 %copy-start.10 = (f32[256,32]{0,1:T(8,128)S(1)}, f32[256,32]{0,1:T(8,128)}, u32[]{:S(2)}) copy-start(f32[256,32]{0,1:T(8,128)} %param.7) | copy-start | bytes 98308
  11.3 3.9 %copy-start.11 = (f32[256,32]{0,1:T(8,128)S(1)}, f32[256,32]{0,1:T(8,128)}, u32[]{:S(2)}) copy-start(f32[256,32]{0,1:T(8,128)} %param.8) | copy-start | bytes 98308
  18.5 32.1 %copy-start.1 = (f32[16,256]{1,0:T(8,128)S(1)}, f32[16,256]{1,0:T(8,128)}, u32[]{:S(2)}) copy-start(f32[16,256]{1,0:T(8,128)} %get-tuple-element.36.weight_ref) | copy-start | bytes 49156
  18.5 32.1 %copy-start.2 = (f32[16,256]{1,0:T(8,128)S(1)}, f32[16,256]{1,0:T(8,128)}, u32[]{:S(2)}) copy-start(f32[16,256]{1,0:T(8,128)} %get-tuple-element.37.reading_ref) | copy-start | bytes 49156
  40.9 31.7 %all-to-all-start.1 = ((f32[16,16,768]{2,1,0:T(8,128)}), f32[16,16,768]{2,1,0:T(8,128)S(1)}, u32[]{:S(2)}, u32[]{:S(2)}) async-start(f32[16,16,768]{2,1,0:T(8,128)} %shard_map.65), calls=%async_computation.1 | async-start | bytes 1572864 | tf_op jit(solution)/shard_map/all_to_all | solution.py:408
  49.5 0.7 copy-start.3
  50.6 22.0 %copy-start.4 = (s32[4,128]{1,0:T(4,128)S(1)}, s32[4,128]{1,0:T(4,128)}, u32[]{:S(2)}) copy-start(s32[4,128]{1,0:T(4,128)} %get-tuple-element.35.position_ref) | copy-start | bytes 6148
  56.9 15.6 %collective-permute-start = (f32[64,512]{1,0:T(8,128)S(1)}, f32[64,512]{1,0:T(8,128)S(1)}, u32[]{:S(2)}, u32[]{:S(2)}) collective-permute-start(f32[64,512]{1,0:T(8,128)S(1)} %get-tuple-element.43), channel_id=1, source_target_pairs={{0,4},{1,5},{2,6},{3,7},{4,0},{5,1},{6,2},{7,3},{8,12},{9,13},{10,... | collective-permute-start | bytes 393224 | tf_op jit(solution)/shard_map/ppermute | solution.py:394
  58.8 34.0 %collective-permute-start.1 = (f32[64,512]{1,0:T(8,128)}, f32[64,512]{1,0:T(8,128)S(1)}, u32[]{:S(2)}, u32[]{:S(2)}) collective-permute-start(f32[64,512]{1,0:T(8,128)} %get-tuple-element.44), channel_id=1, source_target_pairs={{0,8},{1,9},{2,10},{3,11},{4,12},{5,13},{6,14},{7,15},{8,0},{9,1},... | collective-permute-start | bytes 393224 | tf_op jit(solution)/shard_map/ppermute | solution.py:394
  61.2 31.6 %collective-permute-start.2 = (f32[64,512]{1,0:T(8,128)S(1)}, f32[64,512]{1,0:T(8,128)S(1)}, u32[]{:S(2)}, u32[]{:S(2)}) collective-permute-start(f32[64,512]{1,0:T(8,128)S(1)} %get-tuple-element.45), channel_id=1, source_target_pairs={{0,12},{1,13},{2,14},{3,15},{4,8},{5,9},{6,10},{7,11},{8,4},{9,5},... | collective-permute-start | bytes 393224 | tf_op jit(solution)/shard_map/ppermute | solution.py:394
  67.6 0.6 copy-start.5
  68.2 24.6 %collective-permute-start.3 = (f32[64,512]{1,0:T(8,128)}, f32[64,512]{1,0:T(8,128)S(1)}, u32[]{:S(2)}, u32[]{:S(2)}) collective-permute-start(f32[64,512]{1,0:T(8,128)} %get-tuple-element.48), channel_id=1, source_target_pairs={{0,4},{1,5},{2,6},{3,7},{4,0},{5,1},{6,2},{7,3},{8,12},{9,13},{10,... | collective-permute-start | bytes 393224 | tf_op jit(solution)/shard_map/ppermute | solution.py:394
  69.3 24.2 %collective-permute-start.4 = (f32[64,512]{1,0:T(8,128)}, f32[64,512]{1,0:T(8,128)}, u32[]{:S(2)}, u32[]{:S(2)}) collective-permute-start(f32[64,512]{1,0:T(8,128)} %get-tuple-element.49), channel_id=1, source_target_pairs={{0,8},{1,9},{2,10},{3,11},{4,12},{5,13},{6,14},{7,15},{8,0},{9,1},... | collective-permute-start | bytes 393224 | tf_op jit(solution)/shard_map/ppermute | solution.py:394
  72.5 21.0 %collective-permute-start.5 = (f32[64,512]{1,0:T(8,128)}, f32[64,512]{1,0:T(8,128)}, u32[]{:S(2)}, u32[]{:S(2)}) collective-permute-start(f32[64,512]{1,0:T(8,128)} %get-tuple-element.50), channel_id=1, source_target_pairs={{0,12},{1,13},{2,14},{3,15},{4,8},{5,9},{6,10},{7,11},{8,4},{9,5},... | collective-permute-start | bytes 393224 | tf_op jit(solution)/shard_map/ppermute | solution.py:394
  84.5 1.0 copy-start
  85.4 8.0 %copy-start.6 = (f32[64,512]{1,0:T(8,128)S(1)}, f32[64,512]{1,0:T(8,128)}, u32[]{:S(2)}) copy-start(f32[64,512]{1,0:T(8,128)} %copy-done.5) | copy-start | bytes 393220
  85.4 30.4 %all-to-all-start.2 = ((f32[16,16,1024]{2,1,0:T(8,128)}), f32[16,16,1024]{2,1,0:T(8,128)S(1)}, u32[]{:S(2)}, u32[]{:S(2)}) async-start(f32[16,16,1024]{2,1,0:T(8,128)} %bitcast.14), calls=%async_computation.2 | async-start | bytes 2097152 | tf_op jit(solution)/shard_map/all_to_all | solution.py:408
  92.8 0.7 copy-start.7
  93.5 0.9 copy-start.8
  95.4 21.5 %collective-permute-start.6 = (f32[64,1024]{1,0:T(8,128)S(1)}, f32[64,1024]{1,0:T(8,128)S(1)}, u32[]{:S(2)}, u32[]{:S(2)}) collective-permute-start(f32[64,1024]{1,0:T(8,128)S(1)} %get-tuple-element.52), channel_id=1, source_target_pairs={{0,1},{1,0},{2,3},{3,2},{4,5},{5,4},{6,7},{7,6},{8,9},{9,8},{10,11... | collective-permute-start | bytes 786440 | tf_op jit(solution)/shard_map/ppermute | solution.py:394
  95.9 21.0 %collective-permute-start.7 = (f32[64,1024]{1,0:T(8,128)S(1)}, f32[64,1024]{1,0:T(8,128)S(1)}, u32[]{:S(2)}, u32[]{:S(2)}) collective-permute-start(f32[64,1024]{1,0:T(8,128)S(1)} %get-tuple-element.53), channel_id=1, source_target_pairs={{0,2},{1,3},{2,0},{3,1},{4,6},{5,7},{6,4},{7,5},{8,10},{9,11},{10,... | collective-permute-start | bytes 786440 | tf_op jit(solution)/shard_map/ppermute | solution.py:394
  97.6 20.3 %collective-permute-start.8 = (f32[64,1024]{1,0:T(8,128)S(1)}, f32[64,1024]{1,0:T(8,128)S(1)}, u32[]{:S(2)}, u32[]{:S(2)}) collective-permute-start(f32[64,1024]{1,0:T(8,128)S(1)} %get-tuple-element.54), channel_id=1, source_target_pairs={{0,3},{1,2},{2,1},{3,0},{4,7},{5,6},{6,5},{7,4},{8,11},{9,10},{10,... | collective-permute-start | bytes 786440 | tf_op jit(solution)/shard_map/ppermute | solution.py:394

commit v4 on v3

--- a/solution.py
+++ b/solution.py
@@ -120,9 +120,16 @@
         seen_ref[:, quad * span : (quad + 1) * span] = found if quad else jnp.where(low, beyond, found)
 
 
-def pick_second_kernel(fields_ref, beyond_ref, position_ref, seen_ref):
+def second_kernel(devices, beyond_ref, position_ref, *refs):
+    *parts, fields_ref, seen_ref = refs
+    place = lax.axis_index("state")
     span = PARTITION_SPAN
     quads = position_ref.shape[0]
+    rows = fields_ref.shape[0] // devices
+    for distance in range(devices):
+        far, near = divmod(distance, INNER)
+        start = pl.multiple_of((place ^ distance) * rows, rows)
+        fields_ref[pl.ds(start, rows), :] = parts[far][near * rows : (near + 1) * rows, :]
     amount = fields_ref.shape[1] // span
     low = lax.broadcasted_iota(jnp.int32, beyond_ref.shape, 1) < R * OB
     for index in range(seen_ref.shape[1] // span):
@@ -274,44 +281,50 @@
         copy.wait()
 
 
-def second_part_kernel(split, fields_ref, sent_ref, held_ref, sems):
-    devices, _, size = sent_ref.shape
-    for copy in into_held(fields_ref, held_ref, sems, split, size):
+def second_part_kernel(split, fields_ref, *refs):
+    *sent, sems = refs
+    place = lax.axis_index("state")
+    rows = fields_ref.shape[0]
+    size = sent[0].shape[1]
+    cells = split + size
+    copies = []
+    for near, array in enumerate(sent):
+        for far in range(array.shape[0] // rows):
+            start = (place ^ (far * INNER + near)) * cells + split
+            source = fields_ref.at[:, pl.ds(pl.multiple_of(start, PARTITION_SPAN), size)]
+            target = array.at[pl.ds(far * rows, rows), :]
+            copies.append(pltpu.make_async_copy(source, target, sems.at[len(copies)]))
+    for copy in copied(copies):
         copy.wait()
-    for copy in copied([pltpu.make_async_copy(held_ref, sent_ref, sems.at[devices])]):
-        copy.wait()
-
-
-def turn_kernel(rows, parts, *refs):
-    given, made = refs[:-parts], refs[-parts:]
-    width = given[0].shape[1]
-    many = made[0].shape[0] // rows
-    for number, source in enumerate(given):
-        side, i = divmod(number, many)
+
+
+def turn_kernel(rows, *refs):
+    given, made = refs[: len(refs) // 2], refs[len(refs) // 2 :]
+    for i, source in enumerate(given):
         for j, target in enumerate(made):
-            target[i * rows : (i + 1) * rows, side * width : (side + 1) * width] = source[j * rows : (j + 1) * rows, :]
-
-
-def place_kernel(distances, cells, start, *refs):
-    *parts, result_ref, sems = refs
+            target[i * rows : (i + 1) * rows, :] = source[j * rows : (j + 1) * rows, :]
+
+
+def place_kernel(cells, *refs):
+    *parts, last_ref, result_ref, sems = refs
     place = lax.axis_index("state")
     rows = result_ref.shape[0]
-    width = parts[0].shape[1]
-    started = []
-    for i, part in enumerate(parts):
-        for j in range(part.shape[0] // rows):
-            device = place ^ distances[i][j] if distances else j
-            source = part.at[pl.ds(j * rows, rows), :]
-            target = result_ref.at[:, pl.ds(pl.multiple_of(device * cells + start, width), width)]
-            started.append(pltpu.make_async_copy(source, target, sems.at[len(started)]))
-            started[-1].start()
+    moves = []
+    for near, part in enumerate(parts):
+        width = part.shape[1]
+        for far in range(part.shape[0] // rows):
+            start = (place ^ (far * INNER + near)) * cells
+            target = result_ref.at[:, pl.ds(pl.multiple_of(start, width), width)]
+            moves.append((part.at[pl.ds(far * rows, rows), :], target))
+    for device in range(last_ref.shape[0] // rows):
+        size = last_ref.shape[1]
+        target = result_ref.at[:, pl.ds((device + 1) * cells - size, size)]
+        moves.append((last_ref.at[pl.ds(device * rows, rows), :], target))
+    started = [pltpu.make_async_copy(*move, sems.at[index]) for index, move in enumerate(moves)]
+    for copy in started:
+        copy.start()
     for copy in started:
         copy.wait()
-
-
-def place_more_kernel(distances, cells, start, *refs):
-    *parts, _, result_ref, sems = refs
-    place_kernel(distances, cells, start, *parts, result_ref, sems)
 
 
 def reordered(ref, devices):
@@ -331,10 +344,11 @@
     return blocks
 
 
-def head_kernel(quad, devices, fields_ref, here_ref, there_ref, weight_ref, reading_ref, *results):
-    span = PARTITION_SPAN
+def head_kernel(devices, fields_ref, here_ref, there_ref, weight_ref, reading_ref, *results):
+    span = PARTITION_SPAN
+    first = pl.program_id(0) * QUAD
     fields, here, there = [reordered(ref, devices) for ref in (fields_ref, here_ref, there_ref)]
-    for spot, result in enumerate(updated(blocks_of(fields, here, there, quad * QUAD, weight_ref, reading_ref))):
+    for spot, result in enumerate(updated(blocks_of(fields, here, there, first, weight_ref, reading_ref))):
         start = 0
         for result_ref in results:
             rows = result_ref.shape[0]
@@ -354,7 +368,7 @@
         result_ref[:, spot * span : (spot + 1) * span] = result
 
 
-def in_stages(fields, positions, quad_position, root_weight, reading, devices):
+def in_stages(fields, observations, devices):
     own_members, all_cells = fields.shape
     cells = all_cells // devices
     amount = cells // PARTITION_SPAN
@@ -368,7 +382,6 @@
     half = R * PARTITION_SPAN
     anywhere = pl.BlockSpec(memory_space=pl.ANY)
     vmem = pl.BlockSpec(memory_space=pltpu.VMEM)
-    whole = jax.ShapeDtypeStruct((own_members, all_cells), jnp.float32)
 
     def call(kernel, inputs, outputs, grant=16, cost=1, **options):
         return pl.pallas_call(
@@ -393,41 +406,47 @@
         pairs = [[(i, i ^ (unit * k)) for i in range(devices)] for k in range(len(arrays))]
         return [arrays[0]] + [lax.ppermute(arrays[k], "state", pairs[k]) for k in range(1, len(arrays))]
 
-    def placed(parts, order, start, result):
-        options = dict(out_specs=anywhere, scratch_shapes=[pltpu.SemaphoreType.DMA((devices,))])
-        if result is None:
-            kernel = functools.partial(place_kernel, order, cells, start)
-            return call(kernel, [vmem] * len(parts), whole, **options)(*parts)
-        kernel = functools.partial(place_more_kernel, order, cells, start)
-        aliases = {len(parts): 0}
-        return call(kernel, [vmem] * len(parts) + [anywhere], whole, input_output_aliases=aliases, **options)(
-            *parts, result
-        )
+    def second_parts():
+        return call(
+            functools.partial(second_part_kernel, split),
+            [anywhere],
+            [group(INNER, cells - split)] * INNER,
+            out_specs=[vmem] * INNER,
+            scratch_shapes=[pltpu.SemaphoreType.DMA((devices,))],
+        )(fields)
+
+    def turned(arrays, parts, cost=1):
+        return call(
+            functools.partial(turn_kernel, own_members),
+            [vmem] * len(arrays),
+            [group(parts, arrays[0].shape[1])] * parts,
+            cost=cost,
+            out_specs=[vmem] * parts,
+        )(*arrays)
 
     def exchanged(array):
         return lax.all_to_all(array, "state", split_axis=0, concat_axis=0, tiled=True)
 
     split = early * width + half
-    def part(kernel, arguments, size, held):
-        return call(
-            functools.partial(kernel, split),
-            [anywhere] + [vmem] * (len(arguments) - 1),
-            jax.ShapeDtypeStruct((devices, own_members, size), jnp.float32),
-            grant=56,
-            out_specs=anywhere,
-            scratch_shapes=[
-                pltpu.VMEM((devices, own_members, held), jnp.float32),
-                pltpu.SemaphoreType.DMA((2 * devices,)),
-            ],
-        )(*arguments)
-
-    first = part(first_part_kernel, [fields, positions.T], split + lanes, cells + lanes)
-    second = part(second_part_kernel, [fields], cells - split, cells - split)
-    first = exchanged(first).reshape(members, split + lanes)
-    first, second, quad_position, root_weight, reading = lax.optimization_barrier(
-        (first, second, quad_position, root_weight, reading)
+    sent = call(
+        functools.partial(first_part_kernel, split),
+        [anywhere, vmem],
+        jax.ShapeDtypeStruct((devices, own_members, split + lanes), jnp.float32),
+        grant=56,
+        out_specs=anywhere,
+        scratch_shapes=[
+            pltpu.VMEM((devices, own_members, cells + lanes), jnp.float32),
+            pltpu.SemaphoreType.DMA((2 * devices,)),
+        ],
+    )(fields, observations[2].T)
+    first = exchanged(sent).reshape(members, split + lanes)
+    second = turned(swapped(second_parts(), 1), outer)
+    second, observations = lax.optimization_barrier((second, observations))
+    root_weight, reading, quad_position = window_terms(*observations, members)
+    second, root_weight, reading, quad_position = lax.optimization_barrier(
+        (second, root_weight, reading, quad_position)
     )
-    second = exchanged(second).reshape(members, cells - split)
+    second = swapped(second, INNER)
     terms = [root_weight, reading]
     seen = call(
         pick_first_kernel,
@@ -436,29 +455,32 @@
         out_specs=vmem,
     )(first, quad_position)
 
-    sets = []
-    for quad in range(early):
-        groups = call(
-            functools.partial(head_kernel, quad, devices),
-            [columns(width, quad), columns(lanes, quad), columns(lanes, quad + 1), *[full(term) for term in terms]],
-            [group(outer, width)] * outer,
-            grant=40,
-            grid=(1,),
-            out_specs=[pl.BlockSpec((members // outer, width), lambda step: (0, 0))] * outer,
-        )(first, seen, seen, *terms)
-        if quad + 1 < early:
-            seen, groups = lax.optimization_barrier((seen, groups))
-        else:
-            _, second = lax.optimization_barrier((groups, second))
-        sets.append(swapped(groups, INNER))
-
-    tiles = call(
-        pick_second_kernel,
-        [full(second), columns(lanes, split // lanes), full(quad_position)],
-        jax.ShapeDtypeStruct((members, 2 * lanes), jnp.float32),
+    groups = call(
+        functools.partial(head_kernel, devices),
+        [
+            pl.BlockSpec((members, width), lambda step: (0, step)),
+            pl.BlockSpec((members, lanes), lambda step: (0, step)),
+            pl.BlockSpec((members, lanes), lambda step: (0, step + 1)),
+            *[full(term) for term in terms],
+        ],
+        [group(outer, early * width)] * outer,
+        grant=40,
+        grid=(early,),
+        out_specs=[pl.BlockSpec((members // outer, width), lambda step: (0, step))] * outer,
+    )(first, seen, seen, *terms)
+    groups, second = lax.optimization_barrier((groups, second))
+    beyond = swapped(groups, INNER)
+
+    second, tiles = call(
+        functools.partial(second_kernel, devices),
+        [columns(lanes, split // lanes), *[full(array) for array in (quad_position, *second)]],
+        [
+            jax.ShapeDtypeStruct((members, cells - split), jnp.float32),
+            jax.ShapeDtypeStruct((members, 2 * lanes), jnp.float32),
+        ],
         grid=(1,),
-        out_specs=columns(2 * lanes, 0),
-    )(second, first, quad_position)
+        out_specs=[columns(cells - split, 0), columns(2 * lanes, 0)],
+    )(first, quad_position, *second)
     ends = call(
         tail_kernel,
         [
@@ -470,30 +492,29 @@
             *[full(term) for term in terms],
         ],
         jax.ShapeDtypeStruct((members, late * width), jnp.float32),
-        grant=40,
+        grant=60,
         grid=(late,),
         out_specs=pl.BlockSpec((members, width), lambda step: (0, step)),
     )(first, second, second, seen, tiles, *terms)
     ends = exchanged(ends.reshape(devices, own_members, late * width)).reshape(members, late * width)
 
-    near = call(
-        functools.partial(turn_kernel, own_members, INNER),
-        [vmem] * (outer * early),
-        [group(INNER, early * width)] * INNER,
-        cost=1 << 36,
-        out_specs=[vmem] * INNER,
-    )(*[array for arrays in sets for array in arrays])
-    order = [[far * INNER + close for far in range(outer)] for close in range(INNER)]
-    result = placed([ends], None, early * width, None)
-    return placed(swapped(near, 1), order, 0, result)
-
-
-def by_all_to_all(fields, _, quad_position, root_weight, reading, devices):
+    near = turned(beyond, INNER, cost=1 << 36)
+    return call(
+        functools.partial(place_kernel, cells),
+        [vmem] * (INNER + 1),
+        jax.ShapeDtypeStruct((own_members, all_cells), jnp.float32),
+        out_specs=anywhere,
+        scratch_shapes=[pltpu.SemaphoreType.DMA((2 * devices,))],
+    )(*swapped(near, 1), ends)
+
+
+def by_all_to_all(fields, observations, devices):
     own_members, all_cells = fields.shape
     cells = all_cells // devices
     amount = cells // PARTITION_SPAN
     members = own_members * devices
     span = PARTITION_SPAN
+    root_weight, reading, quad_position = window_terms(*observations, members)
     sent = fields.reshape(own_members, devices, cells).transpose(1, 0, 2)
     fields = lax.all_to_all(sent, "state", split_axis=0, concat_axis=0, tiled=True).reshape(members, cells)
     vmem = pl.BlockSpec(memory_space=pltpu.VMEM)
@@ -542,16 +563,15 @@
     adjacent_tile_number,
 ):
     devices = lax.axis_size("state")
-    root_weight, reading, quad_position = window_terms(
+    observations = (
         measurement_reading,
         measurement_precision,
         sensed_point_position,
         measurement_tally,
         adjacent_tile_number,
-        background_draws_table.shape[0] * devices,
     )
     way = in_stages if devices == INNER * INNER else by_all_to_all
-    return way(background_draws_table, sensed_point_position, quad_position, root_weight, reading, devices)
+    return way(background_draws_table, observations, devices)
 
 
 def solution(mesh):

time: 120 us -> 115 us (0.958)
  starting transfers between devices: 34.3 us -> 27.5 us
  local copies, waits for them, and re-layouts: 6.91 us -> 9.01 us
    ppermute x9 -> x12, waiting for transfers between devices: 1.02 us -> 42.4 us  [swapped(): lax.ppermute(arrays[k], 'state', pairs[k])]
    all_to_all x3 -> x2, waiting for transfers between devices: 40.7 us -> 0.01 us  [exchanged(): lax.all_to_all(array, 'state', split_axis=0, concat_axis=0, tiled=True)]
    all_to_all x3 -> x2, starting transfers between devices: 23.3 us -> 11.3 us  [exchanged(): lax.all_to_all(array, 'state', split_axis=0, concat_axis=0, tiled=True)]
    ppermute x9 -> x12, starting transfers between devices: 10.9 us -> 16.3 us  [swapped(): lax.ppermute(arrays[k], 'state', pairs[k])]
    optimization_barrier x0 -> x4, local copies, waits for them, and re-layouts: none -> 3.25 us  [in_stages(): second, observations = lax.optimization_barrier((second, observations))]
    pallas_call x8 -> x7, Pallas kernels: 22.4 us -> 19.9 us  [the longest x1 11.5 us: in_stages(): call(functools.partial(head_kernel, devices), [pl.BlockSpec((members, wid...]
    pallas_call x1, Pallas kernels: 11.4 us -> 13.2 us  [in_stages(): call(tail_kernel, [columns(half, split // half - 1), columns(half, 1), pl...]
    unnamed x30 -> x20, local copies, waits for them, and re-layouts: 4.82 us -> 3.66 us
  transfers between devices with their start and end apart: 12 -> 14, of which waited for: 3 -> 6; matrix products, arithmetic and copies ran while one was open for 3% -> 5% of each run, Pallas kernels for 26% -> 26%
where the time goes in v4:
time: 115 us
  waiting for transfers between devices  42.4 us (37%)
  Pallas kernels  35.3 us (31%)
  starting transfers between devices  27.5 us (24%)
  local copies, waits for them, and re-layouts  9.01 us (8%)
    ppermute x12, waiting for transfers between devices, swapped(): lax.ppermute(arrays[k], 'state', pairs[k])  42.4 us
    ppermute x12, starting transfers between devices, swapped(): lax.ppermute(arrays[k], 'state', pairs[k])  16.3 us
    pallas_call x1, Pallas kernels, in_stages(): call(tail_kernel, [columns(half, split // half - 1), columns(half, 1), pl...  13.2 us
    pallas_call x1, Pallas kernels, in_stages(): call(functools.partial(head_kernel, devices), [pl.BlockSpec((members, wid...  11.5 us
    all_to_all x2, starting transfers between devices, exchanged(): lax.all_to_all(array, 'state', split_axis=0, concat_axis=0, tiled=True)  11.3 us
    pallas_call x1, Pallas kernels, in_stages(): call(functools.partial(first_part_kernel, split), [anywhere, vmem], jax.S...  3.83 us
    unnamed x20, local copies, waits for them, and re-layouts  3.66 us
    optimization_barrier x4, local copies, waits for them, and re-layouts, in_stages(): second, observations = lax.optimization_barrier((second, observations))  3.25 us
  transfers between devices with their start and end apart: 14, of which 6 were waited for; matrix products, arithmetic and copies ran while one was open for 5% of the time, Pallas kernels for 26%

profile of v4, /device:TPU:0, one launch (start us, length us, event | category | flops | bytes accessed | tf_op | source)
XLA Modules:
  0.0 114.5 jit_solution(7970175113726005103)
XLA Ops:
  0.0 3.8 %shard_map.64 = f32[16,16,1408]{2,1,0:T(8,128)} custom-call(f32[16,32768]{1,0:T(8,128)} %fields_ref.3, s32[32,256]{1,0:T(8,128)} %bitcast.10), custom_call_target="tpu_custom_call" | custom-call | flops 1 | bytes 1 | tf_op jit(solution)/shard_map/pallas_call | solution.py:431
  3.8 0.0 copy-start.1
  3.9 7.5 %all-to-all-start = ((f32[16,16,1408]{2,1,0:T(8,128)}), f32[16,16,1408]{2,1,0:T(8,128)S(1)}, u32[]{:S(2)}, u32[]{:S(2)}) async-start(f32[16,16,1408]{2,1,0:T(8,128)} %shard_map.64), calls=%async_computation | async-start | bytes 2883584 | tf_op jit(solution)/shard_map/all_to_all | solution.py:428
  11.4 0.0 copy-start.9
  11.4 0.8 shard_map.65
  12.2 0.5 collective-permute-start
  12.6 1.7 %collective-permute-start.1 = (f32[64,768]{1,0:T(8,128)S(1)}, f32[64,768]{1,0:T(8,128)S(1)}, u32[]{:S(2)}, u32[]{:S(2)}) collective-permute-start(f32[64,768]{1,0:T(8,128)S(1)} %get-tuple-element.52), channel_id=1, source_target_pairs={{0,2},{1,3},{2,0},{3,1},{4,6},{5,7},{6,4},{7,5},{8,10},{9,11},{10,... | collective-permute-start | bytes 589832 | tf_op jit(solution)/shard_map/ppermute | solution.py:407
  14.3 16.3 %collective-permute-done.1.refs_2_ = f32[64,768]{1,0:T(8,128)S(1)} collective-permute-done((f32[64,768]{1,0:T(8,128)S(1)}, f32[64,768]{1,0:T(8,128)S(1)}, u32[]{:S(2)}, u32[]{:S(2)}) %collective-permute-start.1) | collective-permute-done | bytes 196640 | tf_op jit(solution)/shard_map/ppermute | solution.py:407
  30.6 3.7 %collective-permute-done.2.refs_3_ = f32[64,768]{1,0:T(8,128)S(1)} collective-permute-done((f32[64,768]{1,0:T(8,128)S(1)}, f32[64,768]{1,0:T(8,128)S(1)}, u32[]{:S(2)}, u32[]{:S(2)}) %collective-permute-start.2) | collective-permute-done | bytes 196640 | tf_op jit(solution)/shard_map/ppermute | solution.py:407
  34.3 0.8 shard_map.66
  35.2 0.7 copy.14.adjacent_ref
  35.8 0.9 copy.11
  36.7 0.7 reshape.19.reading_ref
  37.4 0.9 copy.12
  38.2 0.7 reshape.20.precision_ref
  38.9 0.9 copy.13
  39.8 0.7 reshape.21.position_ref
  40.5 1.8 %shard_map.67 = (f32[16,256]{1,0:T(8,128)}, f32[16,256]{1,0:T(8,128)}, s32[4,128]{1,0:T(4,128)}) custom-call(f32[64,128]{1,0:T(8,128)} %reshape.19.reading_ref, f32[64,128]{1,0:T(8,128)} %reshape.20.precision_ref, s32[64,128]{1,0:T(8,128)} %reshape.21.position_ref, s32[256]{0:T(256)} %tally_ref, s32[16,5]{1,0:T(8,128)} %copy.14.adjacent_ref), custom_call_target="tpu_custom_call" | custom-call | tf_op jit(solution)/shard_map/pallas_call | solution.py:225
  42.3 0.3 collective-permute-start.3
  42.6 5.2 %collective-permute-start.4 = (f32[64,768]{1,0:T(8,128)}, f32[64,768]{1,0:T(8,128)S(1)}, u32[]{:S(2)}, u32[]{:S(2)}) collective-permute-start(f32[64,768]{1,0:T(8,128)} %get-tuple-element.79), channel_id=1, source_target_pairs={{0,8},{1,9},{2,10},{3,11},{4,12},{5,13},{6,14},{7,15},{8,0},{9,1},... | collective-permute-start | bytes 589832 | tf_op jit(solution)/shard_map/ppermute | solution.py:407
  47.8 0.0 collective-permute-start.5
  47.8 0.6 copy-done.7
  48.4 0.4 shard_map.68.here_ref.there_ref
  48.8 0.7 copy-done.5
  49.5 0.7 copy-done.6
  50.3 11.5 %shard_map.69 = (f32[64,1024]{1,0:T(8,128)S(1)}, f32[64,1024]{1,0:T(8,128)S(1)}, f32[64,1024]{1,0:T(8,128)S(1)}, f32[64,1024]{1,0:T(8,128)S(1)}) custom-call(f32[256,1408]{1,0:T(8,128)S(1)} %bitcast.5, f32[256,384]{1,0:T(8,128)S(1)} %shard_map.68.here_ref.there_ref, f32[256,384]{1,0:T(8,128)S(1)} %shard_map.68.here_ref.there_ref, f32[16,256]{1,0:T(8,128)S(1)} %copy-done.5, ...), custom_call_target="tpu_custom_call" | custom-call | flops 1 | bytes 1 | tf_op jit(solution)/shard_map/pallas_call | solution.py:458
  61.7 0.0 collective-permute-done.3.refs_1_
  61.8 0.4 collective-permute-done.4.refs_2_
  62.1 0.0 collective-permute-done.5.refs_3_
  62.1 4.2 %collective-permute-start.6 = (f32[64,1024]{1,0:T(8,128)S(1)}, f32[64,1024]{1,0:T(8,128)S(1)}, u32[]{:S(2)}, u32[]{:S(2)}) collective-permute-start(f32[64,1024]{1,0:T(8,128)S(1)} %get-tuple-element.82), channel_id=1, source_target_pairs={{0,4},{1,5},{2,6},{3,7},{4,0},{5,1},{6,2},{7,3},{8,12},{9,13},{10,... | collective-permute-start | bytes 786440 | tf_op jit(solution)/shard_map/ppermute | solution.py:407
  66.3 1.0 collective-permute-start.7
  67.3 1.5 %collective-permute-start.8 = (f32[64,1024]{1,0:T(8,128)S(1)}, f32[64,1024]{1,0:T(8,128)}, u32[]{:S(2)}, u32[]{:S(2)}) collective-permute-start(f32[64,1024]{1,0:T(8,128)S(1)} %get-tuple-element.84), channel_id=1, source_target_pairs={{0,12},{1,13},{2,14},{3,15},{4,8},{5,9},{6,10},{7,11},{8,4},{9,5},... | collective-permute-start | bytes 786440 | tf_op jit(solution)/shard_map/ppermute | solution.py:407
  68.7 0.3 shard_map.71
  69.1 0.9 copy-done.3
  70.0 0.7 copy-done.4
  70.7 13.2 %shard_map.72 = f32[256,1024]{1,0:T(8,128)} custom-call(f32[256,1408]{1,0:T(8,128)} %bitcast.7, f32[256,768]{1,0:T(8,128)} %copy-done.3, f32[256,768]{1,0:T(8,128)} %copy-done.3, f32[256,384]{1,0:T(8,128)} %copy-done.2, f32[256,256]{1,0:T(8,128)} %copy-done.4, f32[16,256]{1,0:T(8,128)} %get-tuple-element.71.weight_ref, f32[16,256]{1,0:T(8,128)} %get-tuple-element.72.reading_ref), custom_call_target="tpu_custom_call" | custom-call | flops 1 | bytes 1 | tf_op jit(solution)/shard_map/pallas_call | solution.py:484
  83.9 3.7 %all-to-all-start.1 = ((f32[16,16,1024]{2,1,0:T(8,128)}), f32[16,16,1024]{2,1,0:T(8,128)S(1)}, u32[]{:S(2)}, u32[]{:S(2)}) async-start(f32[16,16,1024]{2,1,0:T(8,128)} %bitcast.9), calls=%async_computation.1 | async-start | bytes 2097152 | tf_op jit(solution)/shard_map/all_to_all | solution.py:428
  87.7 0.0 collective-permute-done.6.refs_1_
  87.7 0.1 collective-permute-done.7.refs_2_
  87.8 0.0 collective-permute-done.8.refs_3_
  87.8 1.1 shard_map.70
  88.9 0.4 collective-permute-start.9
  89.3 1.7 %collective-permute-start.10 = (f32[64,1024]{1,0:T(8,128)S(1)}, f32[64,1024]{1,0:T(8,128)S(1)}, u32[]{:S(2)}, u32[]{:S(2)}) collective-permute-start(f32[64,1024]{1,0:T(8,128)S(1)} %get-tuple-element.87), channel_id=1, source_target_pairs={{0,2},{1,3},{2,0},{3,1},{4,6},{5,7},{6,4},{7,5},{8,10},{9,11},{10,... | collective-permute-start | bytes 786440 | tf_op jit(solution)/shard_map/ppermute | solution.py:407
  90.9 0.0 collective-permute-start.11
  90.9 0.0 collective-permute-done.9.refs_1_
  91.0 14.3 %collective-permute-done.10.refs_2_ = f32[64,1024]{1,0:T(8,128)S(1)} collective-permute-done((f32[64,1024]{1,0:T(8,128)S(1)}, f32[64,1024]{1,0:T(8,128)S(1)}, u32[]{:S(2)}, u32[]{:S(2)}) %collective-permute-start.10) | collective-permute-done | bytes 262176 | tf_op jit(solution)/shard_map/ppermute | solution.py:407
  105.3 7.5 %collective-permute-done.11.refs_3_ = f32[64,1024]{1,0:T(8,128)S(1)} collective-permute-done((f32[64,1024]{1,0:T(8,128)S(1)}, f32[64,1024]{1,0:T(8,128)S(1)}, u32[]{:S(2)}, u32[]{:S(2)}) %collective-permute-start.11) | collective-permute-done | bytes 262176 | tf_op jit(solution)/shard_map/ppermute | solution.py:407
  112.8 1.6 %shard_map.73 = f32[16,32768]{1,0:T(8,128)} custom-call(f32[64,1024]{1,0:T(8,128)S(1)} %get-tuple-element.85.refs_0_, f32[64,1024]{1,0:T(8,128)S(1)} %collective-permute-done.9.refs_1_, f32[64,1024]{1,0:T(8,128)S(1)} %collective-permute-done.10.refs_2_, f32[64,1024]{1,0:T(8,128)S(1)} %collective-permute-done.11.refs_3_, f32[256,1024]{1,0:T(8,128)S(1)} %bitcast.8), custom_call_target="tpu_custom_call" | custom-call | flops 1 | bytes 1 | tf_op jit(solution)/shard_map/pallas_call | solution.py:502
  (17 shorter events, 0.0 us)
Async XLA Ops:
  3.8 7.6 %copy-start.1 = (f32[16,32768]{1,0:T(8,128)S(1)}, f32[16,32768]{1,0:T(8,128)}, u32[]{:S(2)}) copy-start(f32[16,32768]{1,0:T(8,128)} %fields_ref.3) | copy-start | bytes 6291460
  3.9 43.9 %all-to-all-start = ((f32[16,16,1408]{2,1,0:T(8,128)}), f32[16,16,1408]{2,1,0:T(8,128)S(1)}, u32[]{:S(2)}, u32[]{:S(2)}) async-start(f32[16,16,1408]{2,1,0:T(8,128)} %shard_map.64), calls=%async_computation | async-start | bytes 2883584 | tf_op jit(solution)/shard_map/all_to_all | solution.py:428
  11.4 23.8 %copy-start.9 = (s32[16,5]{0,1:T(8,128)S(1)}, s32[16,5]{0,1:T(8,128)}, u32[]{:S(2)}) copy-start(s32[16,5]{0,1:T(8,128)} %param.11) | copy-start | bytes 964
  12.2 2.2 %collective-permute-start = (f32[64,768]{1,0:T(8,128)S(1)}, f32[64,768]{1,0:T(8,128)S(1)}, u32[]{:S(2)}, u32[]{:S(2)}) collective-permute-start(f32[64,768]{1,0:T(8,128)S(1)} %get-tuple-element.51), channel_id=1, source_target_pairs={{0,1},{1,0},{2,3},{3,2},{4,5},{5,4},{6,7},{7,6},{8,9},{9,8},{10,11... | collective-permute-start | bytes 589832 | tf_op jit(solution)/shard_map/ppermute | solution.py:407
  12.6 18.0 %collective-permute-start.1 = (f32[64,768]{1,0:T(8,128)S(1)}, f32[64,768]{1,0:T(8,128)S(1)}, u32[]{:S(2)}, u32[]{:S(2)}) collective-permute-start(f32[64,768]{1,0:T(8,128)S(1)} %get-tuple-element.52), channel_id=1, source_target_pairs={{0,2},{1,3},{2,0},{3,1},{4,6},{5,7},{6,4},{7,5},{8,10},{9,11},{10,... | collective-permute-start | bytes 589832 | tf_op jit(solution)/shard_map/ppermute | solution.py:407
  14.3 20.0 %collective-permute-start.2 = (f32[64,768]{1,0:T(8,128)S(1)}, f32[64,768]{1,0:T(8,128)S(1)}, u32[]{:S(2)}, u32[]{:S(2)}) collective-permute-start(f32[64,768]{1,0:T(8,128)S(1)} %get-tuple-element.53), channel_id=1, source_target_pairs={{0,3},{1,2},{2,1},{3,0},{4,7},{5,6},{6,5},{7,4},{8,11},{9,10},{10,... | collective-permute-start | bytes 589832 | tf_op jit(solution)/shard_map/ppermute | solution.py:407
  42.3 26.5 %copy-start.8 = (s32[4,128]{1,0:T(4,128)S(1)}, s32[4,128]{1,0:T(4,128)}, u32[]{:S(2)}) copy-start(s32[4,128]{1,0:T(4,128)} %get-tuple-element.70.position_ref) | copy-start | bytes 6148
  42.3 19.5 %collective-permute-start.3 = (f32[64,768]{1,0:T(8,128)}, f32[64,768]{1,0:T(8,128)S(1)}, u32[]{:S(2)}, u32[]{:S(2)}) collective-permute-start(f32[64,768]{1,0:T(8,128)} %get-tuple-element.78), channel_id=1, source_target_pairs={{0,4},{1,5},{2,6},{3,7},{4,0},{5,1},{6,2},{7,3},{8,12},{9,13},{10,... | collective-permute-start | bytes 589832 | tf_op jit(solution)/shard_map/ppermute | solution.py:407
  42.6 19.5 %collective-permute-start.4 = (f32[64,768]{1,0:T(8,128)}, f32[64,768]{1,0:T(8,128)S(1)}, u32[]{:S(2)}, u32[]{:S(2)}) collective-permute-start(f32[64,768]{1,0:T(8,128)} %get-tuple-element.79), channel_id=1, source_target_pairs={{0,8},{1,9},{2,10},{3,11},{4,12},{5,13},{6,14},{7,15},{8,0},{9,1},... | collective-permute-start | bytes 589832 | tf_op jit(solution)/shard_map/ppermute | solution.py:407
  47.8 14.4 %collective-permute-start.5 = (f32[64,768]{1,0:T(8,128)S(1)}, f32[64,768]{1,0:T(8,128)S(1)}, u32[]{:S(2)}, u32[]{:S(2)}) collective-permute-start(f32[64,768]{1,0:T(8,128)S(1)} %get-tuple-element.80), channel_id=1, source_target_pairs={{0,12},{1,13},{2,14},{3,15},{4,8},{5,9},{6,10},{7,11},{8,4},{9,5},... | collective-permute-start | bytes 589832 | tf_op jit(solution)/shard_map/ppermute | solution.py:407
  47.8 21.3 %copy-start = (f32[16,16,1408]{2,1,0:T(8,128)}, f32[16,16,1408]{2,1,0:T(8,128)S(1)}, u32[]{:S(2)}) copy-start(f32[16,16,1408]{2,1,0:T(8,128)S(1)} %all-to-all-done) | copy-start | bytes 4325380
  47.8 0.6 copy-start.7
  48.8 0.7 copy-start.5
  49.5 0.7 copy-start.6
  50.3 18.8 %copy-start.2 = (f32[256,384]{1,0:T(8,128)}, f32[256,384]{1,0:T(8,128)S(1)}, u32[]{:S(2)}) copy-start(f32[256,384]{1,0:T(8,128)S(1)} %shard_map.68.here_ref.there_ref) | copy-start | bytes 1179652
  62.1 25.5 %collective-permute-start.6 = (f32[64,1024]{1,0:T(8,128)S(1)}, f32[64,1024]{1,0:T(8,128)S(1)}, u32[]{:S(2)}, u32[]{:S(2)}) collective-permute-start(f32[64,1024]{1,0:T(8,128)S(1)} %get-tuple-element.82), channel_id=1, source_target_pairs={{0,4},{1,5},{2,6},{3,7},{4,0},{5,1},{6,2},{7,3},{8,12},{9,13},{10,... | collective-permute-start | bytes 786440 | tf_op jit(solution)/shard_map/ppermute | solution.py:407
  66.3 21.5 %collective-permute-start.7 = (f32[64,1024]{1,0:T(8,128)S(1)}, f32[64,1024]{1,0:T(8,128)}, u32[]{:S(2)}, u32[]{:S(2)}) collective-permute-start(f32[64,1024]{1,0:T(8,128)S(1)} %get-tuple-element.83), channel_id=1, source_target_pairs={{0,8},{1,9},{2,10},{3,11},{4,12},{5,13},{6,14},{7,15},{8,0},{9,1},... | collective-permute-start | bytes 786440 | tf_op jit(solution)/shard_map/ppermute | solution.py:407
  67.3 20.5 %collective-permute-start.8 = (f32[64,1024]{1,0:T(8,128)S(1)}, f32[64,1024]{1,0:T(8,128)}, u32[]{:S(2)}, u32[]{:S(2)}) collective-permute-start(f32[64,1024]{1,0:T(8,128)S(1)} %get-tuple-element.84), channel_id=1, source_target_pairs={{0,12},{1,13},{2,14},{3,15},{4,8},{5,9},{6,10},{7,11},{8,4},{9,5},... | collective-permute-start | bytes 786440 | tf_op jit(solution)/shard_map/ppermute | solution.py:407
  69.1 0.9 copy-start.3
  70.0 0.7 copy-start.4
  83.9 28.9 %all-to-all-start.1 = ((f32[16,16,1024]{2,1,0:T(8,128)}), f32[16,16,1024]{2,1,0:T(8,128)S(1)}, u32[]{:S(2)}, u32[]{:S(2)}) async-start(f32[16,16,1024]{2,1,0:T(8,128)} %bitcast.9), calls=%async_computation.1 | async-start | bytes 2097152 | tf_op jit(solution)/shard_map/all_to_all | solution.py:428
  88.9 2.1 %collective-permute-start.9 = (f32[64,1024]{1,0:T(8,128)S(1)}, f32[64,1024]{1,0:T(8,128)S(1)}, u32[]{:S(2)}, u32[]{:S(2)}) collective-permute-start(f32[64,1024]{1,0:T(8,128)S(1)} %get-tuple-element.86), channel_id=1, source_target_pairs={{0,1},{1,0},{2,3},{3,2},{4,5},{5,4},{6,7},{7,6},{8,9},{9,8},{10,11... | collective-permute-start | bytes 786440 | tf_op jit(solution)/shard_map/ppermute | solution.py:407
  89.3 16.0 %collective-permute-start.10 = (f32[64,1024]{1,0:T(8,128)S(1)}, f32[64,1024]{1,0:T(8,128)S(1)}, u32[]{:S(2)}, u32[]{:S(2)}) collective-permute-start(f32[64,1024]{1,0:T(8,128)S(1)} %get-tuple-element.87), channel_id=1, source_target_pairs={{0,2},{1,3},{2,0},{3,1},{4,6},{5,7},{6,4},{7,5},{8,10},{9,11},{10,... | collective-permute-start | bytes 786440 | tf_op jit(solution)/shard_map/ppermute | solution.py:407
  90.9 21.8 %collective-permute-start.11 = (f32[64,1024]{1,0:T(8,128)S(1)}, f32[64,1024]{1,0:T(8,128)S(1)}, u32[]{:S(2)}, u32[]{:S(2)}) collective-permute-start(f32[64,1024]{1,0:T(8,128)S(1)} %get-tuple-element.88), channel_id=1, source_target_pairs={{0,3},{1,2},{2,1},{3,0},{4,7},{5,6},{6,5},{7,4},{8,11},{9,10},{10,... | collective-permute-start | bytes 786440 | tf_op jit(solution)/shard_map/ppermute | solution.py:407

commit v5 on v4

--- a/solution.py
+++ b/solution.py
@@ -164,7 +164,7 @@
 
 
 def terms_kernel(
-    amount, members, reading_ref, precision_ref, position_ref, tally_ref, adjacent_ref, weight_ref, shown_ref, quad_ref
+    amount, members, reading_ref, precision_ref, position_ref, tally_ref, adjacent_ref, terms_ref, quad_ref
 ):
     first_block = lax.axis_index("state") * amount
     total = tally_ref.shape[0]
@@ -209,8 +209,8 @@
         decay = jnp.exp(-0.5 * (distance / LOC) ** 2)
         active = jnp.where(wide % OB < pair(tallies, quad), usable, 0.0)
         weight = pair(precisions, quad) * decay * active
-        weight_ref[block : block + 1, :] = jnp.sqrt(weight / (members - 1.0))
-        shown_ref[block : block + 1, :] = pair(readings, quad)
+        terms_ref[0, block : block + 1, :] = jnp.sqrt(weight / (members - 1.0))
+        terms_ref[1, block : block + 1, :] = pair(readings, quad)
     edge = jnp.where(low, positions[quads], positions[0])
     for quad in range(quads):
         quad_ref[quad : quad + 1, :] = positions[quad] if quad else edge
@@ -221,12 +221,12 @@
     lanes = QUAD * OB
     vmem = pl.BlockSpec(memory_space=pltpu.VMEM)
     smem = pl.BlockSpec(memory_space=pltpu.SMEM)
-    terms = jax.ShapeDtypeStruct((amount, 2 * lanes), jnp.float32)
+    terms = jax.ShapeDtypeStruct((2, amount, 2 * lanes), jnp.float32)
     return pl.pallas_call(
         functools.partial(terms_kernel, amount, members),
-        out_shape=[terms, terms, jax.ShapeDtypeStruct((amount // QUAD, lanes), jnp.int32)],
+        out_shape=[terms, jax.ShapeDtypeStruct((amount // QUAD, lanes), jnp.int32)],
         in_specs=[vmem, vmem, vmem, smem, smem],
-        out_specs=[vmem, vmem, vmem],
+        out_specs=[vmem, vmem],
     )(*(array.reshape(-1, lanes) for array in (reading, precision, position)), tally, adjacent)
 
 
@@ -334,21 +334,21 @@
     return jnp.concatenate([ref[pl.ds(start, rows), :] for start in starts], axis=0)
 
 
-def blocks_of(fields, here, there, first, weight_ref, reading_ref):
+def blocks_of(fields, here, there, first, terms_ref):
     span = PARTITION_SPAN
     seen = jnp.concatenate([here, there], axis=1)
     blocks = []
     for spot in range(QUAD):
-        terms = [ref[pl.ds(first + spot, 1), :] for ref in (weight_ref, reading_ref)]
-        blocks.append((fields[:, spot * span : (spot + 1) * span], seen, *terms))
+        root_weight, reading = (terms_ref[term, pl.ds(first + spot, 1), :] for term in range(2))
+        blocks.append((fields[:, spot * span : (spot + 1) * span], seen, root_weight, reading))
     return blocks
 
 
-def head_kernel(devices, fields_ref, here_ref, there_ref, weight_ref, reading_ref, *results):
+def head_kernel(devices, fields_ref, here_ref, there_ref, terms_ref, *results):
     span = PARTITION_SPAN
     first = pl.program_id(0) * QUAD
     fields, here, there = [reordered(ref, devices) for ref in (fields_ref, here_ref, there_ref)]
-    for spot, result in enumerate(updated(blocks_of(fields, here, there, first, weight_ref, reading_ref))):
+    for spot, result in enumerate(updated(blocks_of(fields, here, there, first, terms_ref))):
         start = 0
         for result_ref in results:
             rows = result_ref.shape[0]
@@ -356,15 +356,15 @@
             start += rows
 
 
-def tail_kernel(first_ref, begin_ref, end_ref, here_ref, tiles_ref, weight_ref, reading_ref, result_ref):
+def tail_kernel(first_ref, begin_ref, end_ref, here_ref, tiles_ref, terms_ref, result_ref):
     span = PARTITION_SPAN
     step = pl.program_id(0)
     begin = jnp.where(step == 0, first_ref[...], begin_ref[...])
     fields = jnp.concatenate([begin, end_ref[...]], axis=1)
     here = jnp.where(step == 0, here_ref[...], tiles_ref[:, :span])
     there = jnp.where(step == 0, tiles_ref[:, :span], tiles_ref[:, span:])
-    first = weight_ref.shape[0] + (step - 2) * QUAD
-    for spot, result in enumerate(updated(blocks_of(fields, here, there, first, weight_ref, reading_ref))):
+    first = terms_ref.shape[1] + (step - 2) * QUAD
+    for spot, result in enumerate(updated(blocks_of(fields, here, there, first, terms_ref))):
         result_ref[:, spot * span : (spot + 1) * span] = result
 
 
@@ -397,7 +397,7 @@
         return pl.BlockSpec((members, size), lambda step: (0, index))
 
     def full(array):
-        return pl.BlockSpec(array.shape, lambda step: (0, 0))
+        return pl.BlockSpec(array.shape, lambda step: (0,) * array.ndim)
 
     def group(parts, size):
         return jax.ShapeDtypeStruct((members // parts, size), jnp.float32)
@@ -441,13 +441,11 @@
     )(fields, observations[2].T)
     first = exchanged(sent).reshape(members, split + lanes)
     second = turned(swapped(second_parts(), 1), outer)
-    second, observations = lax.optimization_barrier((second, observations))
-    root_weight, reading, quad_position = window_terms(*observations, members)
-    second, root_weight, reading, quad_position = lax.optimization_barrier(
-        (second, root_weight, reading, quad_position)
-    )
+    second, tied = lax.optimization_barrier((second, [observations[0],observations[3]]))
+    observations = [tied[0], observations[1], observations[2], tied[1], observations[4]]
+    terms, quad_position = window_terms(*observations, members)
+    second, terms, quad_position = lax.optimization_barrier((second, terms, quad_position))
     second = swapped(second, INNER)
-    terms = [root_weight, reading]
     seen = call(
         pick_first_kernel,
         [vmem, vmem],
@@ -461,13 +459,13 @@
             pl.BlockSpec((members, width), lambda step: (0, step)),
             pl.BlockSpec((members, lanes), lambda step: (0, step)),
             pl.BlockSpec((members, lanes), lambda step: (0, step + 1)),
-            *[full(term) for term in terms],
+            full(terms),
         ],
         [group(outer, early * width)] * outer,
         grant=40,
         grid=(early,),
         out_specs=[pl.BlockSpec((members // outer, width), lambda step: (0, step))] * outer,
-    )(first, seen, seen, *terms)
+    )(first, seen, seen, terms)
     groups, second = lax.optimization_barrier((groups, second))
     beyond = swapped(groups, INNER)
 
@@ -489,13 +487,13 @@
             pl.BlockSpec((members, half), lambda step: (0, 2 * step)),
             columns(lanes, early),
             full(tiles),
-            *[full(term) for term in terms],
+            full(terms),
         ],
         jax.ShapeDtypeStruct((members, late * width), jnp.float32),
         grant=60,
         grid=(late,),
         out_specs=pl.BlockSpec((members, width), lambda step: (0, step)),
-    )(first, second, second, seen, tiles, *terms)
+    )(first, second, second, seen, tiles, terms)
     ends = exchanged(ends.reshape(devices, own_members, late * width)).reshape(members, late * width)
 
     near = turned(beyond, INNER, cost=1 << 36)
@@ -514,7 +512,7 @@
     amount = cells // PARTITION_SPAN
     members = own_members * devices
     span = PARTITION_SPAN
-    root_weight, reading, quad_position = window_terms(*observations, members)
+    (root_weight, reading), quad_position = window_terms(*observations, members)
     sent = fields.reshape(own_members, devices, cells).transpose(1, 0, 2)
     fields = lax.all_to_all(sent, "state", split_axis=0, concat_axis=0, tiled=True).reshape(members, cells)
     vmem = pl.BlockSpec(memory_space=pltpu.VMEM)

time: 115 us -> 113 us (0.983)
  waiting for transfers between devices: 42.4 us -> 38.1 us
    ppermute x12, waiting for transfers between devices: 42.4 us -> 38.1 us  [swapped(): lax.ppermute(arrays[k], 'state', pairs[k])]
    unnamed x20 -> x25, local copies, waits for them, and re-layouts: 3.66 us -> 6.99 us
    optimization_barrier x4 -> x1, local copies, waits for them, and re-layouts: 3.25 us -> 0.85 us  [in_stages(): lax.optimization_barrier((second, [observations[0], observations[3]]))]
  transfers between devices with their start and end apart: 14 -> 14, of which waited for: 6 -> 5; matrix products, arithmetic and copies ran while one was open for 5% -> 5% of each run, Pallas kernels for 26% -> 27%
where the time goes in v5:
time: 113 us; the launch traced here: 112 us
  waiting for transfers between devices  38.1 us (34%)
  Pallas kernels  36.1 us (32%)
  starting transfers between devices  27.7 us (25%)
  local copies, waits for them, and re-layouts  9.96 us (9%)
    ppermute x12, waiting for transfers between devices, swapped(): lax.ppermute(arrays[k], 'state', pairs[k])  38.1 us
    ppermute x12, starting transfers between devices, swapped(): lax.ppermute(arrays[k], 'state', pairs[k])  16.3 us
    pallas_call x1, Pallas kernels, in_stages(): call(tail_kernel, [columns(half, split // half - 1), columns(half, 1), pl...  13.2 us
    pallas_call x1, Pallas kernels, in_stages(): call(functools.partial(head_kernel, devices), [pl.BlockSpec((members, wid...  11.5 us
    all_to_all x2, starting transfers between devices, exchanged(): lax.all_to_all(array, 'state', split_axis=0, concat_axis=0, tiled=True)  11.4 us
    unnamed x25, local copies, waits for them, and re-layouts  6.99 us
    pallas_call x1, Pallas kernels, in_stages(): call(functools.partial(first_part_kernel, split), [anywhere, vmem], jax.S...  3.83 us
  transfers between devices with their start and end apart: 14, of which 5 were waited for; matrix products, arithmetic and copies ran while one was open for 5% of the time, Pallas kernels for 27%

profile of v5, /device:TPU:0, one launch (start us, length us, event | category | flops | bytes accessed | tf_op | source)
XLA Modules:
  0.0 112.1 jit_solution(2186076505883327777)
XLA Ops:
  0.0 3.8 %shard_map.64 = f32[16,16,1408]{2,1,0:T(8,128)} custom-call(f32[16,32768]{1,0:T(8,128)} %fields_ref.3, s32[32,256]{1,0:T(8,128)} %bitcast.10), custom_call_target="tpu_custom_call" | custom-call | flops 1 | bytes 1 | tf_op jit(solution)/shard_map/pallas_call | solution.py:431
  3.8 0.0 copy-start.1
  3.9 0.0 copy-start.10
  3.9 7.5 %all-to-all-start = ((f32[16,16,1408]{2,1,0:T(8,128)}), f32[16,16,1408]{2,1,0:T(8,128)S(1)}, u32[]{:S(2)}, u32[]{:S(2)}) async-start(f32[16,16,1408]{2,1,0:T(8,128)} %shard_map.64), calls=%async_computation | async-start | bytes 2883584 | tf_op jit(solution)/shard_map/all_to_all | solution.py:428
  11.4 1.5 %shard_map.65 = (f32[64,768]{1,0:T(8,128)S(1)}, f32[64,768]{1,0:T(8,128)}, f32[64,768]{1,0:T(8,128)}, f32[64,768]{1,0:T(8,128)}) custom-call(f32[16,32768]{1,0:T(8,128)S(1)} %copy-done.1), custom_call_target="tpu_custom_call" | custom-call | flops 1 | bytes 1 | tf_op jit(solution)/shard_map/pallas_call | solution.py:410
  13.0 0.7 copy-done.5
  13.6 0.4 collective-permute-start
  14.0 1.7 %collective-permute-start.1 = (f32[64,768]{1,0:T(8,128)}, f32[64,768]{1,0:T(8,128)S(1)}, u32[]{:S(2)}, u32[]{:S(2)}) collective-permute-start(f32[64,768]{1,0:T(8,128)} %get-tuple-element.47), channel_id=1, source_target_pairs={{0,2},{1,3},{2,0},{3,1},{4,6},{5,7},{6,4},{7,5},{8,10},{9,11},{10,... | collective-permute-start | bytes 589832 | tf_op jit(solution)/shard_map/ppermute | solution.py:407
  15.7 0.0 collective-permute-start.2
  15.7 0.9 copy.13
  16.6 0.7 copy.14.adjacent_ref
  17.3 0.9 copy.12
  18.1 0.7 reshape.20.precision_ref
  18.8 0.7 reshape.21.position_ref
  19.5 11.1 %collective-permute-done.1.refs_2_ = f32[64,768]{1,0:T(8,128)S(1)} collective-permute-done((f32[64,768]{1,0:T(8,128)}, f32[64,768]{1,0:T(8,128)S(1)}, u32[]{:S(2)}, u32[]{:S(2)}) %collective-permute-start.1) | collective-permute-done | bytes 196640 | tf_op jit(solution)/shard_map/ppermute | solution.py:407
  30.6 3.9 %collective-permute-done.2.refs_3_ = f32[64,768]{1,0:T(8,128)S(1)} collective-permute-done((f32[64,768]{1,0:T(8,128)}, f32[64,768]{1,0:T(8,128)S(1)}, u32[]{:S(2)}, u32[]{:S(2)}) %collective-permute-start.2) | collective-permute-done | bytes 196640 | tf_op jit(solution)/shard_map/ppermute | solution.py:407
  34.6 0.9 copy-done.6
  35.5 0.8 shard_map.66
  36.3 0.9 copy.11
  37.2 0.7 reshape.19.reading_ref
  37.9 1.8 %shard_map.67 = (f32[2,16,256]{2,1,0:T(8,128)}, s32[4,128]{1,0:T(4,128)}) custom-call(f32[64,128]{1,0:T(8,128)} %reshape.19.reading_ref, f32[64,128]{1,0:T(8,128)} %reshape.20.precision_ref, s32[64,128]{1,0:T(8,128)} %reshape.21.position_ref, s32[256]{0:T(256)} %tally_ref, s32[16,5]{1,0:T(8,128)} %copy.14.adjacent_ref), custom_call_target="tpu_custom_call" | custom-call | tf_op jit(solution)/shard_map/pallas_call | solution.py:225
  39.7 0.1 collective-permute-start.3
  39.8 5.2 %collective-permute-start.4 = (f32[64,768]{1,0:T(8,128)}, f32[64,768]{1,0:T(8,128)S(1)}, u32[]{:S(2)}, u32[]{:S(2)}) collective-permute-start(f32[64,768]{1,0:T(8,128)} %get-tuple-element.69), channel_id=1, source_target_pairs={{0,8},{1,9},{2,10},{3,11},{4,12},{5,13},{6,14},{7,15},{8,0},{9,1},... | collective-permute-start | bytes 589832 | tf_op jit(solution)/shard_map/ppermute | solution.py:407
  44.9 0.0 all-to-all-done
  44.9 0.6 copy-done.8
  45.6 0.4 shard_map.68.here_ref.there_ref
  46.0 0.7 copy-done.7
  46.7 11.5 %shard_map.69 = (f32[64,1024]{1,0:T(8,128)S(1)}, f32[64,1024]{1,0:T(8,128)S(1)}, f32[64,1024]{1,0:T(8,128)S(1)}, f32[64,1024]{1,0:T(8,128)S(1)}) custom-call(f32[256,1408]{1,0:T(8,128)S(1)} %bitcast.5, f32[256,384]{1,0:T(8,128)S(1)} %shard_map.68.here_ref.there_ref, f32[256,384]{1,0:T(8,128)S(1)} %shard_map.68.here_ref.there_ref, f32[2,16,256]{2,1,0:T(8,128)S(1)} %copy-done.7), custom_call_target="tpu_custom_call" | custom-call | flops 1 | bytes 1 | tf_op jit(solution)/shard_map/pallas_call | solution.py:456
  58.2 0.0 collective-permute-done.3.refs_1_
  58.2 1.1 %collective-permute-done.4.refs_2_ = f32[64,768]{1,0:T(8,128)S(1)} collective-permute-done((f32[64,768]{1,0:T(8,128)}, f32[64,768]{1,0:T(8,128)S(1)}, u32[]{:S(2)}, u32[]{:S(2)}) %collective-permute-start.4) | collective-permute-done | bytes 196640 | tf_op jit(solution)/shard_map/ppermute | solution.py:407
  59.4 4.5 %collective-permute-start.6 = (f32[64,1024]{1,0:T(8,128)S(1)}, f32[64,1024]{1,0:T(8,128)S(1)}, u32[]{:S(2)}, u32[]{:S(2)}) collective-permute-start(f32[64,1024]{1,0:T(8,128)S(1)} %get-tuple-element.72), channel_id=1, source_target_pairs={{0,4},{1,5},{2,6},{3,7},{4,0},{5,1},{6,2},{7,3},{8,12},{9,13},{10,... | collective-permute-start | bytes 786440 | tf_op jit(solution)/shard_map/ppermute | solution.py:407
  63.8 0.6 collective-permute-start.7
  64.4 1.8 %collective-permute-start.8 = (f32[64,1024]{1,0:T(8,128)S(1)}, f32[64,1024]{1,0:T(8,128)}, u32[]{:S(2)}, u32[]{:S(2)}) collective-permute-start(f32[64,1024]{1,0:T(8,128)S(1)} %get-tuple-element.74), channel_id=1, source_target_pairs={{0,12},{1,13},{2,14},{3,15},{4,8},{5,9},{6,10},{7,11},{8,4},{9,5},... | collective-permute-start | bytes 786440 | tf_op jit(solution)/shard_map/ppermute | solution.py:407
  66.2 0.3 shard_map.71
  66.6 0.9 copy-done.3
  67.5 0.7 copy-done.4
  68.2 13.2 %shard_map.72 = f32[256,1024]{1,0:T(8,128)} custom-call(f32[256,1408]{1,0:T(8,128)} %bitcast.7, f32[256,768]{1,0:T(8,128)} %copy-done.3, f32[256,768]{1,0:T(8,128)} %copy-done.3, f32[256,384]{1,0:T(8,128)} %copy-done.2, f32[256,256]{1,0:T(8,128)} %copy-done.4, f32[2,16,256]{2,1,0:T(8,128)} %get-tuple-element.62.terms_ref), custom_call_target="tpu_custom_call" | custom-call | flops 1 | bytes 1 | tf_op jit(solution)/shard_map/pallas_call | solution.py:482
  81.4 3.9 %all-to-all-start.1 = ((f32[16,16,1024]{2,1,0:T(8,128)}), f32[16,16,1024]{2,1,0:T(8,128)S(1)}, u32[]{:S(2)}, u32[]{:S(2)}) async-start(f32[16,16,1024]{2,1,0:T(8,128)} %bitcast.9), calls=%async_computation.1 | async-start | bytes 2097152 | tf_op jit(solution)/shard_map/all_to_all | solution.py:428
  85.3 0.0 collective-permute-done.6.refs_1_
  85.3 0.0 collective-permute-done.7.refs_2_
  85.3 0.0 collective-permute-done.8.refs_3_
  85.3 1.1 shard_map.70
  86.4 0.4 collective-permute-start.9
  86.9 1.7 %collective-permute-start.10 = (f32[64,1024]{1,0:T(8,128)S(1)}, f32[64,1024]{1,0:T(8,128)S(1)}, u32[]{:S(2)}, u32[]{:S(2)}) collective-permute-start(f32[64,1024]{1,0:T(8,128)S(1)} %get-tuple-element.77), channel_id=1, source_target_pairs={{0,2},{1,3},{2,0},{3,1},{4,6},{5,7},{6,4},{7,5},{8,10},{9,11},{10,... | collective-permute-start | bytes 786440 | tf_op jit(solution)/shard_map/ppermute | solution.py:407
  88.6 0.0 collective-permute-start.11
  88.6 14.3 %collective-permute-done.10.refs_2_ = f32[64,1024]{1,0:T(8,128)S(1)} collective-permute-done((f32[64,1024]{1,0:T(8,128)S(1)}, f32[64,1024]{1,0:T(8,128)S(1)}, u32[]{:S(2)}, u32[]{:S(2)}) %collective-permute-start.10) | collective-permute-done | bytes 262176 | tf_op jit(solution)/shard_map/ppermute | solution.py:407
  102.9 7.5 %collective-permute-done.11.refs_3_ = f32[64,1024]{1,0:T(8,128)S(1)} collective-permute-done((f32[64,1024]{1,0:T(8,128)S(1)}, f32[64,1024]{1,0:T(8,128)S(1)}, u32[]{:S(2)}, u32[]{:S(2)}) %collective-permute-start.11) | collective-permute-done | bytes 262176 | tf_op jit(solution)/shard_map/ppermute | solution.py:407
  110.4 1.6 %shard_map.73 = f32[16,32768]{1,0:T(8,128)} custom-call(f32[64,1024]{1,0:T(8,128)S(1)} %get-tuple-element.75.refs_0_, f32[64,1024]{1,0:T(8,128)S(1)} %collective-permute-done.9.refs_1_, f32[64,1024]{1,0:T(8,128)S(1)} %collective-permute-done.10.refs_2_, f32[64,1024]{1,0:T(8,128)S(1)} %collective-permute-done.11.refs_3_, f32[256,1024]{1,0:T(8,128)S(1)} %bitcast.8), custom_call_target="tpu_custom_call" | custom-call | flops 1 | bytes 1 | tf_op jit(solution)/shard_map/pallas_call | solution.py:500
  (19 shorter events, 0.0 us)
Async XLA Ops:
  3.8 7.6 %copy-start.1 = (f32[16,32768]{1,0:T(8,128)S(1)}, f32[16,32768]{1,0:T(8,128)}, u32[]{:S(2)}) copy-start(f32[16,32768]{1,0:T(8,128)} %fields_ref.3) | copy-start | bytes 6291460
  3.9 12.7 %copy-start.10 = (s32[16,5]{0,1:T(8,128)S(1)}, s32[16,5]{0,1:T(8,128)}, u32[]{:S(2)}) copy-start(s32[16,5]{0,1:T(8,128)} %param.11) | copy-start | bytes 964
  3.9 41.1 %all-to-all-start = ((f32[16,16,1408]{2,1,0:T(8,128)}), f32[16,16,1408]{2,1,0:T(8,128)S(1)}, u32[]{:S(2)}, u32[]{:S(2)}) async-start(f32[16,16,1408]{2,1,0:T(8,128)} %shard_map.64), calls=%async_computation | async-start | bytes 2883584 | tf_op jit(solution)/shard_map/all_to_all | solution.py:428
  13.0 0.7 copy-start.5
  13.6 5.9 %collective-permute-start = (f32[64,768]{1,0:T(8,128)}, f32[64,768]{1,0:T(8,128)S(1)}, u32[]{:S(2)}, u32[]{:S(2)}) collective-permute-start(f32[64,768]{1,0:T(8,128)} %get-tuple-element.46), channel_id=1, source_target_pairs={{0,1},{1,0},{2,3},{3,2},{4,5},{5,4},{6,7},{7,6},{8,9},{9,8},{10,11... | collective-permute-start | bytes 589832 | tf_op jit(solution)/shard_map/ppermute | solution.py:407
  14.0 16.6 %collective-permute-start.1 = (f32[64,768]{1,0:T(8,128)}, f32[64,768]{1,0:T(8,128)S(1)}, u32[]{:S(2)}, u32[]{:S(2)}) collective-permute-start(f32[64,768]{1,0:T(8,128)} %get-tuple-element.47), channel_id=1, source_target_pairs={{0,2},{1,3},{2,0},{3,1},{4,6},{5,7},{6,4},{7,5},{8,10},{9,11},{10,... | collective-permute-start | bytes 589832 | tf_op jit(solution)/shard_map/ppermute | solution.py:407
  15.7 18.9 %collective-permute-start.2 = (f32[64,768]{1,0:T(8,128)}, f32[64,768]{1,0:T(8,128)S(1)}, u32[]{:S(2)}, u32[]{:S(2)}) collective-permute-start(f32[64,768]{1,0:T(8,128)} %get-tuple-element.48), channel_id=1, source_target_pairs={{0,3},{1,2},{2,1},{3,0},{4,7},{5,6},{6,5},{7,4},{8,11},{9,10},{10,... | collective-permute-start | bytes 589832 | tf_op jit(solution)/shard_map/ppermute | solution.py:407
  34.6 0.9 copy-start.6
  39.7 26.5 %copy-start.9 = (s32[4,128]{1,0:T(4,128)S(1)}, s32[4,128]{1,0:T(4,128)}, u32[]{:S(2)}) copy-start(s32[4,128]{1,0:T(4,128)} %get-tuple-element.61.position_ref) | copy-start | bytes 6148
  39.7 18.5 %collective-permute-start.3 = (f32[64,768]{1,0:T(8,128)}, f32[64,768]{1,0:T(8,128)S(1)}, u32[]{:S(2)}, u32[]{:S(2)}) collective-permute-start(f32[64,768]{1,0:T(8,128)} %get-tuple-element.68), channel_id=1, source_target_pairs={{0,4},{1,5},{2,6},{3,7},{4,0},{5,1},{6,2},{7,3},{8,12},{9,13},{10,... | collective-permute-start | bytes 589832 | tf_op jit(solution)/shard_map/ppermute | solution.py:407
  39.8 19.6 %collective-permute-start.4 = (f32[64,768]{1,0:T(8,128)}, f32[64,768]{1,0:T(8,128)S(1)}, u32[]{:S(2)}, u32[]{:S(2)}) collective-permute-start(f32[64,768]{1,0:T(8,128)} %get-tuple-element.69), channel_id=1, source_target_pairs={{0,8},{1,9},{2,10},{3,11},{4,12},{5,13},{6,14},{7,15},{8,0},{9,1},... | collective-permute-start | bytes 589832 | tf_op jit(solution)/shard_map/ppermute | solution.py:407
  44.9 14.4 %collective-permute-start.5 = (f32[64,768]{1,0:T(8,128)S(1)}, f32[64,768]{1,0:T(8,128)S(1)}, u32[]{:S(2)}, u32[]{:S(2)}) collective-permute-start(f32[64,768]{1,0:T(8,128)S(1)} %get-tuple-element.70), channel_id=1, source_target_pairs={{0,12},{1,13},{2,14},{3,15},{4,8},{5,9},{6,10},{7,11},{8,4},{9,5},... | collective-permute-start | bytes 589832 | tf_op jit(solution)/shard_map/ppermute | solution.py:407
  44.9 21.6 %copy-start = (f32[16,16,1408]{2,1,0:T(8,128)}, f32[16,16,1408]{2,1,0:T(8,128)S(1)}, u32[]{:S(2)}) copy-start(f32[16,16,1408]{2,1,0:T(8,128)S(1)} %all-to-all-done) | copy-start | bytes 4325380
  44.9 0.6 copy-start.8
  46.0 0.8 copy-start.7
  46.7 19.8 %copy-start.2 = (f32[256,384]{1,0:T(8,128)}, f32[256,384]{1,0:T(8,128)S(1)}, u32[]{:S(2)}) copy-start(f32[256,384]{1,0:T(8,128)S(1)} %shard_map.68.here_ref.there_ref) | copy-start | bytes 1179652
  59.4 25.9 %collective-permute-start.6 = (f32[64,1024]{1,0:T(8,128)S(1)}, f32[64,1024]{1,0:T(8,128)S(1)}, u32[]{:S(2)}, u32[]{:S(2)}) collective-permute-start(f32[64,1024]{1,0:T(8,128)S(1)} %get-tuple-element.72), channel_id=1, source_target_pairs={{0,4},{1,5},{2,6},{3,7},{4,0},{5,1},{6,2},{7,3},{8,12},{9,13},{10,... | collective-permute-start | bytes 786440 | tf_op jit(solution)/shard_map/ppermute | solution.py:407
  63.8 21.5 %collective-permute-start.7 = (f32[64,1024]{1,0:T(8,128)S(1)}, f32[64,1024]{1,0:T(8,128)}, u32[]{:S(2)}, u32[]{:S(2)}) collective-permute-start(f32[64,1024]{1,0:T(8,128)S(1)} %get-tuple-element.73), channel_id=1, source_target_pairs={{0,8},{1,9},{2,10},{3,11},{4,12},{5,13},{6,14},{7,15},{8,0},{9,1},... | collective-permute-start | bytes 786440 | tf_op jit(solution)/shard_map/ppermute | solution.py:407
  64.4 20.9 %collective-permute-start.8 = (f32[64,1024]{1,0:T(8,128)S(1)}, f32[64,1024]{1,0:T(8,128)}, u32[]{:S(2)}, u32[]{:S(2)}) collective-permute-start(f32[64,1024]{1,0:T(8,128)S(1)} %get-tuple-element.74), channel_id=1, source_target_pairs={{0,12},{1,13},{2,14},{3,15},{4,8},{5,9},{6,10},{7,11},{8,4},{9,5},... | collective-permute-start | bytes 786440 | tf_op jit(solution)/shard_map/ppermute | solution.py:407
  66.6 0.9 copy-start.3
  67.5 0.7 copy-start.4
  81.4 29.0 %all-to-all-start.1 = ((f32[16,16,1024]{2,1,0:T(8,128)}), f32[16,16,1024]{2,1,0:T(8,128)S(1)}, u32[]{:S(2)}, u32[]{:S(2)}) async-start(f32[16,16,1024]{2,1,0:T(8,128)} %bitcast.9), calls=%async_computation.1 | async-start | bytes 2097152 | tf_op jit(solution)/shard_map/all_to_all | solution.py:428
  86.4 2.1 %collective-permute-start.9 = (f32[64,1024]{1,0:T(8,128)S(1)}, f32[64,1024]{1,0:T(8,128)S(1)}, u32[]{:S(2)}, u32[]{:S(2)}) collective-permute-start(f32[64,1024]{1,0:T(8,128)S(1)} %get-tuple-element.76), channel_id=1, source_target_pairs={{0,1},{1,0},{2,3},{3,2},{4,5},{5,4},{6,7},{7,6},{8,9},{9,8},{10,11... | collective-permute-start | bytes 786440 | tf_op jit(solution)/shard_map/ppermute | solution.py:407
  86.9 16.0 %collective-permute-start.10 = (f32[64,1024]{1,0:T(8,128)S(1)}, f32[64,1024]{1,0:T(8,128)S(1)}, u32[]{:S(2)}, u32[]{:S(2)}) collective-permute-start(f32[64,1024]{1,0:T(8,128)S(1)} %get-tuple-element.77), channel_id=1, source_target_pairs={{0,2},{1,3},{2,0},{3,1},{4,6},{5,7},{6,4},{7,5},{8,10},{9,11},{10,... | collective-permute-start | bytes 786440 | tf_op jit(solution)/shard_map/ppermute | solution.py:407
  88.6 21.8 %collective-permute-start.11 = (f32[64,1024]{1,0:T(8,128)S(1)}, f32[64,1024]{1,0:T(8,128)S(1)}, u32[]{:S(2)}, u32[]{:S(2)}) collective-permute-start(f32[64,1024]{1,0:T(8,128)S(1)} %get-tuple-element.78), channel_id=1, source_target_pairs={{0,3},{1,2},{2,1},{3,0},{4,7},{5,6},{6,5},{7,4},{8,11},{9,10},{10,... | collective-permute-start | bytes 786440 | tf_op jit(solution)/shard_map/ppermute | solution.py:407

commit v6 on v5

--- a/solution.py
+++ b/solution.py
@@ -236,31 +236,29 @@
     return copies
 
 
-def into_held(fields_ref, held_ref, sems, start, size):
-    devices = held_ref.shape[0]
+def first_part_kernel(fields_ref, given_ref, sent_ref, held_ref, edges_ref, position_ref, sems):
+    devices, rows, size = sent_ref.shape
     cells = fields_ref.shape[1] // devices
-    sources = [fields_ref.at[:, pl.ds(device * cells + start, size)] for device in range(devices)]
-    targets = [held_ref.at[device, :, pl.ds(0, size)] for device in range(devices)]
-    return copied([pltpu.make_async_copy(*pair, sems.at[index]) for index, pair in enumerate(zip(sources, targets))])
-
-
-def first_part_kernel(split, fields_ref, position_ref, sent_ref, held_ref, sems):
-    devices, rows, _ = sent_ref.shape
-    cells = fields_ref.shape[1] // devices
-    span = PARTITION_SPAN
+    span = PARTITION_SPAN
+    half = R * span
+    split = size - span
     amount = cells // span
-    into = into_held(fields_ref, held_ref, sems, 0, cells)
-
-    def out(number, some, start, size, to):
-        source = held_ref.at[some, :, pl.ds(start, size)]
-        target = sent_ref.at[some, :, pl.ds(to, size)]
-        return copied([pltpu.make_async_copy(source, target, sems.at[devices + number])])
-
-    away = []
-    for device, copy in enumerate(into):
+    copies = []
+
+    def add(start, length, target):
+        source = fields_ref.at[:, pl.ds(start, length)]
+        copies.append(pltpu.make_async_copy(source, target, sems.at[len(copies)]))
+
+    for device in range(devices):
+        add((device + 1) * cells - half, half, edges_ref.at[device, :, pl.ds(0, half)])
+        add(device * cells, half, edges_ref.at[device, :, pl.ds(half, half)])
+    copies.append(pltpu.make_async_copy(given_ref, position_ref, sems.at[len(copies)]))
+    ahead = len(copies)
+    for device in range(devices):
+        add(device * cells, split, held_ref.at[device, :, pl.ds(0, split)])
+    copied(copies)
+    for copy in copies[:ahead]:
         copy.wait()
-        if device % INNER == INNER - 1:
-            away += out(len(away), pl.ds(device + 1 - INNER, INNER), 0, split, 0)
 
     def shifted(array, distance):
         if distance > 0:
@@ -272,12 +270,18 @@
     position = jnp.concatenate([shifted(positions[:, block], distance) for block, distance in beyond], axis=1)
     position = jnp.broadcast_to(position[:, None], (devices, rows, span)).reshape(devices * rows, span)
     fields = [
-        shifted(held_ref[:, :, block * span : (block + 1) * span].reshape(devices * rows, span), distance * rows)
-        for block, distance in beyond
+        shifted(edges_ref[:, :, spot * span : (spot + 1) * span].reshape(devices * rows, span), distance * rows)
+        for spot, (_, distance) in enumerate(beyond)
     ]
-    held_ref[:, :, cells : cells + span] = picked(fields, position).reshape(devices, rows, span)
-    away += out(len(away), pl.ds(0, devices), cells, span, split)
-    for copy in away:
+    held_ref[:, :, split:] = picked(fields, position).reshape(devices, rows, span)
+    out = []
+    for device, copy in enumerate(copies[ahead:]):
+        copy.wait()
+        if device % INNER == INNER - 1:
+            some = pl.ds(device + 1 - INNER, INNER)
+            sem = sems.at[len(copies) + len(out)]
+            out += copied([pltpu.make_async_copy(held_ref.at[some], sent_ref.at[some], sem)])
+    for copy in out:
         copy.wait()
 
 
@@ -305,21 +309,7 @@
             target[i * rows : (i + 1) * rows, :] = source[j * rows : (j + 1) * rows, :]
 
 
-def place_kernel(cells, *refs):
-    *parts, last_ref, result_ref, sems = refs
-    place = lax.axis_index("state")
-    rows = result_ref.shape[0]
-    moves = []
-    for near, part in enumerate(parts):
-        width = part.shape[1]
-        for far in range(part.shape[0] // rows):
-            start = (place ^ (far * INNER + near)) * cells
-            target = result_ref.at[:, pl.ds(pl.multiple_of(start, width), width)]
-            moves.append((part.at[pl.ds(far * rows, rows), :], target))
-    for device in range(last_ref.shape[0] // rows):
-        size = last_ref.shape[1]
-        target = result_ref.at[:, pl.ds((device + 1) * cells - size, size)]
-        moves.append((last_ref.at[pl.ds(device * rows, rows), :], target))
+def place_moves(moves, sems):
     started = [pltpu.make_async_copy(*move, sems.at[index]) for index, move in enumerate(moves)]
     for copy in started:
         copy.start()
@@ -327,10 +317,54 @@
         copy.wait()
 
 
-def reordered(ref, devices):
+def place_kernel(cells, *refs):
+    *parts, result_ref, sems = refs
+    firsts, seconds = parts[:-INNER], parts[-INNER:]
+    place = lax.axis_index("state")
+    rows = result_ref.shape[0]
+    width = QUAD * PARTITION_SPAN
+    moves = []
+
+    def add(source, distance, start):
+        target = result_ref.at[:, pl.ds(pl.multiple_of((place ^ distance) * cells + start, width), width)]
+        moves.append((source, target))
+
+    for far, part in enumerate(firsts):
+        for near in range(INNER):
+            add(part.at[pl.ds(near * rows, rows), pl.ds(0, width)], far * INNER + near, 0)
+    for near, part in enumerate(seconds):
+        for far in range(len(firsts)):
+            add(part.at[pl.ds(far * rows, rows), :], far * INNER + near, width)
+    place_moves(moves, sems)
+
+
+def place_last_kernel(cells, last_ref, _, result_ref, sems):
+    rows = result_ref.shape[0]
+    size = last_ref.shape[1]
+    moves = []
+    for device in range(last_ref.shape[0] // rows):
+        target = result_ref.at[:, pl.ds((device + 1) * cells - size, size)]
+        moves.append((last_ref.at[pl.ds(device * rows, rows), :], target))
+    place_moves(moves, sems)
+
+
+def join_kernel(rows, *refs):
+    near, refs = refs[:INNER], refs[INNER:]
+    given, made = refs[: len(refs) // 2], refs[len(refs) // 2 :]
+    width = near[0].shape[1]
+    for far, (source, target) in enumerate(zip(given, made)):
+        for i, part in enumerate(near):
+            target[i * rows : (i + 1) * rows, :width] = part[far * rows : (far + 1) * rows, :]
+        target[:, width:] = source[...]
+
+
+def reordered(ref, devices, near_first):
     place = lax.axis_index("state")
     rows = ref.shape[0] // devices
-    starts = [pl.multiple_of((place ^ distance) * rows, rows) for distance in range(devices)]
+    order = list(range(devices))
+    if near_first:
+        order.sort(key=lambda distance: (distance % INNER, distance // INNER))
+    starts = [pl.multiple_of((place ^ distance) * rows, rows) for distance in order]
     return jnp.concatenate([ref[pl.ds(start, rows), :] for start in starts], axis=0)
 
 
@@ -344,11 +378,10 @@
     return blocks
 
 
-def head_kernel(devices, fields_ref, here_ref, there_ref, terms_ref, *results):
-    span = PARTITION_SPAN
-    first = pl.program_id(0) * QUAD
-    fields, here, there = [reordered(ref, devices) for ref in (fields_ref, here_ref, there_ref)]
-    for spot, result in enumerate(updated(blocks_of(fields, here, there, first, terms_ref))):
+def head_kernel(quad, devices, fields_ref, here_ref, there_ref, terms_ref, *results):
+    span = PARTITION_SPAN
+    fields, here, there = [reordered(ref, devices, quad == 0) for ref in (fields_ref, here_ref, there_ref)]
+    for spot, result in enumerate(updated(blocks_of(fields, here, there, quad * QUAD, terms_ref))):
         start = 0
         for result_ref in results:
             rows = result_ref.shape[0]
@@ -429,14 +462,16 @@
 
     split = early * width + half
     sent = call(
-        functools.partial(first_part_kernel, split),
-        [anywhere, vmem],
+        first_part_kernel,
+        [anywhere, anywhere],
         jax.ShapeDtypeStruct((devices, own_members, split + lanes), jnp.float32),
         grant=56,
         out_specs=anywhere,
         scratch_shapes=[
-            pltpu.VMEM((devices, own_members, cells + lanes), jnp.float32),
-            pltpu.SemaphoreType.DMA((2 * devices,)),
+            pltpu.VMEM((devices, own_members, split + lanes), jnp.float32),
+            pltpu.VMEM((devices, own_members, 2 * half), jnp.float32),
+            pltpu.VMEM(observations[2].shape[::-1], jnp.int32),
+            pltpu.SemaphoreType.DMA((3 * devices + outer + 1,)),
         ],
     )(fields, observations[2].T)
     first = exchanged(sent).reshape(members, split + lanes)
@@ -453,21 +488,28 @@
         out_specs=vmem,
     )(first, quad_position)
 
-    groups = call(
-        functools.partial(head_kernel, devices),
-        [
-            pl.BlockSpec((members, width), lambda step: (0, step)),
-            pl.BlockSpec((members, lanes), lambda step: (0, step)),
-            pl.BlockSpec((members, lanes), lambda step: (0, step + 1)),
-            full(terms),
-        ],
-        [group(outer, early * width)] * outer,
-        grant=40,
-        grid=(early,),
-        out_specs=[pl.BlockSpec((members // outer, width), lambda step: (0, step))] * outer,
-    )(first, seen, seen, terms)
-    groups, second = lax.optimization_barrier((groups, second))
-    beyond = swapped(groups, INNER)
+    def head(quad, parts, seen):
+        return call(
+            functools.partial(head_kernel, quad, devices),
+            [columns(width, quad), columns(lanes, quad), columns(lanes, quad + 1), full(terms)],
+            [group(parts, width)] * parts,
+            grant=40,
+            grid=(1,),
+            out_specs=[pl.BlockSpec((members // parts, width), lambda step: (0, 0))] * parts,
+        )(first, seen, seen, terms)
+
+    groups = head(0, INNER, seen)
+    seen, groups, second[1] = lax.optimization_barrier((seen, groups, second[1]))
+    near = swapped(groups, 1)
+    groups = head(1, outer, seen)
+    away = call(
+        functools.partial(join_kernel, own_members),
+        [vmem] * (INNER + outer),
+        [group(outer, 2 * width)] * outer,
+        out_specs=[vmem] * outer,
+    )(*near, *groups)
+    away, second = lax.optimization_barrier((away, second))
+    away = swapped(away, INNER)
 
     second, tiles = call(
         functools.partial(second_kernel, devices),
@@ -496,14 +538,30 @@
     )(first, second, second, seen, tiles, terms)
     ends = exchanged(ends.reshape(devices, own_members, late * width)).reshape(members, late * width)
 
-    near = turned(beyond, INNER, cost=1 << 36)
-    return call(
+    near = call(
+        functools.partial(turn_kernel, own_members),
+        [pl.BlockSpec((members // outer, width), lambda step: (0, 1))] * outer,
+        [group(INNER, width)] * INNER,
+        cost=1 << 36,
+        grid=(1,),
+        out_specs=[pl.BlockSpec((members // INNER, width), lambda step: (0, 0))] * INNER,
+    )(*away)
+    whole = jax.ShapeDtypeStruct((own_members, all_cells), jnp.float32)
+    result = call(
         functools.partial(place_kernel, cells),
-        [vmem] * (INNER + 1),
-        jax.ShapeDtypeStruct((own_members, all_cells), jnp.float32),
+        [vmem] * (outer + INNER),
+        whole,
         out_specs=anywhere,
         scratch_shapes=[pltpu.SemaphoreType.DMA((2 * devices,))],
-    )(*swapped(near, 1), ends)
+    )(*away, *swapped(near, 1))
+    return call(
+        functools.partial(place_last_kernel, cells),
+        [vmem, anywhere],
+        whole,
+        input_output_aliases={1: 0},
+        out_specs=anywhere,
+        scratch_shapes=[pltpu.SemaphoreType.DMA((devices,))],
+    )(ends, result)
 
 
 def by_all_to_all(fields, observations, devices):

time: 113 us -> 112 us (level)
  waiting for transfers between devices: 38.1 us -> 35.5 us
    ppermute x12 -> x15, waiting for transfers between devices: 38.1 us -> 30.1 us  [swapped(): lax.ppermute(arrays[k], 'state', pairs[k])]
    all_to_all x2, waiting for transfers between devices: 0.01 us -> 5.33 us  [exchanged(): lax.all_to_all(array, 'state', split_axis=0, concat_axis=0, tiled=True)]
    pallas_call x3 -> x7, Pallas kernels: 16.9 us -> 17.7 us  [the longest x2 11.4 us: head(): call(functools.partial(head_kernel, quad, devices), [columns(width, quad)...]
    ppermute x12 -> x15, starting transfers between devices: 16.3 us -> 16.3 us  [swapped(): lax.ppermute(arrays[k], 'state', pairs[k])]
  transfers between devices with their start and end apart: 14 -> 17, of which waited for: 5 -> 6; matrix products, arithmetic and copies ran while one was open for 5% -> 5% of each run, Pallas kernels for 27% -> 29%
where the time goes in v6:
time: 112 us; the launch traced here: 110 us
  Pallas kernels  35.8 us (32%)
  waiting for transfers between devices  35.5 us (32%)
  starting transfers between devices  28.6 us (26%)
  local copies, waits for them, and re-layouts  9.91 us (9%)
    ppermute x15, waiting for transfers between devices, swapped(): lax.ppermute(arrays[k], 'state', pairs[k])  30.1 us
    ppermute x15, starting transfers between devices, swapped(): lax.ppermute(arrays[k], 'state', pairs[k])  16.3 us
    pallas_call x1, Pallas kernels, in_stages(): call(tail_kernel, [columns(half, split // half - 1), columns(half, 1), pl...  13.2 us
    all_to_all x2, starting transfers between devices, exchanged(): lax.all_to_all(array, 'state', split_axis=0, concat_axis=0, tiled=True)  12.2 us
    pallas_call x2, Pallas kernels, head(): call(functools.partial(head_kernel, quad, devices), [columns(width, quad)...  11.4 us
    unnamed x25, local copies, waits for them, and re-layouts  6.97 us
    all_to_all x2, waiting for transfers between devices, exchanged(): lax.all_to_all(array, 'state', split_axis=0, concat_axis=0, tiled=True)  5.33 us
    pallas_call x1, Pallas kernels, in_stages(): call(first_part_kernel, [anywhere, anywhere], jax.ShapeDtypeStruct((devic...  3.13 us
  transfers between devices with their start and end apart: 17, of which 6 were waited for; matrix products, arithmetic and copies ran while one was open for 5% of the time, Pallas kernels for 29%

profile of v6, /device:TPU:0, one launch (start us, length us, event | category | flops | bytes accessed | tf_op | source)
XLA Modules:
  0.0 110.1 jit_solution(15982080236568194906)
XLA Ops:
  0.0 3.1 %shard_map.64 = f32[16,16,1408]{2,1,0:T(8,128)} custom-call(f32[16,32768]{1,0:T(8,128)} %fields_ref.3, s32[32,256]{1,0:T(8,128)} %bitcast.11), custom_call_target="tpu_custom_call" | custom-call | flops 1 | bytes 1 | tf_op jit(solution)/shard_map/pallas_call | solution.py:464
  3.1 0.0 copy-start.2
  3.2 0.0 copy-start.10
  3.2 7.5 %all-to-all-start = ((f32[16,16,1408]{2,1,0:T(8,128)}), f32[16,16,1408]{2,1,0:T(8,128)S(1)}, u32[]{:S(2)}, u32[]{:S(2)}) async-start(f32[16,16,1408]{2,1,0:T(8,128)} %shard_map.64), calls=%async_computation | async-start | bytes 2883584 | tf_op jit(solution)/shard_map/all_to_all | solution.py:461
  10.7 1.5 %shard_map.65 = (f32[64,768]{1,0:T(8,128)S(1)}, f32[64,768]{1,0:T(8,128)}, f32[64,768]{1,0:T(8,128)}, f32[64,768]{1,0:T(8,128)}) custom-call(f32[16,32768]{1,0:T(8,128)S(1)} %copy-done.2), custom_call_target="tpu_custom_call" | custom-call | flops 1 | bytes 1 | tf_op jit(solution)/shard_map/pallas_call | solution.py:443
  12.3 0.7 copy-done.6
  12.9 0.4 collective-permute-start
  13.3 1.7 %collective-permute-start.1 = (f32[64,768]{1,0:T(8,128)}, f32[64,768]{1,0:T(8,128)S(1)}, u32[]{:S(2)}, u32[]{:S(2)}) collective-permute-start(f32[64,768]{1,0:T(8,128)} %get-tuple-element.61), channel_id=1, source_target_pairs={{0,2},{1,3},{2,0},{3,1},{4,6},{5,7},{6,4},{7,5},{8,10},{9,11},{10,... | collective-permute-start | bytes 589832 | tf_op jit(solution)/shard_map/ppermute | solution.py:440
  15.0 0.9 copy.14
  15.9 0.7 copy.15.adjacent_ref
  16.5 0.9 copy.13
  17.4 0.7 reshape.20.precision_ref
  18.1 0.7 reshape.21.position_ref
  18.8 11.1 %collective-permute-done.1.refs_2_ = f32[64,768]{1,0:T(8,128)S(1)} collective-permute-done((f32[64,768]{1,0:T(8,128)}, f32[64,768]{1,0:T(8,128)S(1)}, u32[]{:S(2)}, u32[]{:S(2)}) %collective-permute-start.1) | collective-permute-done | bytes 196640 | tf_op jit(solution)/shard_map/ppermute | solution.py:440
  29.9 3.9 %collective-permute-done.2.refs_3_ = f32[64,768]{1,0:T(8,128)S(1)} collective-permute-done((f32[64,768]{1,0:T(8,128)}, f32[64,768]{1,0:T(8,128)S(1)}, u32[]{:S(2)}, u32[]{:S(2)}) %collective-permute-start.2) | collective-permute-done | bytes 196640 | tf_op jit(solution)/shard_map/ppermute | solution.py:440
  33.9 0.9 copy-done.7
  34.8 0.8 shard_map.66
  35.6 0.9 copy.12
  36.4 0.7 reshape.19.reading_ref
  37.1 1.8 %shard_map.67 = (f32[2,16,256]{2,1,0:T(8,128)}, s32[4,128]{1,0:T(4,128)}) custom-call(f32[64,128]{1,0:T(8,128)} %reshape.19.reading_ref, f32[64,128]{1,0:T(8,128)} %reshape.20.precision_ref, s32[64,128]{1,0:T(8,128)} %reshape.21.position_ref, s32[256]{0:T(256)} %tally_ref, s32[16,5]{1,0:T(8,128)} %copy.15.adjacent_ref), custom_call_target="tpu_custom_call" | custom-call | tf_op jit(solution)/shard_map/pallas_call | solution.py:225
  38.9 0.1 collective-permute-start.3
  39.0 5.2 %collective-permute-start.7 = (f32[64,768]{1,0:T(8,128)}, f32[64,768]{1,0:T(8,128)S(1)}, u32[]{:S(2)}, u32[]{:S(2)}) collective-permute-start(f32[64,768]{1,0:T(8,128)} %get-tuple-element.97), channel_id=1, source_target_pairs={{0,8},{1,9},{2,10},{3,11},{4,12},{5,13},{6,14},{7,15},{8,0},{9,1},... | collective-permute-start | bytes 589832 | tf_op jit(solution)/shard_map/ppermute | solution.py:440
  44.2 0.0 collective-permute-start.8
  44.2 0.6 copy-done.8
  44.8 0.4 shard_map.68.here_ref.there_ref
  45.3 0.7 copy-done.4
  46.0 5.6 %shard_map.69 = (f32[64,512]{1,0:T(8,128)S(1)}, f32[64,512]{1,0:T(8,128)S(1)}, f32[64,512]{1,0:T(8,128)S(1)}, f32[64,512]{1,0:T(8,128)S(1)}) custom-call(f32[256,1408]{1,0:T(8,128)S(1)} %bitcast.5, f32[256,384]{1,0:T(8,128)S(1)} %shard_map.68.here_ref.there_ref, f32[256,384]{1,0:T(8,128)S(1)} %shard_map.68.here_ref.there_ref, f32[2,16,256]{2,1,0:T(8,128)S(1)} %copy-done.4), custom_call_target="tpu_custom_call" | custom-call | flops 1 | bytes 1 | tf_op jit(solution)/shard_map/pallas_call | solution.py:492
  51.6 0.1 collective-permute-start.4
  51.7 1.0 collective-permute-start.5
  52.7 0.8 collective-permute-start.6
  53.6 5.8 %shard_map.70 = (f32[64,512]{1,0:T(8,128)S(1)}, f32[64,512]{1,0:T(8,128)S(1)}, f32[64,512]{1,0:T(8,128)S(1)}, f32[64,512]{1,0:T(8,128)S(1)}) custom-call(f32[256,1408]{1,0:T(8,128)S(1)} %bitcast.6, f32[256,384]{1,0:T(8,128)S(1)} %shard_map.68.here_ref.there_ref, f32[256,384]{1,0:T(8,128)S(1)} %shard_map.68.here_ref.there_ref, f32[2,16,256]{2,1,0:T(8,128)S(1)} %copy-done.4), custom_call_target="tpu_custom_call" | custom-call | flops 1 | bytes 1 | tf_op jit(solution)/shard_map/pallas_call | solution.py:492
  59.4 0.6 collective-permute-done.6.refs_3_
  60.0 0.9 shard_map.71
  60.8 2.3 %collective-permute-start.9 = (f32[64,1024]{1,0:T(8,128)}, f32[64,1024]{1,0:T(8,128)S(1)}, u32[]{:S(2)}, u32[]{:S(2)}) collective-permute-start(f32[64,1024]{1,0:T(8,128)} %get-tuple-element.106), channel_id=1, source_target_pairs={{0,4},{1,5},{2,6},{3,7},{4,0},{5,1},{6,2},{7,3},{8,12},{9,13},{10,... | collective-permute-start | bytes 786440 | tf_op jit(solution)/shard_map/ppermute | solution.py:440
  63.1 2.1 %collective-permute-start.10 = (f32[64,1024]{1,0:T(8,128)}, f32[64,1024]{1,0:T(8,128)S(1)}, u32[]{:S(2)}, u32[]{:S(2)}) collective-permute-start(f32[64,1024]{1,0:T(8,128)} %get-tuple-element.107), channel_id=1, source_target_pairs={{0,8},{1,9},{2,10},{3,11},{4,12},{5,13},{6,14},{7,15},{8,0},{9,1},... | collective-permute-start | bytes 786440 | tf_op jit(solution)/shard_map/ppermute | solution.py:440
  65.2 0.5 collective-permute-start.11
  65.7 0.3 shard_map.72
  66.1 0.9 copy-done.3
  67.0 0.7 copy-done.5
  67.7 13.2 %shard_map.73 = f32[256,1024]{1,0:T(8,128)} custom-call(f32[256,1408]{1,0:T(8,128)} %bitcast.8, f32[256,768]{1,0:T(8,128)} %copy-done.3, f32[256,768]{1,0:T(8,128)} %copy-done.3, f32[256,384]{1,0:T(8,128)} %copy-done.1, f32[256,256]{1,0:T(8,128)} %copy-done.5, f32[2,16,256]{2,1,0:T(8,128)} %get-tuple-element.76.terms_ref), custom_call_target="tpu_custom_call" | custom-call | flops 1 | bytes 1 | tf_op jit(solution)/shard_map/pallas_call | solution.py:524
  80.9 4.7 %all-to-all-start.1 = ((f32[16,16,1024]{2,1,0:T(8,128)}), f32[16,16,1024]{2,1,0:T(8,128)S(1)}, u32[]{:S(2)}, u32[]{:S(2)}) async-start(f32[16,16,1024]{2,1,0:T(8,128)} %bitcast.10), calls=%async_computation.1 | async-start | bytes 2097152 | tf_op jit(solution)/shard_map/all_to_all | solution.py:461
  85.7 0.5 collective-permute-start.12
  86.1 1.7 %collective-permute-start.13 = (f32[64,512]{1,0:T(8,128)S(1)}, f32[64,512]{1,0:T(8,128)S(1)}, u32[]{:S(2)}, u32[]{:S(2)}) collective-permute-start(f32[64,512]{1,0:T(8,128)S(1)} %get-tuple-element.111), channel_id=1, source_target_pairs={{0,2},{1,3},{2,0},{3,1},{4,6},{5,7},{6,4},{7,5},{8,10},{9,11},{10,... | collective-permute-start | bytes 393224 | tf_op jit(solution)/shard_map/ppermute | solution.py:440
  87.8 12.5 %collective-permute-done.13.refs_6_ = f32[64,512]{1,0:T(8,128)S(1)} collective-permute-done((f32[64,512]{1,0:T(8,128)S(1)}, f32[64,512]{1,0:T(8,128)S(1)}, u32[]{:S(2)}, u32[]{:S(2)}) %collective-permute-start.13) | collective-permute-done | bytes 131104 | tf_op jit(solution)/shard_map/ppermute | solution.py:440
  100.3 2.0 %collective-permute-done.14.refs_7_ = f32[64,512]{1,0:T(8,128)S(1)} collective-permute-done((f32[64,512]{1,0:T(8,128)S(1)}, f32[64,512]{1,0:T(8,128)S(1)}, u32[]{:S(2)}, u32[]{:S(2)}) %collective-permute-start.14) | collective-permute-done | bytes 131104 | tf_op jit(solution)/shard_map/ppermute | solution.py:440
  102.3 1.2 %shard_map.75._ = f32[16,32768]{1,0:T(8,128)} custom-call(f32[64,1024]{1,0:T(8,128)S(1)} %get-tuple-element.105.refs_0_, f32[64,1024]{1,0:T(8,128)S(1)} %collective-permute-done.9.refs_1_, f32[64,1024]{1,0:T(8,128)S(1)} %collective-permute-done.10.refs_2_, f32[64,1024]{1,0:T(8,128)S(1)} %collective-permute-done.11.refs_3_, ...), custom_call_target="tpu_custom_call" | custom-call | flops 1 | bytes 1 | tf_op jit(solution)/shard_map/pallas_call | solution.py:550
  103.5 5.3 %all-to-all-done.1 = f32[16,16,1024]{2,1,0:T(8,128)S(1)} async-done(((f32[16,16,1024]{2,1,0:T(8,128)}), f32[16,16,1024]{2,1,0:T(8,128)S(1)}, u32[]{:S(2)}, u32[]{:S(2)}) %all-to-all-start.1) | async-done | bytes 1048608 | tf_op jit(solution)/shard_map/all_to_all | solution.py:461
  108.9 1.1 shard_map.76
  (28 shorter events, 0.1 us)
Async XLA Ops:
  3.1 7.6 %copy-start.2 = (f32[16,32768]{1,0:T(8,128)S(1)}, f32[16,32768]{1,0:T(8,128)}, u32[]{:S(2)}) copy-start(f32[16,32768]{1,0:T(8,128)} %fields_ref.3) | copy-start | bytes 6291460
  3.2 12.7 %copy-start.10 = (s32[16,5]{0,1:T(8,128)S(1)}, s32[16,5]{0,1:T(8,128)}, u32[]{:S(2)}) copy-start(s32[16,5]{0,1:T(8,128)} %param.11) | copy-start | bytes 964
  3.2 41.0 %all-to-all-start = ((f32[16,16,1408]{2,1,0:T(8,128)}), f32[16,16,1408]{2,1,0:T(8,128)S(1)}, u32[]{:S(2)}, u32[]{:S(2)}) async-start(f32[16,16,1408]{2,1,0:T(8,128)} %shard_map.64), calls=%async_computation | async-start | bytes 2883584 | tf_op jit(solution)/shard_map/all_to_all | solution.py:461
  12.2 0.7 copy-start.6
  12.9 5.9 %collective-permute-start = (f32[64,768]{1,0:T(8,128)}, f32[64,768]{1,0:T(8,128)S(1)}, u32[]{:S(2)}, u32[]{:S(2)}) collective-permute-start(f32[64,768]{1,0:T(8,128)} %get-tuple-element.60), channel_id=1, source_target_pairs={{0,1},{1,0},{2,3},{3,2},{4,5},{5,4},{6,7},{7,6},{8,9},{9,8},{10,11... | collective-permute-start | bytes 589832 | tf_op jit(solution)/shard_map/ppermute | solution.py:440
  13.3 16.6 %collective-permute-start.1 = (f32[64,768]{1,0:T(8,128)}, f32[64,768]{1,0:T(8,128)S(1)}, u32[]{:S(2)}, u32[]{:S(2)}) collective-permute-start(f32[64,768]{1,0:T(8,128)} %get-tuple-element.61), channel_id=1, source_target_pairs={{0,2},{1,3},{2,0},{3,1},{4,6},{5,7},{6,4},{7,5},{8,10},{9,11},{10,... | collective-permute-start | bytes 589832 | tf_op jit(solution)/shard_map/ppermute | solution.py:440
  15.0 18.9 %collective-permute-start.2 = (f32[64,768]{1,0:T(8,128)}, f32[64,768]{1,0:T(8,128)S(1)}, u32[]{:S(2)}, u32[]{:S(2)}) collective-permute-start(f32[64,768]{1,0:T(8,128)} %get-tuple-element.62), channel_id=1, source_target_pairs={{0,3},{1,2},{2,1},{3,0},{4,7},{5,6},{6,5},{7,4},{8,11},{9,10},{10,... | collective-permute-start | bytes 589832 | tf_op jit(solution)/shard_map/ppermute | solution.py:440
  33.9 0.9 copy-start.7
  38.9 12.7 %collective-permute-start.3 = (f32[64,768]{1,0:T(8,128)S(1)}, f32[64,768]{1,0:T(8,128)S(1)}, u32[]{:S(2)}, u32[]{:S(2)}) collective-permute-start(f32[64,768]{1,0:T(8,128)S(1)} %get-tuple-element.81), channel_id=1, source_target_pairs={{0,4},{1,5},{2,6},{3,7},{4,0},{5,1},{6,2},{7,3},{8,12},{9,13},{10,... | collective-permute-start | bytes 589832 | tf_op jit(solution)/shard_map/ppermute | solution.py:440
  39.0 21.8 %collective-permute-start.7 = (f32[64,768]{1,0:T(8,128)}, f32[64,768]{1,0:T(8,128)S(1)}, u32[]{:S(2)}, u32[]{:S(2)}) collective-permute-start(f32[64,768]{1,0:T(8,128)} %get-tuple-element.97), channel_id=1, source_target_pairs={{0,8},{1,9},{2,10},{3,11},{4,12},{5,13},{6,14},{7,15},{8,0},{9,1},... | collective-permute-start | bytes 589832 | tf_op jit(solution)/shard_map/ppermute | solution.py:440
  44.2 16.7 %collective-permute-start.8 = (f32[64,768]{1,0:T(8,128)}, f32[64,768]{1,0:T(8,128)S(1)}, u32[]{:S(2)}, u32[]{:S(2)}) collective-permute-start(f32[64,768]{1,0:T(8,128)} %get-tuple-element.98), channel_id=1, source_target_pairs={{0,12},{1,13},{2,14},{3,15},{4,8},{5,9},{6,10},{7,11},{8,4},{9,5},... | collective-permute-start | bytes 589832 | tf_op jit(solution)/shard_map/ppermute | solution.py:440
  44.2 21.5 %copy-start = (f32[16,16,1408]{2,1,0:T(8,128)}, f32[16,16,1408]{2,1,0:T(8,128)S(1)}, u32[]{:S(2)}) copy-start(f32[16,16,1408]{2,1,0:T(8,128)S(1)} %all-to-all-done) | copy-start | bytes 4325380
  44.2 0.6 copy-start.8
  45.2 0.8 copy-start.4
  46.0 13.3 %copy-start.1 = (f32[256,384]{1,0:T(8,128)}, f32[256,384]{1,0:T(8,128)S(1)}, u32[]{:S(2)}) copy-start(f32[256,384]{1,0:T(8,128)S(1)} %shard_map.68.here_ref.there_ref) | copy-start | bytes 1179652
  51.6 14.1 %copy-start.9 = (s32[4,128]{1,0:T(4,128)S(1)}, s32[4,128]{1,0:T(4,128)}, u32[]{:S(2)}) copy-start(s32[4,128]{1,0:T(4,128)} %get-tuple-element.75.position_ref) | copy-start | bytes 6148
  51.6 7.7 %collective-permute-start.4 = (f32[64,512]{1,0:T(8,128)S(1)}, f32[64,512]{1,0:T(8,128)S(1)}, u32[]{:S(2)}, u32[]{:S(2)}) collective-permute-start(f32[64,512]{1,0:T(8,128)S(1)} %get-tuple-element.83), channel_id=1, source_target_pairs={{0,1},{1,0},{2,3},{3,2},{4,5},{5,4},{6,7},{7,6},{8,9},{9,8},{10,11... | collective-permute-start | bytes 393224 | tf_op jit(solution)/shard_map/ppermute | solution.py:440
  51.7 7.7 %collective-permute-start.5 = (f32[64,512]{1,0:T(8,128)S(1)}, f32[64,512]{1,0:T(8,128)S(1)}, u32[]{:S(2)}, u32[]{:S(2)}) collective-permute-start(f32[64,512]{1,0:T(8,128)S(1)} %get-tuple-element.84), channel_id=1, source_target_pairs={{0,2},{1,3},{2,0},{3,1},{4,6},{5,7},{6,4},{7,5},{8,10},{9,11},{10,... | collective-permute-start | bytes 393224 | tf_op jit(solution)/shard_map/ppermute | solution.py:440
  52.7 7.3 %collective-permute-start.6 = (f32[64,512]{1,0:T(8,128)S(1)}, f32[64,512]{1,0:T(8,128)S(1)}, u32[]{:S(2)}, u32[]{:S(2)}) collective-permute-start(f32[64,512]{1,0:T(8,128)S(1)} %get-tuple-element.85), channel_id=1, source_target_pairs={{0,3},{1,2},{2,1},{3,0},{4,7},{5,6},{6,5},{7,4},{8,11},{9,10},{10,... | collective-permute-start | bytes 393224 | tf_op jit(solution)/shard_map/ppermute | solution.py:440
  60.8 24.8 %collective-permute-start.9 = (f32[64,1024]{1,0:T(8,128)}, f32[64,1024]{1,0:T(8,128)S(1)}, u32[]{:S(2)}, u32[]{:S(2)}) collective-permute-start(f32[64,1024]{1,0:T(8,128)} %get-tuple-element.106), channel_id=1, source_target_pairs={{0,4},{1,5},{2,6},{3,7},{4,0},{5,1},{6,2},{7,3},{8,12},{9,13},{10,... | collective-permute-start | bytes 786440 | tf_op jit(solution)/shard_map/ppermute | solution.py:440
  63.1 22.5 %collective-permute-start.10 = (f32[64,1024]{1,0:T(8,128)}, f32[64,1024]{1,0:T(8,128)S(1)}, u32[]{:S(2)}, u32[]{:S(2)}) collective-permute-start(f32[64,1024]{1,0:T(8,128)} %get-tuple-element.107), channel_id=1, source_target_pairs={{0,8},{1,9},{2,10},{3,11},{4,12},{5,13},{6,14},{7,15},{8,0},{9,1},... | collective-permute-start | bytes 786440 | tf_op jit(solution)/shard_map/ppermute | solution.py:440
  65.2 20.4 %collective-permute-start.11 = (f32[64,1024]{1,0:T(8,128)S(1)}, f32[64,1024]{1,0:T(8,128)S(1)}, u32[]{:S(2)}, u32[]{:S(2)}) collective-permute-start(f32[64,1024]{1,0:T(8,128)S(1)} %get-tuple-element.108), channel_id=1, source_target_pairs={{0,12},{1,13},{2,14},{3,15},{4,8},{5,9},{6,10},{7,11},{8,4},{9,5},... | collective-permute-start | bytes 786440 | tf_op jit(solution)/shard_map/ppermute | solution.py:440
  66.1 0.9 copy-start.3
  67.0 0.7 copy-start.5
  80.9 28.0 %all-to-all-start.1 = ((f32[16,16,1024]{2,1,0:T(8,128)}), f32[16,16,1024]{2,1,0:T(8,128)S(1)}, u32[]{:S(2)}, u32[]{:S(2)}) async-start(f32[16,16,1024]{2,1,0:T(8,128)} %bitcast.10), calls=%async_computation.1 | async-start | bytes 2097152 | tf_op jit(solution)/shard_map/all_to_all | solution.py:461
  85.7 2.2 %collective-permute-start.12 = (f32[64,512]{1,0:T(8,128)S(1)}, f32[64,512]{1,0:T(8,128)S(1)}, u32[]{:S(2)}, u32[]{:S(2)}) collective-permute-start(f32[64,512]{1,0:T(8,128)S(1)} %get-tuple-element.110), channel_id=1, source_target_pairs={{0,1},{1,0},{2,3},{3,2},{4,5},{5,4},{6,7},{7,6},{8,9},{9,8},{10,11... | collective-permute-start | bytes 393224 | tf_op jit(solution)/shard_map/ppermute | solution.py:440
  86.1 14.2 %collective-permute-start.13 = (f32[64,512]{1,0:T(8,128)S(1)}, f32[64,512]{1,0:T(8,128)S(1)}, u32[]{:S(2)}, u32[]{:S(2)}) collective-permute-start(f32[64,512]{1,0:T(8,128)S(1)} %get-tuple-element.111), channel_id=1, source_target_pairs={{0,2},{1,3},{2,0},{3,1},{4,6},{5,7},{6,4},{7,5},{8,10},{9,11},{10,... | collective-permute-start | bytes 393224 | tf_op jit(solution)/shard_map/ppermute | solution.py:440
  87.8 14.5 %collective-permute-start.14 = (f32[64,512]{1,0:T(8,128)S(1)}, f32[64,512]{1,0:T(8,128)S(1)}, u32[]{:S(2)}, u32[]{:S(2)}) collective-permute-start(f32[64,512]{1,0:T(8,128)S(1)} %get-tuple-element.112), channel_id=1, source_target_pairs={{0,3},{1,2},{2,1},{3,0},{4,7},{5,6},{6,5},{7,4},{8,11},{9,10},{10,... | collective-permute-start | bytes 393224 | tf_op jit(solution)/shard_map/ppermute | solution.py:440

commit v7 on v6

--- a/solution.py
+++ b/solution.py
@@ -122,6 +122,7 @@
 
 def second_kernel(devices, beyond_ref, position_ref, *refs):
     *parts, fields_ref, seen_ref = refs
+    parts = parts[::-1]
     place = lax.axis_index("state")
     span = PARTITION_SPAN
     quads = position_ref.shape[0]
@@ -303,7 +304,7 @@
 
 
 def turn_kernel(rows, *refs):
-    given, made = refs[: len(refs) // 2], refs[len(refs) // 2 :]
+    given, made = refs[: len(refs) // 2][::-1], refs[len(refs) // 2 :]
     for i, source in enumerate(given):
         for j, target in enumerate(made):
             target[i * rows : (i + 1) * rows, :] = source[j * rows : (j + 1) * rows, :]
@@ -437,7 +438,8 @@
 
     def swapped(arrays, unit):
         pairs = [[(i, i ^ (unit * k)) for i in range(devices)] for k in range(len(arrays))]
-        return [arrays[0]] + [lax.ppermute(arrays[k], "state", pairs[k]) for k in range(1, len(arrays))]
+        far_first = [lax.ppermute(arrays[k], "state", pairs[k]) for k in reversed(range(1, len(arrays)))]
+        return [arrays[0]] + far_first[::-1]
 
     def second_parts():
         return call(
@@ -455,7 +457,7 @@
             [group(parts, arrays[0].shape[1])] * parts,
             cost=cost,
             out_specs=[vmem] * parts,
-        )(*arrays)
+        )(*arrays[::-1])
 
     def exchanged(array):
         return lax.all_to_all(array, "state", split_axis=0, concat_axis=0, tiled=True)
@@ -513,14 +515,14 @@
 
     second, tiles = call(
         functools.partial(second_kernel, devices),
-        [columns(lanes, split // lanes), *[full(array) for array in (quad_position, *second)]],
+        [columns(lanes, split // lanes), *[full(array) for array in (quad_position, *second[::-1])]],
         [
             jax.ShapeDtypeStruct((members, cells - split), jnp.float32),
             jax.ShapeDtypeStruct((members, 2 * lanes), jnp.float32),
         ],
         grid=(1,),
         out_specs=[columns(cells - split, 0), columns(2 * lanes, 0)],
-    )(first, quad_position, *second)
+    )(first, quad_position, *second[::-1])
     ends = call(
         tail_kernel,
         [
@@ -532,7 +534,7 @@
             full(terms),
         ],
         jax.ShapeDtypeStruct((members, late * width), jnp.float32),
-        grant=60,
+        grant=40,
         grid=(late,),
         out_specs=pl.BlockSpec((members, width), lambda step: (0, step)),
     )(first, second, second, seen, tiles, terms)
@@ -545,7 +547,7 @@
         cost=1 << 36,
         grid=(1,),
         out_specs=[pl.BlockSpec((members // INNER, width), lambda step: (0, 0))] * INNER,
-    )(*away)
+    )(*away[::-1])
     whole = jax.ShapeDtypeStruct((own_members, all_cells), jnp.float32)
     result = call(
         functools.partial(place_kernel, cells),

time: 112 us -> 112 us (level)
  waiting for transfers between devices: 35.5 us -> 38.1 us
  local copies, waits for them, and re-layouts: 9.91 us -> 8.36 us
    all_to_all x2, waiting for transfers between devices: 5.33 us -> 7.92 us  [exchanged(): lax.all_to_all(array, 'state', split_axis=0, concat_axis=0, tiled=True)]
    unnamed x25 -> x17, local copies, waits for them, and re-layouts: 6.97 us -> 5.42 us
  transfers between devices with their start and end apart: 17 -> 17, of which waited for: 6 -> 7; matrix products, arithmetic and copies ran while one was open for 5% -> 5% of each run, Pallas kernels for 29% -> 28%
where the time goes in v7:
time: 112 us; the launch traced here: 110 us
  waiting for transfers between devices  38.1 us (34%)
  Pallas kernels  34.7 us (31%)
  starting transfers between devices  28.8 us (26%)
  local copies, waits for them, and re-layouts  8.36 us (7%)
    ppermute x15, waiting for transfers between devices, swapped(): lax.ppermute(arrays[k], 'state', pairs[k])  30.1 us
    ppermute x15, starting transfers between devices, swapped(): lax.ppermute(arrays[k], 'state', pairs[k])  16.2 us
    all_to_all x2, starting transfers between devices, exchanged(): lax.all_to_all(array, 'state', split_axis=0, concat_axis=0, tiled=True)  12.7 us
    pallas_call x1, Pallas kernels, in_stages(): call(tail_kernel, [columns(half, split // half - 1), columns(half, 1), pl...  12.1 us
    pallas_call x2, Pallas kernels, head(): call(functools.partial(head_kernel, quad, devices), [columns(width, quad)...  11.4 us
    all_to_all x2, waiting for transfers between devices, exchanged(): lax.all_to_all(array, 'state', split_axis=0, concat_axis=0, tiled=True)  7.92 us
    unnamed x17, local copies, waits for them, and re-layouts  5.42 us
    pallas_call x1, Pallas kernels, in_stages(): call(first_part_kernel, [anywhere, anywhere], jax.ShapeDtypeStruct((devic...  3.13 us
  transfers between devices with their start and end apart: 17, of which 7 were waited for; matrix products, arithmetic and copies ran while one was open for 5% of the time, Pallas kernels for 28%

profile of v7, /device:TPU:0, one launch (start us, length us, event | category | flops | bytes accessed | tf_op | source)
XLA Modules:
  0.0 110.2 jit_solution(4707550912158469714)
XLA Ops:
  0.0 3.1 %shard_map.64 = f32[16,16,1408]{2,1,0:T(8,128)} custom-call(f32[16,32768]{1,0:T(8,128)} %fields_ref.3, s32[32,256]{1,0:T(8,128)} %bitcast.10), custom_call_target="tpu_custom_call" | custom-call | flops 1 | bytes 1 | tf_op jit(solution)/shard_map/pallas_call | solution.py:466
  3.1 0.0 copy-start
  3.2 0.0 copy-start.6
  3.2 7.5 %all-to-all-start = ((f32[16,16,1408]{2,1,0:T(8,128)}), f32[16,16,1408]{2,1,0:T(8,128)S(1)}, u32[]{:S(2)}, u32[]{:S(2)}) async-start(f32[16,16,1408]{2,1,0:T(8,128)} %shard_map.64), calls=%async_computation | async-start | bytes 2883584 | tf_op jit(solution)/shard_map/all_to_all | solution.py:463
  10.7 1.5 %shard_map.65 = (f32[64,768]{1,0:T(8,128)S(1)}, f32[64,768]{1,0:T(8,128)}, f32[64,768]{1,0:T(8,128)}, f32[64,768]{1,0:T(8,128)}) custom-call(f32[16,32768]{1,0:T(8,128)S(1)} %copy-done), custom_call_target="tpu_custom_call" | custom-call | flops 1 | bytes 1 | tf_op jit(solution)/shard_map/pallas_call | solution.py:445
  12.3 0.7 copy-done.2
  12.9 1.7 %collective-permute-start = (f32[64,768]{1,0:T(8,128)}, f32[64,768]{1,0:T(8,128)S(1)}, u32[]{:S(2)}, u32[]{:S(2)}) collective-permute-start(f32[64,768]{1,0:T(8,128)} %get-tuple-element.59), channel_id=1, source_target_pairs={{0,3},{1,2},{2,1},{3,0},{4,7},{5,6},{6,5},{7,4},{8,11},{9,10},{10,... | collective-permute-start | bytes 589832 | tf_op jit(solution)/shard_map/ppermute | solution.py:441
  14.6 0.4 collective-permute-start.1
  15.0 0.0 collective-permute-start.2
  15.0 0.9 copy.14
  15.9 0.7 copy.15.adjacent_ref
  16.5 0.9 copy.13
  17.4 0.7 reshape.20.precision_ref
  18.1 0.7 reshape.21.position_ref
  18.8 10.2 %collective-permute-done.refs_0_ = f32[64,768]{1,0:T(8,128)S(1)} collective-permute-done((f32[64,768]{1,0:T(8,128)}, f32[64,768]{1,0:T(8,128)S(1)}, u32[]{:S(2)}, u32[]{:S(2)}) %collective-permute-start) | collective-permute-done | bytes 196640 | tf_op jit(solution)/shard_map/ppermute | solution.py:441
  29.0 4.9 %collective-permute-done.1.refs_1_ = f32[64,768]{1,0:T(8,128)S(1)} collective-permute-done((f32[64,768]{1,0:T(8,128)}, f32[64,768]{1,0:T(8,128)S(1)}, u32[]{:S(2)}, u32[]{:S(2)}) %collective-permute-start.1) | collective-permute-done | bytes 196640 | tf_op jit(solution)/shard_map/ppermute | solution.py:441
  33.8 0.9 copy-done.3
  34.8 0.8 shard_map.66
  35.6 0.9 copy.12
  36.4 0.7 reshape.19.reading_ref
  37.1 1.8 %shard_map.67 = (f32[2,16,256]{2,1,0:T(8,128)}, s32[4,128]{1,0:T(4,128)}) custom-call(f32[64,128]{1,0:T(8,128)} %reshape.19.reading_ref, f32[64,128]{1,0:T(8,128)} %reshape.20.precision_ref, s32[64,128]{1,0:T(8,128)} %reshape.21.position_ref, s32[256]{0:T(256)} %tally_ref, s32[16,5]{1,0:T(8,128)} %copy.15.adjacent_ref), custom_call_target="tpu_custom_call" | custom-call | tf_op jit(solution)/shard_map/pallas_call | solution.py:226
  38.9 0.6 collective-permute-start.3
  39.5 5.1 %collective-permute-start.7 = (f32[64,768]{1,0:T(8,128)}, f32[64,768]{1,0:T(8,128)S(1)}, u32[]{:S(2)}, u32[]{:S(2)}) collective-permute-start(f32[64,768]{1,0:T(8,128)} %get-tuple-element.97), channel_id=1, source_target_pairs={{0,8},{1,9},{2,10},{3,11},{4,12},{5,13},{6,14},{7,15},{8,0},{9,1},... | collective-permute-start | bytes 589832 | tf_op jit(solution)/shard_map/ppermute | solution.py:441
  44.7 0.7 copy-done.4
  45.4 0.4 shard_map.68.here_ref.there_ref
  45.8 0.7 copy-done.1
  46.5 5.6 %shard_map.69 = (f32[64,512]{1,0:T(8,128)S(1)}, f32[64,512]{1,0:T(8,128)S(1)}, f32[64,512]{1,0:T(8,128)S(1)}, f32[64,512]{1,0:T(8,128)S(1)}) custom-call(f32[256,1408]{1,0:T(8,128)S(1)} %bitcast.5, f32[256,384]{1,0:T(8,128)S(1)} %shard_map.68.here_ref.there_ref, f32[256,384]{1,0:T(8,128)S(1)} %shard_map.68.here_ref.there_ref, f32[2,16,256]{2,1,0:T(8,128)S(1)} %copy-done.1), custom_call_target="tpu_custom_call" | custom-call | flops 1 | bytes 1 | tf_op jit(solution)/shard_map/pallas_call | solution.py:494
  52.1 0.1 collective-permute-start.4
  52.2 1.0 collective-permute-start.5
  53.2 0.9 collective-permute-start.6
  54.1 5.8 %shard_map.70 = (f32[64,512]{1,0:T(8,128)S(1)}, f32[64,512]{1,0:T(8,128)S(1)}, f32[64,512]{1,0:T(8,128)S(1)}, f32[64,512]{1,0:T(8,128)S(1)}) custom-call(f32[256,1408]{1,0:T(8,128)S(1)} %bitcast.6, f32[256,384]{1,0:T(8,128)S(1)} %shard_map.68.here_ref.there_ref, f32[256,384]{1,0:T(8,128)S(1)} %shard_map.68.here_ref.there_ref, f32[2,16,256]{2,1,0:T(8,128)S(1)} %copy-done.1), custom_call_target="tpu_custom_call" | custom-call | flops 1 | bytes 1 | tf_op jit(solution)/shard_map/pallas_call | solution.py:494
  59.9 0.6 collective-permute-done.6.refs_3_
  60.5 0.9 shard_map.71
  61.3 1.9 %collective-permute-start.9 = (f32[64,1024]{1,0:T(8,128)}, f32[64,1024]{1,0:T(8,128)S(1)}, u32[]{:S(2)}, u32[]{:S(2)}) collective-permute-start(f32[64,1024]{1,0:T(8,128)} %get-tuple-element.106), channel_id=1, source_target_pairs={{0,4},{1,5},{2,6},{3,7},{4,0},{5,1},{6,2},{7,3},{8,12},{9,13},{10,... | collective-permute-start | bytes 786440 | tf_op jit(solution)/shard_map/ppermute | solution.py:441
  63.2 2.5 %collective-permute-start.10 = (f32[64,1024]{1,0:T(8,128)}, f32[64,1024]{1,0:T(8,128)S(1)}, u32[]{:S(2)}, u32[]{:S(2)}) collective-permute-start(f32[64,1024]{1,0:T(8,128)} %get-tuple-element.107), channel_id=1, source_target_pairs={{0,8},{1,9},{2,10},{3,11},{4,12},{5,13},{6,14},{7,15},{8,0},{9,1},... | collective-permute-start | bytes 786440 | tf_op jit(solution)/shard_map/ppermute | solution.py:441
  65.7 0.1 collective-permute-start.11
  65.8 0.3 shard_map.72
  66.2 12.1 %shard_map.73 = f32[256,1024]{1,0:T(8,128)} custom-call(f32[256,1408]{1,0:T(8,128)S(1)} %bitcast.8, f32[256,768]{1,0:T(8,128)S(1)} %get-tuple-element.103.begin_ref.end_ref, f32[256,768]{1,0:T(8,128)S(1)} %get-tuple-element.103.begin_ref.end_ref, f32[256,384]{1,0:T(8,128)S(1)} %shard_map.68.here_ref.there_ref, f32[256,256]{1,0:T(8,128)S(1)} %get-tuple-element.104.tiles_ref, ...), custom_call_target="tpu_custom_call" | custom-call | flops 1 | bytes 1 | tf_op jit(solution)/shard_map/pallas_call | solution.py:526
  78.2 5.1 %all-to-all-start.1 = ((f32[16,16,1024]{2,1,0:T(8,128)}), f32[16,16,1024]{2,1,0:T(8,128)S(1)}, u32[]{:S(2)}, u32[]{:S(2)}) async-start(f32[16,16,1024]{2,1,0:T(8,128)} %bitcast.2), calls=%async_computation.1 | async-start | bytes 2097152 | tf_op jit(solution)/shard_map/all_to_all | solution.py:463
  83.4 1.4 %collective-permute-done.10.refs_1_.refs_2_ = f32[64,1024]{1,0:T(8,128)S(1)} collective-permute-done((f32[64,1024]{1,0:T(8,128)}, f32[64,1024]{1,0:T(8,128)S(1)}, u32[]{:S(2)}, u32[]{:S(2)}) %collective-permute-start.10) | collective-permute-done | bytes 262176 | tf_op jit(solution)/shard_map/ppermute | solution.py:441
  84.8 0.1 collective-permute-start.12
  84.9 1.5 %collective-permute-start.13 = (f32[64,512]{1,0:T(8,128)S(1)}, f32[64,512]{1,0:T(8,128)S(1)}, u32[]{:S(2)}, u32[]{:S(2)}) collective-permute-start(f32[64,512]{1,0:T(8,128)S(1)} %get-tuple-element.111), channel_id=1, source_target_pairs={{0,2},{1,3},{2,0},{3,1},{4,6},{5,7},{6,4},{7,5},{8,10},{9,11},{10,... | collective-permute-start | bytes 393224 | tf_op jit(solution)/shard_map/ppermute | solution.py:441
  86.4 0.4 collective-permute-start.14
  86.7 10.9 %collective-permute-done.13.refs_6_ = f32[64,512]{1,0:T(8,128)S(1)} collective-permute-done((f32[64,512]{1,0:T(8,128)S(1)}, f32[64,512]{1,0:T(8,128)S(1)}, u32[]{:S(2)}, u32[]{:S(2)}) %collective-permute-start.13) | collective-permute-done | bytes 131104 | tf_op jit(solution)/shard_map/ppermute | solution.py:441
  97.7 2.2 %collective-permute-done.14.refs_7_ = f32[64,512]{1,0:T(8,128)S(1)} collective-permute-done((f32[64,512]{1,0:T(8,128)S(1)}, f32[64,512]{1,0:T(8,128)S(1)}, u32[]{:S(2)}, u32[]{:S(2)}) %collective-permute-start.14) | collective-permute-done | bytes 131104 | tf_op jit(solution)/shard_map/ppermute | solution.py:441
  99.8 1.2 %shard_map.75._ = f32[16,32768]{1,0:T(8,128)} custom-call(f32[64,1024]{1,0:T(8,128)S(1)} %get-tuple-element.105.refs_3_.refs_0_, f32[64,1024]{1,0:T(8,128)S(1)} %collective-permute-done.9.refs_2_.refs_1_, f32[64,1024]{1,0:T(8,128)S(1)} %collective-permute-done.10.refs_1_.refs_2_, f32[64,1024]{1,0:T(8,128)S(1)} %collective-permute-done.11.refs_0_.refs_3_, ...), custom_call_target="tpu_custom_call" | custom-call | flops 1 | bytes 1 | tf_op jit(solution)/shard_map/pallas_call | solution.py:552
  101.1 7.9 %all-to-all-done.1 = f32[16,16,1024]{2,1,0:T(8,128)S(1)} async-done(((f32[16,16,1024]{2,1,0:T(8,128)}), f32[16,16,1024]{2,1,0:T(8,128)S(1)}, u32[]{:S(2)}, u32[]{:S(2)}) %all-to-all-start.1) | async-done | bytes 1048608 | tf_op jit(solution)/shard_map/all_to_all | solution.py:463
  109.0 1.1 shard_map.76
  (20 shorter events, 0.1 us)
Async XLA Ops:
  3.1 7.6 %copy-start = (f32[16,32768]{1,0:T(8,128)S(1)}, f32[16,32768]{1,0:T(8,128)}, u32[]{:S(2)}) copy-start(f32[16,32768]{1,0:T(8,128)} %fields_ref.3) | copy-start | bytes 6291460
  3.2 12.7 %copy-start.6 = (s32[16,5]{0,1:T(8,128)S(1)}, s32[16,5]{0,1:T(8,128)}, u32[]{:S(2)}) copy-start(s32[16,5]{0,1:T(8,128)} %param.11) | copy-start | bytes 964
  3.2 41.5 %all-to-all-start = ((f32[16,16,1408]{2,1,0:T(8,128)}), f32[16,16,1408]{2,1,0:T(8,128)S(1)}, u32[]{:S(2)}, u32[]{:S(2)}) async-start(f32[16,16,1408]{2,1,0:T(8,128)} %shard_map.64), calls=%async_computation | async-start | bytes 2883584 | tf_op jit(solution)/shard_map/all_to_all | solution.py:463
  12.3 0.7 copy-start.2
  12.9 16.0 %collective-permute-start = (f32[64,768]{1,0:T(8,128)}, f32[64,768]{1,0:T(8,128)S(1)}, u32[]{:S(2)}, u32[]{:S(2)}) collective-permute-start(f32[64,768]{1,0:T(8,128)} %get-tuple-element.59), channel_id=1, source_target_pairs={{0,3},{1,2},{2,1},{3,0},{4,7},{5,6},{6,5},{7,4},{8,11},{9,10},{10,... | collective-permute-start | bytes 589832 | tf_op jit(solution)/shard_map/ppermute | solution.py:441
  14.6 19.2 %collective-permute-start.1 = (f32[64,768]{1,0:T(8,128)}, f32[64,768]{1,0:T(8,128)S(1)}, u32[]{:S(2)}, u32[]{:S(2)}) collective-permute-start(f32[64,768]{1,0:T(8,128)} %get-tuple-element.60), channel_id=1, source_target_pairs={{0,2},{1,3},{2,0},{3,1},{4,6},{5,7},{6,4},{7,5},{8,10},{9,11},{10,... | collective-permute-start | bytes 589832 | tf_op jit(solution)/shard_map/ppermute | solution.py:441
  15.0 18.8 %collective-permute-start.2 = (f32[64,768]{1,0:T(8,128)}, f32[64,768]{1,0:T(8,128)S(1)}, u32[]{:S(2)}, u32[]{:S(2)}) collective-permute-start(f32[64,768]{1,0:T(8,128)} %get-tuple-element.61), channel_id=1, source_target_pairs={{0,1},{1,0},{2,3},{3,2},{4,5},{5,4},{6,7},{7,6},{8,9},{9,8},{10,11... | collective-permute-start | bytes 589832 | tf_op jit(solution)/shard_map/ppermute | solution.py:441
  33.8 0.9 copy-start.3
  38.9 13.2 %collective-permute-start.3 = (f32[64,768]{1,0:T(8,128)S(1)}, f32[64,768]{1,0:T(8,128)S(1)}, u32[]{:S(2)}, u32[]{:S(2)}) collective-permute-start(f32[64,768]{1,0:T(8,128)S(1)} %get-tuple-element.81), channel_id=1, source_target_pairs={{0,4},{1,5},{2,6},{3,7},{4,0},{5,1},{6,2},{7,3},{8,12},{9,13},{10,... | collective-permute-start | bytes 589832 | tf_op jit(solution)/shard_map/ppermute | solution.py:441
  39.5 21.8 %collective-permute-start.7 = (f32[64,768]{1,0:T(8,128)}, f32[64,768]{1,0:T(8,128)S(1)}, u32[]{:S(2)}, u32[]{:S(2)}) collective-permute-start(f32[64,768]{1,0:T(8,128)} %get-tuple-element.97), channel_id=1, source_target_pairs={{0,8},{1,9},{2,10},{3,11},{4,12},{5,13},{6,14},{7,15},{8,0},{9,1},... | collective-permute-start | bytes 589832 | tf_op jit(solution)/shard_map/ppermute | solution.py:441
  44.7 16.7 %collective-permute-start.8 = (f32[64,768]{1,0:T(8,128)}, f32[64,768]{1,0:T(8,128)S(1)}, u32[]{:S(2)}, u32[]{:S(2)}) collective-permute-start(f32[64,768]{1,0:T(8,128)} %get-tuple-element.98), channel_id=1, source_target_pairs={{0,12},{1,13},{2,14},{3,15},{4,8},{5,9},{6,10},{7,11},{8,4},{9,5},... | collective-permute-start | bytes 589832 | tf_op jit(solution)/shard_map/ppermute | solution.py:441
  44.7 0.7 copy-start.4
  45.8 0.8 copy-start.1
  52.1 13.7 %copy-start.5 = (s32[4,128]{1,0:T(4,128)S(1)}, s32[4,128]{1,0:T(4,128)}, u32[]{:S(2)}) copy-start(s32[4,128]{1,0:T(4,128)} %get-tuple-element.75.position_ref) | copy-start | bytes 6148
  52.1 7.7 %collective-permute-start.4 = (f32[64,512]{1,0:T(8,128)S(1)}, f32[64,512]{1,0:T(8,128)S(1)}, u32[]{:S(2)}, u32[]{:S(2)}) collective-permute-start(f32[64,512]{1,0:T(8,128)S(1)} %get-tuple-element.83), channel_id=1, source_target_pairs={{0,1},{1,0},{2,3},{3,2},{4,5},{5,4},{6,7},{7,6},{8,9},{9,8},{10,11... | collective-permute-start | bytes 393224 | tf_op jit(solution)/shard_map/ppermute | solution.py:441
  52.2 7.7 %collective-permute-start.5 = (f32[64,512]{1,0:T(8,128)S(1)}, f32[64,512]{1,0:T(8,128)S(1)}, u32[]{:S(2)}, u32[]{:S(2)}) collective-permute-start(f32[64,512]{1,0:T(8,128)S(1)} %get-tuple-element.84), channel_id=1, source_target_pairs={{0,2},{1,3},{2,0},{3,1},{4,6},{5,7},{6,4},{7,5},{8,10},{9,11},{10,... | collective-permute-start | bytes 393224 | tf_op jit(solution)/shard_map/ppermute | solution.py:441
  53.2 7.3 %collective-permute-start.6 = (f32[64,512]{1,0:T(8,128)S(1)}, f32[64,512]{1,0:T(8,128)S(1)}, u32[]{:S(2)}, u32[]{:S(2)}) collective-permute-start(f32[64,512]{1,0:T(8,128)S(1)} %get-tuple-element.85), channel_id=1, source_target_pairs={{0,3},{1,2},{2,1},{3,0},{4,7},{5,6},{6,5},{7,4},{8,11},{9,10},{10,... | collective-permute-start | bytes 393224 | tf_op jit(solution)/shard_map/ppermute | solution.py:441
  61.3 22.1 %collective-permute-start.9 = (f32[64,1024]{1,0:T(8,128)}, f32[64,1024]{1,0:T(8,128)S(1)}, u32[]{:S(2)}, u32[]{:S(2)}) collective-permute-start(f32[64,1024]{1,0:T(8,128)} %get-tuple-element.106), channel_id=1, source_target_pairs={{0,4},{1,5},{2,6},{3,7},{4,0},{5,1},{6,2},{7,3},{8,12},{9,13},{10,... | collective-permute-start | bytes 786440 | tf_op jit(solution)/shard_map/ppermute | solution.py:441
  63.2 21.5 %collective-permute-start.10 = (f32[64,1024]{1,0:T(8,128)}, f32[64,1024]{1,0:T(8,128)S(1)}, u32[]{:S(2)}, u32[]{:S(2)}) collective-permute-start(f32[64,1024]{1,0:T(8,128)} %get-tuple-element.107), channel_id=1, source_target_pairs={{0,8},{1,9},{2,10},{3,11},{4,12},{5,13},{6,14},{7,15},{8,0},{9,1},... | collective-permute-start | bytes 786440 | tf_op jit(solution)/shard_map/ppermute | solution.py:441
  65.7 19.0 %collective-permute-start.11 = (f32[64,1024]{1,0:T(8,128)S(1)}, f32[64,1024]{1,0:T(8,128)S(1)}, u32[]{:S(2)}, u32[]{:S(2)}) collective-permute-start(f32[64,1024]{1,0:T(8,128)S(1)} %get-tuple-element.108), channel_id=1, source_target_pairs={{0,12},{1,13},{2,14},{3,15},{4,8},{5,9},{6,10},{7,11},{8,4},{9,5},... | collective-permute-start | bytes 786440 | tf_op jit(solution)/shard_map/ppermute | solution.py:441
  78.2 30.8 %all-to-all-start.1 = ((f32[16,16,1024]{2,1,0:T(8,128)}), f32[16,16,1024]{2,1,0:T(8,128)S(1)}, u32[]{:S(2)}, u32[]{:S(2)}) async-start(f32[16,16,1024]{2,1,0:T(8,128)} %bitcast.2), calls=%async_computation.1 | async-start | bytes 2097152 | tf_op jit(solution)/shard_map/all_to_all | solution.py:463
  84.8 1.9 %collective-permute-start.12 = (f32[64,512]{1,0:T(8,128)S(1)}, f32[64,512]{1,0:T(8,128)S(1)}, u32[]{:S(2)}, u32[]{:S(2)}) collective-permute-start(f32[64,512]{1,0:T(8,128)S(1)} %get-tuple-element.110), channel_id=1, source_target_pairs={{0,1},{1,0},{2,3},{3,2},{4,5},{5,4},{6,7},{7,6},{8,9},{9,8},{10,11... | collective-permute-start | bytes 393224 | tf_op jit(solution)/shard_map/ppermute | solution.py:441
  84.9 12.8 %collective-permute-start.13 = (f32[64,512]{1,0:T(8,128)S(1)}, f32[64,512]{1,0:T(8,128)S(1)}, u32[]{:S(2)}, u32[]{:S(2)}) collective-permute-start(f32[64,512]{1,0:T(8,128)S(1)} %get-tuple-element.111), channel_id=1, source_target_pairs={{0,2},{1,3},{2,0},{3,1},{4,6},{5,7},{6,4},{7,5},{8,10},{9,11},{10,... | collective-permute-start | bytes 393224 | tf_op jit(solution)/shard_map/ppermute | solution.py:441
  86.4 13.5 %collective-permute-start.14 = (f32[64,512]{1,0:T(8,128)S(1)}, f32[64,512]{1,0:T(8,128)S(1)}, u32[]{:S(2)}, u32[]{:S(2)}) collective-permute-start(f32[64,512]{1,0:T(8,128)S(1)} %get-tuple-element.112), channel_id=1, source_target_pairs={{0,3},{1,2},{2,1},{3,0},{4,7},{5,6},{6,5},{7,4},{8,11},{9,10},{10,... | collective-permute-start | bytes 393224 | tf_op jit(solution)/shard_map/ppermute | solution.py:441

commit v8 on v7

--- a/solution.py
+++ b/solution.py
@@ -250,9 +250,9 @@
         source = fields_ref.at[:, pl.ds(start, length)]
         copies.append(pltpu.make_async_copy(source, target, sems.at[len(copies)]))
 
-    for device in range(devices):
-        add((device + 1) * cells - half, half, edges_ref.at[device, :, pl.ds(0, half)])
-        add(device * cells, half, edges_ref.at[device, :, pl.ds(half, half)])
+    for border in range(devices + 1):
+        start = min(max(border * cells - half, 0), devices * cells - 2 * half)
+        add(start, 2 * half, edges_ref.at[border])
     copies.append(pltpu.make_async_copy(given_ref, position_ref, sems.at[len(copies)]))
     ahead = len(copies)
     for device in range(devices):
@@ -270,10 +270,11 @@
     positions = position_ref[...].T.reshape(devices, amount, OB)
     position = jnp.concatenate([shifted(positions[:, block], distance) for block, distance in beyond], axis=1)
     position = jnp.broadcast_to(position[:, None], (devices, rows, span)).reshape(devices * rows, span)
-    fields = [
-        shifted(edges_ref[:, :, spot * span : (spot + 1) * span].reshape(devices * rows, span), distance * rows)
-        for spot, (_, distance) in enumerate(beyond)
-    ]
+    fields = []
+    for spot, (_, distance) in enumerate(beyond):
+        first = 0 if distance > 0 else 1
+        found = edges_ref[first : first + devices, :, spot * span : (spot + 1) * span]
+        fields.append(found.reshape(devices * rows, span))
     held_ref[:, :, split:] = picked(fields, position).reshape(devices, rows, span)
     out = []
     for device, copy in enumerate(copies[ahead:]):
@@ -471,7 +472,7 @@
         out_specs=anywhere,
         scratch_shapes=[
             pltpu.VMEM((devices, own_members, split + lanes), jnp.float32),
-            pltpu.VMEM((devices, own_members, 2 * half), jnp.float32),
+            pltpu.VMEM((devices + 1, own_members, 2 * half), jnp.float32),
             pltpu.VMEM(observations[2].shape[::-1], jnp.int32),
             pltpu.SemaphoreType.DMA((3 * devices + outer + 1,)),
         ],

time: 112 us -> 112 us (level)
  no operation moved by 1% of the time
where the time goes in v8:
time: 112 us; the launch traced here: 110 us
  waiting for transfers between devices  38 us (34%)
  Pallas kernels  34.7 us (31%)
  starting transfers between devices  28.8 us (26%)
  local copies, waits for them, and re-layouts  8.36 us (7%)
    ppermute x15, waiting for transfers between devices, swapped(): lax.ppermute(arrays[k], 'state', pairs[k])  30.1 us
    ppermute x15, starting transfers between devices, swapped(): lax.ppermute(arrays[k], 'state', pairs[k])  16.2 us
    all_to_all x2, starting transfers between devices, exchanged(): lax.all_to_all(array, 'state', split_axis=0, concat_axis=0, tiled=True)  12.7 us
    pallas_call x1, Pallas kernels, in_stages(): call(tail_kernel, [columns(half, split // half - 1), columns(half, 1), pl...  12.1 us
    pallas_call x2, Pallas kernels, head(): call(functools.partial(head_kernel, quad, devices), [columns(width, quad)...  11.4 us
    all_to_all x2, waiting for transfers between devices, exchanged(): lax.all_to_all(array, 'state', split_axis=0, concat_axis=0, tiled=True)  7.92 us
    unnamed x17, local copies, waits for them, and re-layouts  5.42 us
    pallas_call x1, Pallas kernels, in_stages(): call(first_part_kernel, [anywhere, anywhere], jax.ShapeDtypeStruct((devic...  3.14 us
  transfers between devices with their start and end apart: 17, of which 7 were waited for; matrix products, arithmetic and copies ran while one was open for 5% of the time, Pallas kernels for 28%

profile of v8, /device:TPU:0, one launch (start us, length us, event | category | flops | bytes accessed | tf_op | source)
XLA Modules:
  0.0 110.3 jit_solution(6050596236944692645)
XLA Ops:
  0.0 3.1 %shard_map.64 = f32[16,16,1408]{2,1,0:T(8,128)} custom-call(f32[16,32768]{1,0:T(8,128)} %fields_ref.3, s32[32,256]{1,0:T(8,128)} %bitcast.10), custom_call_target="tpu_custom_call" | custom-call | flops 1 | bytes 1 | tf_op jit(solution)/shard_map/pallas_call | solution.py:467
  3.1 0.0 copy-start
  3.2 0.0 copy-start.6
  3.2 7.5 %all-to-all-start = ((f32[16,16,1408]{2,1,0:T(8,128)}), f32[16,16,1408]{2,1,0:T(8,128)S(1)}, u32[]{:S(2)}, u32[]{:S(2)}) async-start(f32[16,16,1408]{2,1,0:T(8,128)} %shard_map.64), calls=%async_computation | async-start | bytes 2883584 | tf_op jit(solution)/shard_map/all_to_all | solution.py:464
  10.7 1.5 %shard_map.65 = (f32[64,768]{1,0:T(8,128)S(1)}, f32[64,768]{1,0:T(8,128)}, f32[64,768]{1,0:T(8,128)}, f32[64,768]{1,0:T(8,128)}) custom-call(f32[16,32768]{1,0:T(8,128)S(1)} %copy-done), custom_call_target="tpu_custom_call" | custom-call | flops 1 | bytes 1 | tf_op jit(solution)/shard_map/pallas_call | solution.py:446
  12.3 0.7 copy-done.2
  12.9 1.7 %collective-permute-start = (f32[64,768]{1,0:T(8,128)}, f32[64,768]{1,0:T(8,128)S(1)}, u32[]{:S(2)}, u32[]{:S(2)}) collective-permute-start(f32[64,768]{1,0:T(8,128)} %get-tuple-element.59), channel_id=1, source_target_pairs={{0,3},{1,2},{2,1},{3,0},{4,7},{5,6},{6,5},{7,4},{8,11},{9,10},{10,... | collective-permute-start | bytes 589832 | tf_op jit(solution)/shard_map/ppermute | solution.py:442
  14.6 0.4 collective-permute-start.1
  15.0 0.9 copy.14
  15.9 0.7 copy.15.adjacent_ref
  16.6 0.9 copy.13
  17.4 0.7 reshape.20.precision_ref
  18.1 0.7 reshape.21.position_ref
  18.8 10.2 %collective-permute-done.refs_0_ = f32[64,768]{1,0:T(8,128)S(1)} collective-permute-done((f32[64,768]{1,0:T(8,128)}, f32[64,768]{1,0:T(8,128)S(1)}, u32[]{:S(2)}, u32[]{:S(2)}) %collective-permute-start) | collective-permute-done | bytes 196640 | tf_op jit(solution)/shard_map/ppermute | solution.py:442
  29.0 4.9 %collective-permute-done.1.refs_1_ = f32[64,768]{1,0:T(8,128)S(1)} collective-permute-done((f32[64,768]{1,0:T(8,128)}, f32[64,768]{1,0:T(8,128)S(1)}, u32[]{:S(2)}, u32[]{:S(2)}) %collective-permute-start.1) | collective-permute-done | bytes 196640 | tf_op jit(solution)/shard_map/ppermute | solution.py:442
  33.9 0.0 collective-permute-done.2.refs_2_
  33.9 0.9 copy-done.3
  34.8 0.8 shard_map.66
  35.6 0.9 copy.12
  36.4 0.7 reshape.19.reading_ref
  37.1 1.8 %shard_map.67 = (f32[2,16,256]{2,1,0:T(8,128)}, s32[4,128]{1,0:T(4,128)}) custom-call(f32[64,128]{1,0:T(8,128)} %reshape.19.reading_ref, f32[64,128]{1,0:T(8,128)} %reshape.20.precision_ref, s32[64,128]{1,0:T(8,128)} %reshape.21.position_ref, s32[256]{0:T(256)} %tally_ref, s32[16,5]{1,0:T(8,128)} %copy.15.adjacent_ref), custom_call_target="tpu_custom_call" | custom-call | tf_op jit(solution)/shard_map/pallas_call | solution.py:226
  38.9 0.6 collective-permute-start.3
  39.5 5.1 %collective-permute-start.7 = (f32[64,768]{1,0:T(8,128)}, f32[64,768]{1,0:T(8,128)S(1)}, u32[]{:S(2)}, u32[]{:S(2)}) collective-permute-start(f32[64,768]{1,0:T(8,128)} %get-tuple-element.97), channel_id=1, source_target_pairs={{0,8},{1,9},{2,10},{3,11},{4,12},{5,13},{6,14},{7,15},{8,0},{9,1},... | collective-permute-start | bytes 589832 | tf_op jit(solution)/shard_map/ppermute | solution.py:442
  44.7 0.7 copy-done.4
  45.4 0.4 shard_map.68.here_ref.there_ref
  45.8 0.7 copy-done.1
  46.5 5.6 %shard_map.69 = (f32[64,512]{1,0:T(8,128)S(1)}, f32[64,512]{1,0:T(8,128)S(1)}, f32[64,512]{1,0:T(8,128)S(1)}, f32[64,512]{1,0:T(8,128)S(1)}) custom-call(f32[256,1408]{1,0:T(8,128)S(1)} %bitcast.5, f32[256,384]{1,0:T(8,128)S(1)} %shard_map.68.here_ref.there_ref, f32[256,384]{1,0:T(8,128)S(1)} %shard_map.68.here_ref.there_ref, f32[2,16,256]{2,1,0:T(8,128)S(1)} %copy-done.1), custom_call_target="tpu_custom_call" | custom-call | flops 1 | bytes 1 | tf_op jit(solution)/shard_map/pallas_call | solution.py:495
  52.1 0.1 collective-permute-start.4
  52.2 1.0 collective-permute-start.5
  53.2 0.9 collective-permute-start.6
  54.1 5.8 %shard_map.70 = (f32[64,512]{1,0:T(8,128)S(1)}, f32[64,512]{1,0:T(8,128)S(1)}, f32[64,512]{1,0:T(8,128)S(1)}, f32[64,512]{1,0:T(8,128)S(1)}) custom-call(f32[256,1408]{1,0:T(8,128)S(1)} %bitcast.6, f32[256,384]{1,0:T(8,128)S(1)} %shard_map.68.here_ref.there_ref, f32[256,384]{1,0:T(8,128)S(1)} %shard_map.68.here_ref.there_ref, f32[2,16,256]{2,1,0:T(8,128)S(1)} %copy-done.1), custom_call_target="tpu_custom_call" | custom-call | flops 1 | bytes 1 | tf_op jit(solution)/shard_map/pallas_call | solution.py:495
  59.9 0.6 collective-permute-done.6.refs_3_
  60.5 0.9 shard_map.71
  61.4 1.9 %collective-permute-start.9 = (f32[64,1024]{1,0:T(8,128)}, f32[64,1024]{1,0:T(8,128)S(1)}, u32[]{:S(2)}, u32[]{:S(2)}) collective-permute-start(f32[64,1024]{1,0:T(8,128)} %get-tuple-element.106), channel_id=1, source_target_pairs={{0,4},{1,5},{2,6},{3,7},{4,0},{5,1},{6,2},{7,3},{8,12},{9,13},{10,... | collective-permute-start | bytes 786440 | tf_op jit(solution)/shard_map/ppermute | solution.py:442
  63.2 2.5 %collective-permute-start.10 = (f32[64,1024]{1,0:T(8,128)}, f32[64,1024]{1,0:T(8,128)S(1)}, u32[]{:S(2)}, u32[]{:S(2)}) collective-permute-start(f32[64,1024]{1,0:T(8,128)} %get-tuple-element.107), channel_id=1, source_target_pairs={{0,8},{1,9},{2,10},{3,11},{4,12},{5,13},{6,14},{7,15},{8,0},{9,1},... | collective-permute-start | bytes 786440 | tf_op jit(solution)/shard_map/ppermute | solution.py:442
  65.8 0.1 collective-permute-start.11
  65.8 0.3 shard_map.72
  66.2 12.1 %shard_map.73 = f32[256,1024]{1,0:T(8,128)} custom-call(f32[256,1408]{1,0:T(8,128)S(1)} %bitcast.8, f32[256,768]{1,0:T(8,128)S(1)} %get-tuple-element.103.begin_ref.end_ref, f32[256,768]{1,0:T(8,128)S(1)} %get-tuple-element.103.begin_ref.end_ref, f32[256,384]{1,0:T(8,128)S(1)} %shard_map.68.here_ref.there_ref, f32[256,256]{1,0:T(8,128)S(1)} %get-tuple-element.104.tiles_ref, ...), custom_call_target="tpu_custom_call" | custom-call | flops 1 | bytes 1 | tf_op jit(solution)/shard_map/pallas_call | solution.py:527
  78.2 5.1 %all-to-all-start.1 = ((f32[16,16,1024]{2,1,0:T(8,128)}), f32[16,16,1024]{2,1,0:T(8,128)S(1)}, u32[]{:S(2)}, u32[]{:S(2)}) async-start(f32[16,16,1024]{2,1,0:T(8,128)} %bitcast.2), calls=%async_computation.1 | async-start | bytes 2097152 | tf_op jit(solution)/shard_map/all_to_all | solution.py:464
  83.4 1.4 %collective-permute-done.10.refs_1_.refs_2_ = f32[64,1024]{1,0:T(8,128)S(1)} collective-permute-done((f32[64,1024]{1,0:T(8,128)}, f32[64,1024]{1,0:T(8,128)S(1)}, u32[]{:S(2)}, u32[]{:S(2)}) %collective-permute-start.10) | collective-permute-done | bytes 262176 | tf_op jit(solution)/shard_map/ppermute | solution.py:442
  84.8 0.1 collective-permute-start.12
  84.9 1.5 %collective-permute-start.13 = (f32[64,512]{1,0:T(8,128)S(1)}, f32[64,512]{1,0:T(8,128)S(1)}, u32[]{:S(2)}, u32[]{:S(2)}) collective-permute-start(f32[64,512]{1,0:T(8,128)S(1)} %get-tuple-element.111), channel_id=1, source_target_pairs={{0,2},{1,3},{2,0},{3,1},{4,6},{5,7},{6,4},{7,5},{8,10},{9,11},{10,... | collective-permute-start | bytes 393224 | tf_op jit(solution)/shard_map/ppermute | solution.py:442
  86.4 0.4 collective-permute-start.14
  86.7 10.9 %collective-permute-done.13.refs_6_ = f32[64,512]{1,0:T(8,128)S(1)} collective-permute-done((f32[64,512]{1,0:T(8,128)S(1)}, f32[64,512]{1,0:T(8,128)S(1)}, u32[]{:S(2)}, u32[]{:S(2)}) %collective-permute-start.13) | collective-permute-done | bytes 131104 | tf_op jit(solution)/shard_map/ppermute | solution.py:442
  97.7 2.2 %collective-permute-done.14.refs_7_ = f32[64,512]{1,0:T(8,128)S(1)} collective-permute-done((f32[64,512]{1,0:T(8,128)S(1)}, f32[64,512]{1,0:T(8,128)S(1)}, u32[]{:S(2)}, u32[]{:S(2)}) %collective-permute-start.14) | collective-permute-done | bytes 131104 | tf_op jit(solution)/shard_map/ppermute | solution.py:442
  99.9 1.2 %shard_map.75._ = f32[16,32768]{1,0:T(8,128)} custom-call(f32[64,1024]{1,0:T(8,128)S(1)} %get-tuple-element.105.refs_3_.refs_0_, f32[64,1024]{1,0:T(8,128)S(1)} %collective-permute-done.9.refs_2_.refs_1_, f32[64,1024]{1,0:T(8,128)S(1)} %collective-permute-done.10.refs_1_.refs_2_, f32[64,1024]{1,0:T(8,128)S(1)} %collective-permute-done.11.refs_0_.refs_3_, ...), custom_call_target="tpu_custom_call" | custom-call | flops 1 | bytes 1 | tf_op jit(solution)/shard_map/pallas_call | solution.py:553
  101.1 7.9 %all-to-all-done.1 = f32[16,16,1024]{2,1,0:T(8,128)S(1)} async-done(((f32[16,16,1024]{2,1,0:T(8,128)}), f32[16,16,1024]{2,1,0:T(8,128)S(1)}, u32[]{:S(2)}, u32[]{:S(2)}) %all-to-all-start.1) | async-done | bytes 1048608 | tf_op jit(solution)/shard_map/all_to_all | solution.py:464
  109.0 1.1 shard_map.76
  (20 shorter events, 0.1 us)
Async XLA Ops:
  3.1 7.6 %copy-start = (f32[16,32768]{1,0:T(8,128)S(1)}, f32[16,32768]{1,0:T(8,128)}, u32[]{:S(2)}) copy-start(f32[16,32768]{1,0:T(8,128)} %fields_ref.3) | copy-start | bytes 6291460
  3.2 12.7 %copy-start.6 = (s32[16,5]{0,1:T(8,128)S(1)}, s32[16,5]{0,1:T(8,128)}, u32[]{:S(2)}) copy-start(s32[16,5]{0,1:T(8,128)} %param.11) | copy-start | bytes 964
  3.2 41.5 %all-to-all-start = ((f32[16,16,1408]{2,1,0:T(8,128)}), f32[16,16,1408]{2,1,0:T(8,128)S(1)}, u32[]{:S(2)}, u32[]{:S(2)}) async-start(f32[16,16,1408]{2,1,0:T(8,128)} %shard_map.64), calls=%async_computation | async-start | bytes 2883584 | tf_op jit(solution)/shard_map/all_to_all | solution.py:464
  12.3 0.7 copy-start.2
  12.9 16.0 %collective-permute-start = (f32[64,768]{1,0:T(8,128)}, f32[64,768]{1,0:T(8,128)S(1)}, u32[]{:S(2)}, u32[]{:S(2)}) collective-permute-start(f32[64,768]{1,0:T(8,128)} %get-tuple-element.59), channel_id=1, source_target_pairs={{0,3},{1,2},{2,1},{3,0},{4,7},{5,6},{6,5},{7,4},{8,11},{9,10},{10,... | collective-permute-start | bytes 589832 | tf_op jit(solution)/shard_map/ppermute | solution.py:442
  14.6 19.2 %collective-permute-start.1 = (f32[64,768]{1,0:T(8,128)}, f32[64,768]{1,0:T(8,128)S(1)}, u32[]{:S(2)}, u32[]{:S(2)}) collective-permute-start(f32[64,768]{1,0:T(8,128)} %get-tuple-element.60), channel_id=1, source_target_pairs={{0,2},{1,3},{2,0},{3,1},{4,6},{5,7},{6,4},{7,5},{8,10},{9,11},{10,... | collective-permute-start | bytes 589832 | tf_op jit(solution)/shard_map/ppermute | solution.py:442
  15.0 18.8 %collective-permute-start.2 = (f32[64,768]{1,0:T(8,128)}, f32[64,768]{1,0:T(8,128)S(1)}, u32[]{:S(2)}, u32[]{:S(2)}) collective-permute-start(f32[64,768]{1,0:T(8,128)} %get-tuple-element.61), channel_id=1, source_target_pairs={{0,1},{1,0},{2,3},{3,2},{4,5},{5,4},{6,7},{7,6},{8,9},{9,8},{10,11... | collective-permute-start | bytes 589832 | tf_op jit(solution)/shard_map/ppermute | solution.py:442
  33.9 0.9 copy-start.3
  38.9 13.2 %collective-permute-start.3 = (f32[64,768]{1,0:T(8,128)S(1)}, f32[64,768]{1,0:T(8,128)S(1)}, u32[]{:S(2)}, u32[]{:S(2)}) collective-permute-start(f32[64,768]{1,0:T(8,128)S(1)} %get-tuple-element.81), channel_id=1, source_target_pairs={{0,4},{1,5},{2,6},{3,7},{4,0},{5,1},{6,2},{7,3},{8,12},{9,13},{10,... | collective-permute-start | bytes 589832 | tf_op jit(solution)/shard_map/ppermute | solution.py:442
  39.5 21.8 %collective-permute-start.7 = (f32[64,768]{1,0:T(8,128)}, f32[64,768]{1,0:T(8,128)S(1)}, u32[]{:S(2)}, u32[]{:S(2)}) collective-permute-start(f32[64,768]{1,0:T(8,128)} %get-tuple-element.97), channel_id=1, source_target_pairs={{0,8},{1,9},{2,10},{3,11},{4,12},{5,13},{6,14},{7,15},{8,0},{9,1},... | collective-permute-start | bytes 589832 | tf_op jit(solution)/shard_map/ppermute | solution.py:442
  44.7 16.7 %collective-permute-start.8 = (f32[64,768]{1,0:T(8,128)}, f32[64,768]{1,0:T(8,128)S(1)}, u32[]{:S(2)}, u32[]{:S(2)}) collective-permute-start(f32[64,768]{1,0:T(8,128)} %get-tuple-element.98), channel_id=1, source_target_pairs={{0,12},{1,13},{2,14},{3,15},{4,8},{5,9},{6,10},{7,11},{8,4},{9,5},... | collective-permute-start | bytes 589832 | tf_op jit(solution)/shard_map/ppermute | solution.py:442
  44.7 0.7 copy-start.4
  45.8 0.8 copy-start.1
  52.1 13.7 %copy-start.5 = (s32[4,128]{1,0:T(4,128)S(1)}, s32[4,128]{1,0:T(4,128)}, u32[]{:S(2)}) copy-start(s32[4,128]{1,0:T(4,128)} %get-tuple-element.75.position_ref) | copy-start | bytes 6148
  52.1 7.7 %collective-permute-start.4 = (f32[64,512]{1,0:T(8,128)S(1)}, f32[64,512]{1,0:T(8,128)S(1)}, u32[]{:S(2)}, u32[]{:S(2)}) collective-permute-start(f32[64,512]{1,0:T(8,128)S(1)} %get-tuple-element.83), channel_id=1, source_target_pairs={{0,1},{1,0},{2,3},{3,2},{4,5},{5,4},{6,7},{7,6},{8,9},{9,8},{10,11... | collective-permute-start | bytes 393224 | tf_op jit(solution)/shard_map/ppermute | solution.py:442
  52.2 7.7 %collective-permute-start.5 = (f32[64,512]{1,0:T(8,128)S(1)}, f32[64,512]{1,0:T(8,128)S(1)}, u32[]{:S(2)}, u32[]{:S(2)}) collective-permute-start(f32[64,512]{1,0:T(8,128)S(1)} %get-tuple-element.84), channel_id=1, source_target_pairs={{0,2},{1,3},{2,0},{3,1},{4,6},{5,7},{6,4},{7,5},{8,10},{9,11},{10,... | collective-permute-start | bytes 393224 | tf_op jit(solution)/shard_map/ppermute | solution.py:442
  53.2 7.3 %collective-permute-start.6 = (f32[64,512]{1,0:T(8,128)S(1)}, f32[64,512]{1,0:T(8,128)S(1)}, u32[]{:S(2)}, u32[]{:S(2)}) collective-permute-start(f32[64,512]{1,0:T(8,128)S(1)} %get-tuple-element.85), channel_id=1, source_target_pairs={{0,3},{1,2},{2,1},{3,0},{4,7},{5,6},{6,5},{7,4},{8,11},{9,10},{10,... | collective-permute-start | bytes 393224 | tf_op jit(solution)/shard_map/ppermute | solution.py:442
  61.4 22.1 %collective-permute-start.9 = (f32[64,1024]{1,0:T(8,128)}, f32[64,1024]{1,0:T(8,128)S(1)}, u32[]{:S(2)}, u32[]{:S(2)}) collective-permute-start(f32[64,1024]{1,0:T(8,128)} %get-tuple-element.106), channel_id=1, source_target_pairs={{0,4},{1,5},{2,6},{3,7},{4,0},{5,1},{6,2},{7,3},{8,12},{9,13},{10,... | collective-permute-start | bytes 786440 | tf_op jit(solution)/shard_map/ppermute | solution.py:442
  63.2 21.5 %collective-permute-start.10 = (f32[64,1024]{1,0:T(8,128)}, f32[64,1024]{1,0:T(8,128)S(1)}, u32[]{:S(2)}, u32[]{:S(2)}) collective-permute-start(f32[64,1024]{1,0:T(8,128)} %get-tuple-element.107), channel_id=1, source_target_pairs={{0,8},{1,9},{2,10},{3,11},{4,12},{5,13},{6,14},{7,15},{8,0},{9,1},... | collective-permute-start | bytes 786440 | tf_op jit(solution)/shard_map/ppermute | solution.py:442
  65.8 19.0 %collective-permute-start.11 = (f32[64,1024]{1,0:T(8,128)S(1)}, f32[64,1024]{1,0:T(8,128)S(1)}, u32[]{:S(2)}, u32[]{:S(2)}) collective-permute-start(f32[64,1024]{1,0:T(8,128)S(1)} %get-tuple-element.108), channel_id=1, source_target_pairs={{0,12},{1,13},{2,14},{3,15},{4,8},{5,9},{6,10},{7,11},{8,4},{9,5},... | collective-permute-start | bytes 786440 | tf_op jit(solution)/shard_map/ppermute | solution.py:442
  78.2 30.8 %all-to-all-start.1 = ((f32[16,16,1024]{2,1,0:T(8,128)}), f32[16,16,1024]{2,1,0:T(8,128)S(1)}, u32[]{:S(2)}, u32[]{:S(2)}) async-start(f32[16,16,1024]{2,1,0:T(8,128)} %bitcast.2), calls=%async_computation.1 | async-start | bytes 2097152 | tf_op jit(solution)/shard_map/all_to_all | solution.py:464
  84.8 1.9 %collective-permute-start.12 = (f32[64,512]{1,0:T(8,128)S(1)}, f32[64,512]{1,0:T(8,128)S(1)}, u32[]{:S(2)}, u32[]{:S(2)}) collective-permute-start(f32[64,512]{1,0:T(8,128)S(1)} %get-tuple-element.110), channel_id=1, source_target_pairs={{0,1},{1,0},{2,3},{3,2},{4,5},{5,4},{6,7},{7,6},{8,9},{9,8},{10,11... | collective-permute-start | bytes 393224 | tf_op jit(solution)/shard_map/ppermute | solution.py:442
  84.9 12.8 %collective-permute-start.13 = (f32[64,512]{1,0:T(8,128)S(1)}, f32[64,512]{1,0:T(8,128)S(1)}, u32[]{:S(2)}, u32[]{:S(2)}) collective-permute-start(f32[64,512]{1,0:T(8,128)S(1)} %get-tuple-element.111), channel_id=1, source_target_pairs={{0,2},{1,3},{2,0},{3,1},{4,6},{5,7},{6,4},{7,5},{8,10},{9,11},{10,... | collective-permute-start | bytes 393224 | tf_op jit(solution)/shard_map/ppermute | solution.py:442
  86.4 13.5 %collective-permute-start.14 = (f32[64,512]{1,0:T(8,128)S(1)}, f32[64,512]{1,0:T(8,128)S(1)}, u32[]{:S(2)}, u32[]{:S(2)}) collective-permute-start(f32[64,512]{1,0:T(8,128)S(1)} %get-tuple-element.112), channel_id=1, source_target_pairs={{0,3},{1,2},{2,1},{3,0},{4,7},{5,6},{6,5},{7,4},{8,11},{9,10},{10,... | collective-permute-start | bytes 393224 | tf_op jit(solution)/shard_map/ppermute | solution.py:442

commit v9 on v8

--- a/solution.py
+++ b/solution.py
@@ -479,8 +479,8 @@
     )(fields, observations[2].T)
     first = exchanged(sent).reshape(members, split + lanes)
     second = turned(swapped(second_parts(), 1), outer)
-    second, tied = lax.optimization_barrier((second, [observations[0],observations[3]]))
-    observations = [tied[0], observations[1], observations[2], tied[1], observations[4]]
+    second, reading = lax.optimization_barrier((second, observations[0]))
+    observations = [reading, *observations[1:]]
     terms, quad_position = window_terms(*observations, members)
     second, terms, quad_position = lax.optimization_barrier((second, terms, quad_position))
     second = swapped(second, INNER)

time: 112 us -> 112 us (level)
  no operation moved by 1% of the time
where the time goes in v9:
time: 112 us; the launch traced here: 110 us
  waiting for transfers between devices  38 us (34%)
  Pallas kernels  34.7 us (31%)
  starting transfers between devices  28.8 us (26%)
  local copies, waits for them, and re-layouts  8.36 us (7%)
    ppermute x15, waiting for transfers between devices, swapped(): lax.ppermute(arrays[k], 'state', pairs[k])  30.1 us
    ppermute x15, starting transfers between devices, swapped(): lax.ppermute(arrays[k], 'state', pairs[k])  16.2 us
    all_to_all x2, starting transfers between devices, exchanged(): lax.all_to_all(array, 'state', split_axis=0, concat_axis=0, tiled=True)  12.7 us
    pallas_call x1, Pallas kernels, in_stages(): call(tail_kernel, [columns(half, split // half - 1), columns(half, 1), pl...  12.1 us
    pallas_call x2, Pallas kernels, head(): call(functools.partial(head_kernel, quad, devices), [columns(width, quad)...  11.4 us
    all_to_all x2, waiting for transfers between devices, exchanged(): lax.all_to_all(array, 'state', split_axis=0, concat_axis=0, tiled=True)  7.92 us
    unnamed x17, local copies, waits for them, and re-layouts  5.42 us
    pallas_call x1, Pallas kernels, in_stages(): call(first_part_kernel, [anywhere, anywhere], jax.ShapeDtypeStruct((devic...  3.14 us
  transfers between devices with their start and end apart: 17, of which 7 were waited for; matrix products, arithmetic and copies ran while one was open for 5% of the time, Pallas kernels for 28%

profile of v9, /device:TPU:0, one launch (start us, length us, event | category | flops | bytes accessed | tf_op | source)
XLA Modules:
  0.0 110.3 jit_solution(6050596236944692645)
XLA Ops:
  0.0 3.1 %shard_map.64 = f32[16,16,1408]{2,1,0:T(8,128)} custom-call(f32[16,32768]{1,0:T(8,128)} %fields_ref.3, s32[32,256]{1,0:T(8,128)} %bitcast.10), custom_call_target="tpu_custom_call" | custom-call | flops 1 | bytes 1 | tf_op jit(solution)/shard_map/pallas_call | solution.py:467
  3.1 0.0 copy-start
  3.2 0.0 copy-start.6
  3.2 7.5 %all-to-all-start = ((f32[16,16,1408]{2,1,0:T(8,128)}), f32[16,16,1408]{2,1,0:T(8,128)S(1)}, u32[]{:S(2)}, u32[]{:S(2)}) async-start(f32[16,16,1408]{2,1,0:T(8,128)} %shard_map.64), calls=%async_computation | async-start | bytes 2883584 | tf_op jit(solution)/shard_map/all_to_all | solution.py:464
  10.7 1.5 %shard_map.65 = (f32[64,768]{1,0:T(8,128)S(1)}, f32[64,768]{1,0:T(8,128)}, f32[64,768]{1,0:T(8,128)}, f32[64,768]{1,0:T(8,128)}) custom-call(f32[16,32768]{1,0:T(8,128)S(1)} %copy-done), custom_call_target="tpu_custom_call" | custom-call | flops 1 | bytes 1 | tf_op jit(solution)/shard_map/pallas_call | solution.py:446
  12.3 0.7 copy-done.2
  12.9 1.7 %collective-permute-start = (f32[64,768]{1,0:T(8,128)}, f32[64,768]{1,0:T(8,128)S(1)}, u32[]{:S(2)}, u32[]{:S(2)}) collective-permute-start(f32[64,768]{1,0:T(8,128)} %get-tuple-element.58), channel_id=1, source_target_pairs={{0,3},{1,2},{2,1},{3,0},{4,7},{5,6},{6,5},{7,4},{8,11},{9,10},{10,... | collective-permute-start | bytes 589832 | tf_op jit(solution)/shard_map/ppermute | solution.py:442
  14.6 0.4 collective-permute-start.1
  15.0 0.9 copy.14
  15.9 0.7 copy.15.adjacent_ref
  16.6 0.9 copy.13
  17.4 0.7 reshape.20.precision_ref
  18.1 0.7 reshape.21.position_ref
  18.8 10.2 %collective-permute-done.refs_0_ = f32[64,768]{1,0:T(8,128)S(1)} collective-permute-done((f32[64,768]{1,0:T(8,128)}, f32[64,768]{1,0:T(8,128)S(1)}, u32[]{:S(2)}, u32[]{:S(2)}) %collective-permute-start) | collective-permute-done | bytes 196640 | tf_op jit(solution)/shard_map/ppermute | solution.py:442
  29.0 4.9 %collective-permute-done.1.refs_1_ = f32[64,768]{1,0:T(8,128)S(1)} collective-permute-done((f32[64,768]{1,0:T(8,128)}, f32[64,768]{1,0:T(8,128)S(1)}, u32[]{:S(2)}, u32[]{:S(2)}) %collective-permute-start.1) | collective-permute-done | bytes 196640 | tf_op jit(solution)/shard_map/ppermute | solution.py:442
  33.9 0.0 collective-permute-done.2.refs_2_
  33.9 0.9 copy-done.3
  34.8 0.8 shard_map.66
  35.6 0.9 copy.12
  36.4 0.7 reshape.19.reading_ref
  37.1 1.8 %shard_map.67 = (f32[2,16,256]{2,1,0:T(8,128)}, s32[4,128]{1,0:T(4,128)}) custom-call(f32[64,128]{1,0:T(8,128)} %reshape.19.reading_ref, f32[64,128]{1,0:T(8,128)} %reshape.20.precision_ref, s32[64,128]{1,0:T(8,128)} %reshape.21.position_ref, s32[256]{0:T(256)} %tally_ref.1, s32[16,5]{1,0:T(8,128)} %copy.15.adjacent_ref), custom_call_target="tpu_custom_call" | custom-call | tf_op jit(solution)/shard_map/pallas_call | solution.py:226
  38.9 0.6 collective-permute-start.3
  39.5 5.1 %collective-permute-start.7 = (f32[64,768]{1,0:T(8,128)}, f32[64,768]{1,0:T(8,128)S(1)}, u32[]{:S(2)}, u32[]{:S(2)}) collective-permute-start(f32[64,768]{1,0:T(8,128)} %get-tuple-element.95), channel_id=1, source_target_pairs={{0,8},{1,9},{2,10},{3,11},{4,12},{5,13},{6,14},{7,15},{8,0},{9,1},... | collective-permute-start | bytes 589832 | tf_op jit(solution)/shard_map/ppermute | solution.py:442
  44.7 0.7 copy-done.4
  45.4 0.4 shard_map.68.here_ref.there_ref
  45.8 0.7 copy-done.1
  46.5 5.6 %shard_map.69 = (f32[64,512]{1,0:T(8,128)S(1)}, f32[64,512]{1,0:T(8,128)S(1)}, f32[64,512]{1,0:T(8,128)S(1)}, f32[64,512]{1,0:T(8,128)S(1)}) custom-call(f32[256,1408]{1,0:T(8,128)S(1)} %bitcast.5, f32[256,384]{1,0:T(8,128)S(1)} %shard_map.68.here_ref.there_ref, f32[256,384]{1,0:T(8,128)S(1)} %shard_map.68.here_ref.there_ref, f32[2,16,256]{2,1,0:T(8,128)S(1)} %copy-done.1), custom_call_target="tpu_custom_call" | custom-call | flops 1 | bytes 1 | tf_op jit(solution)/shard_map/pallas_call | solution.py:495
  52.1 0.1 collective-permute-start.4
  52.2 1.0 collective-permute-start.5
  53.2 0.9 collective-permute-start.6
  54.1 5.8 %shard_map.70 = (f32[64,512]{1,0:T(8,128)S(1)}, f32[64,512]{1,0:T(8,128)S(1)}, f32[64,512]{1,0:T(8,128)S(1)}, f32[64,512]{1,0:T(8,128)S(1)}) custom-call(f32[256,1408]{1,0:T(8,128)S(1)} %bitcast.6, f32[256,384]{1,0:T(8,128)S(1)} %shard_map.68.here_ref.there_ref, f32[256,384]{1,0:T(8,128)S(1)} %shard_map.68.here_ref.there_ref, f32[2,16,256]{2,1,0:T(8,128)S(1)} %copy-done.1), custom_call_target="tpu_custom_call" | custom-call | flops 1 | bytes 1 | tf_op jit(solution)/shard_map/pallas_call | solution.py:495
  59.9 0.6 collective-permute-done.6.refs_3_
  60.5 0.9 shard_map.71
  61.4 1.9 %collective-permute-start.9 = (f32[64,1024]{1,0:T(8,128)}, f32[64,1024]{1,0:T(8,128)S(1)}, u32[]{:S(2)}, u32[]{:S(2)}) collective-permute-start(f32[64,1024]{1,0:T(8,128)} %get-tuple-element.104), channel_id=1, source_target_pairs={{0,4},{1,5},{2,6},{3,7},{4,0},{5,1},{6,2},{7,3},{8,12},{9,13},{10,... | collective-permute-start | bytes 786440 | tf_op jit(solution)/shard_map/ppermute | solution.py:442
  63.2 2.5 %collective-permute-start.10 = (f32[64,1024]{1,0:T(8,128)}, f32[64,1024]{1,0:T(8,128)S(1)}, u32[]{:S(2)}, u32[]{:S(2)}) collective-permute-start(f32[64,1024]{1,0:T(8,128)} %get-tuple-element.105), channel_id=1, source_target_pairs={{0,8},{1,9},{2,10},{3,11},{4,12},{5,13},{6,14},{7,15},{8,0},{9,1},... | collective-permute-start | bytes 786440 | tf_op jit(solution)/shard_map/ppermute | solution.py:442
  65.8 0.1 collective-permute-start.11
  65.8 0.3 shard_map.72
  66.2 12.1 %shard_map.73 = f32[256,1024]{1,0:T(8,128)} custom-call(f32[256,1408]{1,0:T(8,128)S(1)} %bitcast.8, f32[256,768]{1,0:T(8,128)S(1)} %get-tuple-element.101.begin_ref.end_ref, f32[256,768]{1,0:T(8,128)S(1)} %get-tuple-element.101.begin_ref.end_ref, f32[256,384]{1,0:T(8,128)S(1)} %shard_map.68.here_ref.there_ref, f32[256,256]{1,0:T(8,128)S(1)} %get-tuple-element.102.tiles_ref, ...), custom_call_target="tpu_custom_call" | custom-call | flops 1 | bytes 1 | tf_op jit(solution)/shard_map/pallas_call | solution.py:527
  78.2 5.1 %all-to-all-start.1 = ((f32[16,16,1024]{2,1,0:T(8,128)}), f32[16,16,1024]{2,1,0:T(8,128)S(1)}, u32[]{:S(2)}, u32[]{:S(2)}) async-start(f32[16,16,1024]{2,1,0:T(8,128)} %bitcast.2), calls=%async_computation.1 | async-start | bytes 2097152 | tf_op jit(solution)/shard_map/all_to_all | solution.py:464
  83.4 1.4 %collective-permute-done.10.refs_1_.refs_2_ = f32[64,1024]{1,0:T(8,128)S(1)} collective-permute-done((f32[64,1024]{1,0:T(8,128)}, f32[64,1024]{1,0:T(8,128)S(1)}, u32[]{:S(2)}, u32[]{:S(2)}) %collective-permute-start.10) | collective-permute-done | bytes 262176 | tf_op jit(solution)/shard_map/ppermute | solution.py:442
  84.8 0.1 collective-permute-start.12
  84.9 1.5 %collective-permute-start.13 = (f32[64,512]{1,0:T(8,128)S(1)}, f32[64,512]{1,0:T(8,128)S(1)}, u32[]{:S(2)}, u32[]{:S(2)}) collective-permute-start(f32[64,512]{1,0:T(8,128)S(1)} %get-tuple-element.109), channel_id=1, source_target_pairs={{0,2},{1,3},{2,0},{3,1},{4,6},{5,7},{6,4},{7,5},{8,10},{9,11},{10,... | collective-permute-start | bytes 393224 | tf_op jit(solution)/shard_map/ppermute | solution.py:442
  86.4 0.4 collective-permute-start.14
  86.7 10.9 %collective-permute-done.13.refs_6_ = f32[64,512]{1,0:T(8,128)S(1)} collective-permute-done((f32[64,512]{1,0:T(8,128)S(1)}, f32[64,512]{1,0:T(8,128)S(1)}, u32[]{:S(2)}, u32[]{:S(2)}) %collective-permute-start.13) | collective-permute-done | bytes 131104 | tf_op jit(solution)/shard_map/ppermute | solution.py:442
  97.7 2.2 %collective-permute-done.14.refs_7_ = f32[64,512]{1,0:T(8,128)S(1)} collective-permute-done((f32[64,512]{1,0:T(8,128)S(1)}, f32[64,512]{1,0:T(8,128)S(1)}, u32[]{:S(2)}, u32[]{:S(2)}) %collective-permute-start.14) | collective-permute-done | bytes 131104 | tf_op jit(solution)/shard_map/ppermute | solution.py:442
  99.9 1.2 %shard_map.75._ = f32[16,32768]{1,0:T(8,128)} custom-call(f32[64,1024]{1,0:T(8,128)S(1)} %get-tuple-element.103.refs_3_.refs_0_, f32[64,1024]{1,0:T(8,128)S(1)} %collective-permute-done.9.refs_2_.refs_1_, f32[64,1024]{1,0:T(8,128)S(1)} %collective-permute-done.10.refs_1_.refs_2_, f32[64,1024]{1,0:T(8,128)S(1)} %collective-permute-done.11.refs_0_.refs_3_, ...), custom_call_target="tpu_custom_call" | custom-call | flops 1 | bytes 1 | tf_op jit(solution)/shard_map/pallas_call | solution.py:553
  101.1 7.9 %all-to-all-done.1 = f32[16,16,1024]{2,1,0:T(8,128)S(1)} async-done(((f32[16,16,1024]{2,1,0:T(8,128)}), f32[16,16,1024]{2,1,0:T(8,128)S(1)}, u32[]{:S(2)}, u32[]{:S(2)}) %all-to-all-start.1) | async-done | bytes 1048608 | tf_op jit(solution)/shard_map/all_to_all | solution.py:464
  109.0 1.1 shard_map.76
  (20 shorter events, 0.1 us)
Async XLA Ops:
  3.1 7.6 %copy-start = (f32[16,32768]{1,0:T(8,128)S(1)}, f32[16,32768]{1,0:T(8,128)}, u32[]{:S(2)}) copy-start(f32[16,32768]{1,0:T(8,128)} %fields_ref.3) | copy-start | bytes 6291460
  3.2 12.7 %copy-start.6 = (s32[16,5]{0,1:T(8,128)S(1)}, s32[16,5]{0,1:T(8,128)}, u32[]{:S(2)}) copy-start(s32[16,5]{0,1:T(8,128)} %param.11) | copy-start | bytes 964
  3.2 41.5 %all-to-all-start = ((f32[16,16,1408]{2,1,0:T(8,128)}), f32[16,16,1408]{2,1,0:T(8,128)S(1)}, u32[]{:S(2)}, u32[]{:S(2)}) async-start(f32[16,16,1408]{2,1,0:T(8,128)} %shard_map.64), calls=%async_computation | async-start | bytes 2883584 | tf_op jit(solution)/shard_map/all_to_all | solution.py:464
  12.3 0.7 copy-start.2
  12.9 16.0 %collective-permute-start = (f32[64,768]{1,0:T(8,128)}, f32[64,768]{1,0:T(8,128)S(1)}, u32[]{:S(2)}, u32[]{:S(2)}) collective-permute-start(f32[64,768]{1,0:T(8,128)} %get-tuple-element.58), channel_id=1, source_target_pairs={{0,3},{1,2},{2,1},{3,0},{4,7},{5,6},{6,5},{7,4},{8,11},{9,10},{10,... | collective-permute-start | bytes 589832 | tf_op jit(solution)/shard_map/ppermute | solution.py:442
  14.6 19.2 %collective-permute-start.1 = (f32[64,768]{1,0:T(8,128)}, f32[64,768]{1,0:T(8,128)S(1)}, u32[]{:S(2)}, u32[]{:S(2)}) collective-permute-start(f32[64,768]{1,0:T(8,128)} %get-tuple-element.59), channel_id=1, source_target_pairs={{0,2},{1,3},{2,0},{3,1},{4,6},{5,7},{6,4},{7,5},{8,10},{9,11},{10,... | collective-permute-start | bytes 589832 | tf_op jit(solution)/shard_map/ppermute | solution.py:442
  15.0 18.8 %collective-permute-start.2 = (f32[64,768]{1,0:T(8,128)}, f32[64,768]{1,0:T(8,128)S(1)}, u32[]{:S(2)}, u32[]{:S(2)}) collective-permute-start(f32[64,768]{1,0:T(8,128)} %get-tuple-element.60), channel_id=1, source_target_pairs={{0,1},{1,0},{2,3},{3,2},{4,5},{5,4},{6,7},{7,6},{8,9},{9,8},{10,11... | collective-permute-start | bytes 589832 | tf_op jit(solution)/shard_map/ppermute | solution.py:442
  33.9 0.9 copy-start.3
  38.9 13.2 %collective-permute-start.3 = (f32[64,768]{1,0:T(8,128)S(1)}, f32[64,768]{1,0:T(8,128)S(1)}, u32[]{:S(2)}, u32[]{:S(2)}) collective-permute-start(f32[64,768]{1,0:T(8,128)S(1)} %get-tuple-element.79), channel_id=1, source_target_pairs={{0,4},{1,5},{2,6},{3,7},{4,0},{5,1},{6,2},{7,3},{8,12},{9,13},{10,... | collective-permute-start | bytes 589832 | tf_op jit(solution)/shard_map/ppermute | solution.py:442
  39.5 21.8 %collective-permute-start.7 = (f32[64,768]{1,0:T(8,128)}, f32[64,768]{1,0:T(8,128)S(1)}, u32[]{:S(2)}, u32[]{:S(2)}) collective-permute-start(f32[64,768]{1,0:T(8,128)} %get-tuple-element.95), channel_id=1, source_target_pairs={{0,8},{1,9},{2,10},{3,11},{4,12},{5,13},{6,14},{7,15},{8,0},{9,1},... | collective-permute-start | bytes 589832 | tf_op jit(solution)/shard_map/ppermute | solution.py:442
  44.7 16.7 %collective-permute-start.8 = (f32[64,768]{1,0:T(8,128)}, f32[64,768]{1,0:T(8,128)S(1)}, u32[]{:S(2)}, u32[]{:S(2)}) collective-permute-start(f32[64,768]{1,0:T(8,128)} %get-tuple-element.96), channel_id=1, source_target_pairs={{0,12},{1,13},{2,14},{3,15},{4,8},{5,9},{6,10},{7,11},{8,4},{9,5},... | collective-permute-start | bytes 589832 | tf_op jit(solution)/shard_map/ppermute | solution.py:442
  44.7 0.7 copy-start.4
  45.8 0.8 copy-start.1
  52.1 13.7 %copy-start.5 = (s32[4,128]{1,0:T(4,128)S(1)}, s32[4,128]{1,0:T(4,128)}, u32[]{:S(2)}) copy-start(s32[4,128]{1,0:T(4,128)} %get-tuple-element.73.position_ref) | copy-start | bytes 6148
  52.1 7.7 %collective-permute-start.4 = (f32[64,512]{1,0:T(8,128)S(1)}, f32[64,512]{1,0:T(8,128)S(1)}, u32[]{:S(2)}, u32[]{:S(2)}) collective-permute-start(f32[64,512]{1,0:T(8,128)S(1)} %get-tuple-element.81), channel_id=1, source_target_pairs={{0,1},{1,0},{2,3},{3,2},{4,5},{5,4},{6,7},{7,6},{8,9},{9,8},{10,11... | collective-permute-start | bytes 393224 | tf_op jit(solution)/shard_map/ppermute | solution.py:442
  52.2 7.7 %collective-permute-start.5 = (f32[64,512]{1,0:T(8,128)S(1)}, f32[64,512]{1,0:T(8,128)S(1)}, u32[]{:S(2)}, u32[]{:S(2)}) collective-permute-start(f32[64,512]{1,0:T(8,128)S(1)} %get-tuple-element.82), channel_id=1, source_target_pairs={{0,2},{1,3},{2,0},{3,1},{4,6},{5,7},{6,4},{7,5},{8,10},{9,11},{10,... | collective-permute-start | bytes 393224 | tf_op jit(solution)/shard_map/ppermute | solution.py:442
  53.2 7.3 %collective-permute-start.6 = (f32[64,512]{1,0:T(8,128)S(1)}, f32[64,512]{1,0:T(8,128)S(1)}, u32[]{:S(2)}, u32[]{:S(2)}) collective-permute-start(f32[64,512]{1,0:T(8,128)S(1)} %get-tuple-element.83), channel_id=1, source_target_pairs={{0,3},{1,2},{2,1},{3,0},{4,7},{5,6},{6,5},{7,4},{8,11},{9,10},{10,... | collective-permute-start | bytes 393224 | tf_op jit(solution)/shard_map/ppermute | solution.py:442
  61.4 22.1 %collective-permute-start.9 = (f32[64,1024]{1,0:T(8,128)}, f32[64,1024]{1,0:T(8,128)S(1)}, u32[]{:S(2)}, u32[]{:S(2)}) collective-permute-start(f32[64,1024]{1,0:T(8,128)} %get-tuple-element.104), channel_id=1, source_target_pairs={{0,4},{1,5},{2,6},{3,7},{4,0},{5,1},{6,2},{7,3},{8,12},{9,13},{10,... | collective-permute-start | bytes 786440 | tf_op jit(solution)/shard_map/ppermute | solution.py:442
  63.2 21.5 %collective-permute-start.10 = (f32[64,1024]{1,0:T(8,128)}, f32[64,1024]{1,0:T(8,128)S(1)}, u32[]{:S(2)}, u32[]{:S(2)}) collective-permute-start(f32[64,1024]{1,0:T(8,128)} %get-tuple-element.105), channel_id=1, source_target_pairs={{0,8},{1,9},{2,10},{3,11},{4,12},{5,13},{6,14},{7,15},{8,0},{9,1},... | collective-permute-start | bytes 786440 | tf_op jit(solution)/shard_map/ppermute | solution.py:442
  65.8 19.0 %collective-permute-start.11 = (f32[64,1024]{1,0:T(8,128)S(1)}, f32[64,1024]{1,0:T(8,128)S(1)}, u32[]{:S(2)}, u32[]{:S(2)}) collective-permute-start(f32[64,1024]{1,0:T(8,128)S(1)} %get-tuple-element.106), channel_id=1, source_target_pairs={{0,12},{1,13},{2,14},{3,15},{4,8},{5,9},{6,10},{7,11},{8,4},{9,5},... | collective-permute-start | bytes 786440 | tf_op jit(solution)/shard_map/ppermute | solution.py:442
  78.2 30.8 %all-to-all-start.1 = ((f32[16,16,1024]{2,1,0:T(8,128)}), f32[16,16,1024]{2,1,0:T(8,128)S(1)}, u32[]{:S(2)}, u32[]{:S(2)}) async-start(f32[16,16,1024]{2,1,0:T(8,128)} %bitcast.2), calls=%async_computation.1 | async-start | bytes 2097152 | tf_op jit(solution)/shard_map/all_to_all | solution.py:464
  84.8 1.9 %collective-permute-start.12 = (f32[64,512]{1,0:T(8,128)S(1)}, f32[64,512]{1,0:T(8,128)S(1)}, u32[]{:S(2)}, u32[]{:S(2)}) collective-permute-start(f32[64,512]{1,0:T(8,128)S(1)} %get-tuple-element.108), channel_id=1, source_target_pairs={{0,1},{1,0},{2,3},{3,2},{4,5},{5,4},{6,7},{7,6},{8,9},{9,8},{10,11... | collective-permute-start | bytes 393224 | tf_op jit(solution)/shard_map/ppermute | solution.py:442
  84.9 12.8 %collective-permute-start.13 = (f32[64,512]{1,0:T(8,128)S(1)}, f32[64,512]{1,0:T(8,128)S(1)}, u32[]{:S(2)}, u32[]{:S(2)}) collective-permute-start(f32[64,512]{1,0:T(8,128)S(1)} %get-tuple-element.109), channel_id=1, source_target_pairs={{0,2},{1,3},{2,0},{3,1},{4,6},{5,7},{6,4},{7,5},{8,10},{9,11},{10,... | collective-permute-start | bytes 393224 | tf_op jit(solution)/shard_map/ppermute | solution.py:442
  86.4 13.5 %collective-permute-start.14 = (f32[64,512]{1,0:T(8,128)S(1)}, f32[64,512]{1,0:T(8,128)S(1)}, u32[]{:S(2)}, u32[]{:S(2)}) collective-permute-start(f32[64,512]{1,0:T(8,128)S(1)} %get-tuple-element.110), channel_id=1, source_target_pairs={{0,3},{1,2},{2,1},{3,0},{4,7},{5,6},{6,5},{7,4},{8,11},{9,10},{10,... | collective-permute-start | bytes 393224 | tf_op jit(solution)/shard_map/ppermute | solution.py:442
